TPU v7x, 128 devices: a whole 4x4x4 slice. The times are simulated.
128 devices in a mesh: prow: 8 (over y, core), pcol: 16 (over z, x).
Axes of the slice: x: 4, y: 4, z: 4, core: 2. Of those that a mesh axis runs over, the one named last changes fastest.
Arguments:
- omega: bfloat16 [320, 2, 131072], P(None, None, ('prow', 'pcol')), may hold values from -6 to 6
- u_basis: bfloat16 [2, 131072, 1024], P(None, ('prow', 'pcol')), may hold values from -0.1875 to 0.1875
- v_basis: bfloat16 [2, 131072, 1024], P(None, ('prow', 'pcol')), may hold values from -0.015625 to 0.015625
- coupling: bfloat16 [2, 1024, 1024], replicated, may hold values from -0.1875 to 0.1875
- leaf_blocks: bfloat16 [2, 512, 256, 256], P(None, ('prow', 'pcol')), may hold values from -0.375 to 0.375
- child_map: int32 [2, 1024], P(None, ('prow', 'pcol')), may hold values from 0 to 2047, as said below
Outputs:
- parent_y: float32 [2048, 320, 128], P('prow', 'pcol')
- parent_z: float32 [2048, 320, 128], P('prow', 'pcol')
Inputs may be any that keep to these rules, and one draw needn't show every extreme that they name: `child_map`: parent block q belongs to process row q // 256. The blocks of one child go to distinct parent blocks. Process row p holds blocks p * 128 to (p + 1) * 128 - 1 of each child; of the 256 child blocks that one process row holds, at most 64 go to the parent blocks of one process row, and in every draw some process row receives exactly 64 from every process row.
All inputs are finite; a program needn't handle non-finite values.
Results may differ from a plain program's by a relative error of at most 0.006.
Values may be sent and summed in bfloat16 or wider, within the bound.
No kernel may reach another device: no remote copies, remote signals or barrier semaphores. Data moves between devices by JAX's collectives and lax.ppermute only.
A program may use at most 128 MiB of HBM per device.

v0:
```python
import jax
import jax.numpy as jnp
from jax import lax
from jax.sharding import PartitionSpec as P

BLK = 128


def per_device(omega, u_basis, v_basis, coupling, leaf_blocks, child_map):
    row_count = lax.axis_size("prow")
    col_count = lax.axis_size("pcol")
    samples = omega.shape[0]
    half_local = omega.shape[2]
    leaf_size = leaf_blocks.shape[2]
    v_part = jnp.einsum("scn,cnr->csr", omega, v_basis, preferred_element_type=jnp.float32)
    u_part = jnp.einsum("scn,cnr->csr", omega, u_basis, preferred_element_type=jnp.float32)
    v_total, u_total = lax.psum((v_part, u_part), ("prow", "pcol"))
    v_probe = v_total.astype(jnp.bfloat16)
    u_probe = u_total.astype(jnp.bfloat16)
    y_inner = jnp.einsum(
        "csr,ctr->cst", v_probe, coupling, preferred_element_type=jnp.float32
    ).astype(jnp.bfloat16)
    z_inner = jnp.einsum(
        "csr,crt->cst", u_probe, coupling, preferred_element_type=jnp.float32
    ).astype(jnp.bfloat16)
    y_low = jnp.einsum("cst,cnt->scn", y_inner, u_basis, preferred_element_type=jnp.float32)
    z_low = jnp.einsum("cst,cnt->scn", z_inner, v_basis, preferred_element_type=jnp.float32)
    grid = omega.reshape(samples, 2, half_local // leaf_size, leaf_size)
    y_leaf = jnp.einsum("sclk,clik->scli", grid, leaf_blocks, preferred_element_type=jnp.float32)
    z_leaf = jnp.einsum("scli,clik->sclk", grid, leaf_blocks, preferred_element_type=jnp.float32)
    y_samp = (
        (y_low + y_leaf.reshape(samples, 2, half_local))
        .astype(jnp.bfloat16)
        .reshape(samples, 2, half_local // BLK, BLK)
    )
    z_samp = (
        (z_low + z_leaf.reshape(samples, 2, half_local))
        .astype(jnp.bfloat16)
        .reshape(samples, 2, half_local // BLK, BLK)
    )
    left_split, right_split = (
        lax.all_to_all(y_samp, "pcol", split_axis=0, concat_axis=2, tiled=True),
        lax.all_to_all(z_samp, "pcol", split_axis=0, concat_axis=2, tiled=True),
    )
    left_sample_columns = left_split.reshape(samples // col_count, -1, BLK)
    right_sample_columns = right_split.reshape(samples // col_count, -1, BLK)
    targets = lax.all_gather(child_map, "pcol", axis=1, tiled=True).reshape(-1)
    owner_rows = targets.shape[0]
    capacity = 2 * owner_rows // row_count
    dest_row = targets // owner_rows
    local_target = targets % owner_rows
    dest_hits = (dest_row[:, None] == jnp.arange(row_count)[None, :]).astype(jnp.int32)
    earlier = jnp.cumsum(dest_hits, axis=0) - dest_hits
    order = jnp.sum(earlier * dest_hits, axis=1)
    slot_index = dest_row * capacity + order
    chosen = jnp.arange(row_count * capacity)[:, None] == slot_index[None, :]
    piece_selector = chosen.astype(jnp.bfloat16)
    outgoing_left_samples = jnp.einsum(
        "af,mfv->amv", piece_selector, left_sample_columns, preferred_element_type=jnp.float32
    ).astype(jnp.bfloat16)
    outgoing_right_samples = jnp.einsum(
        "af,mfv->amv", piece_selector, right_sample_columns, preferred_element_type=jnp.float32
    ).astype(jnp.bfloat16)
    send_ids = jnp.sum(chosen.astype(jnp.int32) * (local_target + 1)[None, :], axis=1) - 1
    recv_y, recv_z, recv_ids = (
        lax.all_to_all(outgoing_left_samples, "prow", split_axis=0, concat_axis=0, tiled=True),
        lax.all_to_all(outgoing_right_samples, "prow", split_axis=0, concat_axis=0, tiled=True),
        lax.all_to_all(send_ids, "prow", split_axis=0, concat_axis=0, tiled=True),
    )
    placer = (jnp.arange(owner_rows)[:, None] == recv_ids[None, :]).astype(jnp.bfloat16)
    parent_y = jnp.einsum("qb,bsr->qsr", placer, recv_y, preferred_element_type=jnp.float32)
    parent_z = jnp.einsum("qb,bsr->qsr", placer, recv_z, preferred_element_type=jnp.float32)
    return (parent_y, parent_z)


def solution(mesh):
    return jax.shard_map(
        per_device,
        mesh=mesh,
        in_specs=(
            P(None, None, ("prow", "pcol")),
            P(None, ("prow", "pcol"), None),
            P(None, ("prow", "pcol"), None),
            P(),
            P(None, ("prow", "pcol"), None, None),
            P(None, ("prow", "pcol")),
        ),
        out_specs=(P("prow", "pcol", None), P("prow", "pcol", None)),
        check_vma=False,
    )
```

profile of v0, /device:TPU:1, one launch (start us, length us, event | category | flops | bytes accessed | tf_op | source)
XLA Modules:
  0.0 307.6 jit_solution(16432042543382512507)
XLA Ops:
  0.6 20.2 %all-gather = s32[16,8,2]{1,2,0:T(2,128)S(1)} all-gather(s32[1,8,2]{1,2,0:T(2,128)} %bitcast.109), channel_id=1, replica_groups=mesh['prow'=8,'pcol'=16] {'pcol'}, dimensions={0}, use_global_device_ids=true | all-gather | bytes 1088 | tf_op jit(solution)/shard_map/all_gather | solution.py:47
  22.8 10.5 %all-to-all-start = ((s32[8,64,1]{1,2,0:T(1,128)}), s32[8,64,1]{1,2,0:T(1,128)S(1)}, u32[]{:S(2)}, u32[]{:S(2)}) async-start(s32[8,64,1]{1,2,0:T(1,128)} %bitcast.7), calls=%async_computation | async-start | bytes 8192 | tf_op jit(solution)/shard_map/all_to_all | solution.py:68
  33.3 3.7 %reshape.146 = bf16[320,2,4,256]{3,2,1,0:T(4,128)(2,1)S(1)} reshape(bf16[320,2,1024]{2,1,0:T(2,128)(2,1)} %param.6) | data formatting | bytes 2621440 | tf_op jit(solution)/shard_map/reshape | solution.py:28
  37.0 5.8 %fusion.10 = f32[2,320,1024]{2,1,0:T(8,128)} fusion(bf16[2,1024,1024]{2,1,0:T(8,128)(2,1)} %param.7, bf16[320,2,1024]{2,1,0:T(2,128)(2,1)} %param.6), kind=kOutput, calls=%fused_computation.18 | convolution fusion | flops 1342177280 | bytes 8126464 | tf_op jit(solution)/shard_map/scn,cnr->csr/dot_general | solution.py:16
  42.8 3.1 fusion.12
  46.3 1.9 copy.45
  48.2 105.2 %all-reduce.2 = (bf16[2,320,1024]{2,1,0:T(8,128)(2,1)}, bf16[2,320,1024]{2,1,0:T(8,128)(2,1)}) all-reduce(f32[2,320,1024]{2,1,0:T(8,128)} %fusion.12, f32[2,320,1024]{2,1,0:T(8,128)} %fusion.10), channel_id=1, replica_groups=mesh['prow'=8,'pcol'=16] {'prow','pcol'}, use_global_device_ids=true, to_apply=%region_4.5 | all-reduce | flops 1310720 | bytes 7864320 | tf_op jit(solution)/shard_map/psum | solution.py:17
  153.4 8.5 %fusion = bf16[320,2,1024]{2,0,1:T(8,128)(2,1)} fusion(f32[320,2,1024]{2,0,1:T(8,128)} %bitcast.105, bf16[2,1024,1024]{2,1,0:T(8,128)(2,1)} %param.8, bf16[2,1024,1024]{2,1,0:T(8,128)(2,1)} %param.9, bf16[2,320,1024]{2,1,0:T(8,128)(2,1)} %get-tuple-element.3), kind=kOutput, calls=%fused_computation.1 | convolution fusion | flops 2686320640 | bytes 13631488 | tf_op jit(solution)/shard_map/cst,cnt->scn/dot_general | solution.py:27
  161.9 1.7 copy.47
  164.9 6.1 %all-to-all-start.3 = ((bf16[320,2,8,128]{3,2,1,0:T(8,128)(2,1)}), bf16[320,2,8,128]{3,2,1,0:T(8,128)(2,1)}, u32[]{:S(2)}, u32[]{:S(2)}) async-start(bf16[320,2,8,128]{3,2,1,0:T(8,128)(2,1)} %copy.40), calls=%async_computation.3 | async-start | bytes 2621440 | tf_op jit(solution)/shard_map/all_to_all | solution.py:43
  171.5 1.9 copy.44
  173.4 7.5 %fusion.1 = bf16[320,2,1024]{2,0,1:T(8,128)(2,1)S(1)} fusion(f32[320,2,1024]{2,0,1:T(8,128)} %bitcast.106, bf16[2,1024,1024]{2,1,0:T(8,128)(2,1)} %param.7, bf16[2,1024,1024]{2,1,0:T(8,128)(2,1)} %param.9, bf16[2,320,1024]{2,1,0:T(8,128)(2,1)} %get-tuple-element.2), kind=kOutput, calls=%fused_computation.3 | convolution fusion | flops 2686320640 | bytes 13631488 | tf_op jit(solution)/shard_map/cst,cnt->scn/dot_general | solution.py:26
  182.6 7.3 %all-to-all-done.3 = bf16[320,2,8,128]{3,2,1,0:T(8,128)(2,1)} async-done(((bf16[320,2,8,128]{3,2,1,0:T(8,128)(2,1)}), bf16[320,2,8,128]{3,2,1,0:T(8,128)(2,1)}, u32[]{:S(2)}, u32[]{:S(2)}) %all-to-all-start.3) | async-done | bytes 1310752 | tf_op jit(solution)/shard_map/all_to_all | solution.py:43
  189.9 5.4 %all-to-all-start.1 = ((bf16[320,2,8,128]{3,2,1,0:T(8,128)(2,1)}), bf16[320,2,8,128]{3,2,1,0:T(8,128)(2,1)S(1)}, u32[]{:S(2)}, u32[]{:S(2)}) async-start(bf16[320,2,8,128]{3,2,1,0:T(8,128)(2,1)} %copy.33), calls=%async_computation.1 | async-start | bytes 2621440 | tf_op jit(solution)/shard_map/all_to_all | solution.py:42
  195.3 1.7 copy.41
  197.8 3.5 %copy.42 = bf16[512,20,128]{2,1,0:T(8,128)(2,1)} copy(bf16[512,20,128]{2,0,1:T(8,128)(2,1)S(1)} %convolution_convert_fusion) | data formatting | bytes 5242880 | tf_op jit(solution)/shard_map/convert_element_type | solution.py:63
  201.3 12.5 %all-to-all-done.1 = bf16[320,2,8,128]{3,2,1,0:T(8,128)(2,1)S(1)} async-done(((bf16[320,2,8,128]{3,2,1,0:T(8,128)(2,1)}), bf16[320,2,8,128]{3,2,1,0:T(8,128)(2,1)S(1)}, u32[]{:S(2)}, u32[]{:S(2)}) %all-to-all-start.1) | async-done | bytes 1310752 | tf_op jit(solution)/shard_map/all_to_all | solution.py:42
  213.8 8.9 %all-to-all-start.4 = ((bf16[512,20,128]{2,1,0:T(8,128)(2,1)}), bf16[512,20,128]{2,1,0:T(8,128)(2,1)}, u32[]{:S(2)}, u32[]{:S(2)}) async-start(bf16[512,20,128]{2,1,0:T(8,128)(2,1)} %copy.42), calls=%async_computation.4 | async-start | bytes 6291456 | tf_op jit(solution)/shard_map/all_to_all | solution.py:67
  224.0 3.5 %copy.35 = bf16[512,20,128]{2,1,0:T(8,128)(2,1)} copy(bf16[512,20,128]{2,0,1:T(8,128)(2,1)S(1)} %convolution_convert_fusion.1) | data formatting | bytes 5242880 | tf_op jit(solution)/shard_map/convert_element_type | solution.py:60
  227.4 33.0 %all-to-all-done.4 = bf16[512,20,128]{2,1,0:T(8,128)(2,1)} async-done(((bf16[512,20,128]{2,1,0:T(8,128)(2,1)}), bf16[512,20,128]{2,1,0:T(8,128)(2,1)}, u32[]{:S(2)}, u32[]{:S(2)}) %all-to-all-start.4) | async-done | bytes 2621472 | tf_op jit(solution)/shard_map/all_to_all | solution.py:67
  260.4 5.2 %all-to-all-start.2 = ((bf16[512,20,128]{2,1,0:T(8,128)(2,1)}), bf16[512,20,128]{2,1,0:T(8,128)(2,1)}, u32[]{:S(2)}, u32[]{:S(2)}) async-start(bf16[512,20,128]{2,1,0:T(8,128)(2,1)} %copy.35), calls=%async_computation.2 | async-start | bytes 6291456 | tf_op jit(solution)/shard_map/all_to_all | solution.py:66
  266.9 4.3 %fusion.2 = f32[256,20,128]{2,0,1:T(8,128)} fusion(bf16[512,20,128]{2,1,0:T(8,128)(2,1)} %all-to-all-done.4, s32[512]{0:T(512)S(1)} %eq.61), kind=kOutput, calls=%fused_computation.4 | convolution fusion | flops 671219712 | bytes 5244928 | tf_op jit(solution)/shard_map/qb,bsr->qsr/dot_general | solution.py:72
  271.2 32.1 %all-to-all-done.2 = bf16[512,20,128]{2,1,0:T(8,128)(2,1)} async-done(((bf16[512,20,128]{2,1,0:T(8,128)(2,1)}), bf16[512,20,128]{2,1,0:T(8,128)(2,1)}, u32[]{:S(2)}, u32[]{:S(2)}) %all-to-all-start.2) | async-done | bytes 2621472 | tf_op jit(solution)/shard_map/all_to_all | solution.py:66
  303.3 4.2 %fusion.4 = f32[256,20,128]{2,0,1:T(8,128)} fusion(bf16[512,20,128]{2,1,0:T(8,128)(2,1)} %all-to-all-done.2, s32[512]{0:T(512)S(1)} %eq.61), kind=kOutput, calls=%fused_computation.6 | convolution fusion | flops 671219712 | bytes 5244928 | tf_op jit(solution)/shard_map/qb,bsr->qsr/dot_general | solution.py:71
  (34 shorter events, 9.2 us)
Async XLA Ops:
  0.6 45.2 %copy-start = (bf16[2,4,256,256]{3,2,1,0:T(8,128)(2,1)S(1)}, bf16[2,4,256,256]{3,2,1,0:T(8,128)(2,1)}, u32[]{:S(2)}) copy-start(bf16[2,4,256,256]{3,2,1,0:T(8,128)(2,1)} %param.10) | copy-start | bytes 3145732
  22.8 142.1 %all-to-all-start = ((s32[8,64,1]{1,2,0:T(1,128)}), s32[8,64,1]{1,2,0:T(1,128)S(1)}, u32[]{:S(2)}, u32[]{:S(2)}) async-start(s32[8,64,1]{1,2,0:T(1,128)} %bitcast.7), calls=%async_computation | async-start | bytes 8192 | tf_op jit(solution)/shard_map/all_to_all | solution.py:68
  37.0 5.8 %copy-start.2 = (bf16[320,2,1024]{2,1,0:T(2,128)(2,1)S(1)}, bf16[320,2,1024]{2,1,0:T(2,128)(2,1)}, u32[]{:S(2)}) copy-start(bf16[320,2,1024]{2,1,0:T(2,128)(2,1)} %param.6) | copy-start | bytes 3932164
  37.0 5.8 %copy-start.3 = (bf16[2,1024,1024]{2,1,0:T(8,128)(2,1)S(1)}, bf16[2,1024,1024]{2,1,0:T(8,128)(2,1)}, u32[]{:S(2)}) copy-start(bf16[2,1024,1024]{2,1,0:T(8,128)(2,1)} %param.8) | copy-start | bytes 12582916
  164.9 24.9 %all-to-all-start.3 = ((bf16[320,2,8,128]{3,2,1,0:T(8,128)(2,1)}), bf16[320,2,8,128]{3,2,1,0:T(8,128)(2,1)}, u32[]{:S(2)}, u32[]{:S(2)}) async-start(bf16[320,2,8,128]{3,2,1,0:T(8,128)(2,1)} %copy.40), calls=%async_computation.3 | async-start | bytes 2621440 | tf_op jit(solution)/shard_map/all_to_all | solution.py:43
  189.9 24.0 %all-to-all-start.1 = ((bf16[320,2,8,128]{3,2,1,0:T(8,128)(2,1)}), bf16[320,2,8,128]{3,2,1,0:T(8,128)(2,1)S(1)}, u32[]{:S(2)}, u32[]{:S(2)}) async-start(bf16[320,2,8,128]{3,2,1,0:T(8,128)(2,1)} %copy.33), calls=%async_computation.1 | async-start | bytes 2621440 | tf_op jit(solution)/shard_map/all_to_all | solution.py:42
  213.8 46.6 %all-to-all-start.4 = ((bf16[512,20,128]{2,1,0:T(8,128)(2,1)}), bf16[512,20,128]{2,1,0:T(8,128)(2,1)}, u32[]{:S(2)}, u32[]{:S(2)}) async-start(bf16[512,20,128]{2,1,0:T(8,128)(2,1)} %copy.42), calls=%async_computation.4 | async-start | bytes 6291456 | tf_op jit(solution)/shard_map/all_to_all | solution.py:67
  260.4 42.9 %all-to-all-start.2 = ((bf16[512,20,128]{2,1,0:T(8,128)(2,1)}), bf16[512,20,128]{2,1,0:T(8,128)(2,1)}, u32[]{:S(2)}, u32[]{:S(2)}) async-start(bf16[512,20,128]{2,1,0:T(8,128)(2,1)} %copy.35), calls=%async_computation.2 | async-start | bytes 6291456 | tf_op jit(solution)/shard_map/all_to_all | solution.py:66
  266.9 40.7 %copy-start.1 = (bf16[2,4,256,256]{3,2,1,0:T(8,128)(2,1)S(1)}, bf16[2,4,256,256]{3,2,1,0:T(8,128)(2,1)}, u32[]{:S(2)}) copy-start(bf16[2,4,256,256]{3,2,1,0:T(8,128)(2,1)} %param.10) | copy-start | bytes 3145732
where the time goes:
time: 308 us
  blocking collectives  125 us (41%)
  waiting for transfers between devices  84.9 us (28%)
  matrix products  36.2 us (12%)
  starting transfers between devices  36.1 us (12%)
  local copies, waits for them, and re-layouts  22.6 us (7%)
    psum x1, blocking collectives, per_device(): v_total, u_total = lax.psum((v_part, u_part), ('prow', 'pcol'))  105 us
    all_to_all x1, waiting for transfers between devices, per_device(): lax.all_to_all(outgoing_right_samples, 'prow', split_axis=0, concat_axis=...  33 us
    all_to_all x1, waiting for transfers between devices, per_device(): lax.all_to_all(outgoing_left_samples, 'prow', split_axis=0, concat_axis=0...  32.1 us
    all_gather x1, blocking collectives, per_device(): targets = lax.all_gather(child_map, 'pcol', axis=1, tiled=True).reshape(-1)  20.2 us
    all_to_all x1, waiting for transfers between devices, per_device(): lax.all_to_all(y_samp, 'pcol', split_axis=0, concat_axis=2, tiled=True)  12.5 us
    all_to_all x1, starting transfers between devices, per_device(): lax.all_to_all(send_ids, 'prow', split_axis=0, concat_axis=0, tiled=True)  10.5 us
    all_to_all x1, starting transfers between devices, per_device(): lax.all_to_all(outgoing_right_samples, 'prow', split_axis=0, concat_axis=...  8.9 us
    dot_general x1, matrix products, per_device(): jnp.einsum('cst,cnt->scn', z_inner, v_basis, preferred_element_type=jnp.f...  8.53 us
  transfers between devices with their start and end apart: 5, of which 4 were waited for; matrix products, arithmetic and copies ran while one was open for 18% of the time, Pallas kernels for 0%

commit v1 on v0

v1 whole, which is shorter than its diff:
```python
import functools

import jax
import jax.numpy as jnp
from jax import lax
from jax.experimental import pallas as pl
from jax.experimental.pallas import tpu as pltpu
from jax.sharding import Mesh, PartitionSpec as P

BLK = 128
ALL = ("y", "core", "z", "x")
RING = 4
STEPS = (1, 3, 2)
INFO = 8
BF16, F32 = jnp.bfloat16, jnp.float32


def ring_y(x, step):
    return lax.ppermute(x, "y", [(i, (i + step) % RING) for i in range(RING)])


def swap_core(x):
    return lax.ppermute(x, "core", [(0, 1), (1, 0)])


def ring_zx(x, first, step):
    pairs = []
    for core in range(2):
        for zz in range(RING):
            for xx in range(RING):
                along_x = (core == 0) == first
                to_z = zz if along_x else (zz + step) % RING
                to_x = (xx + step) % RING if along_x else xx
                pairs.append(((core * RING + zz) * RING + xx, (core * RING + to_z) * RING + to_x))
    return lax.ppermute(x, ("core", "z", "x"), pairs)


VMEM = pl.BlockSpec(memory_space=pltpu.VMEM)
SMEM = pl.BlockSpec(memory_space=pltpu.SMEM)
HBM = pl.BlockSpec(memory_space=pl.ANY)


def params(mib):
    return pltpu.CompilerParams(vmem_limit_bytes=mib * 2**20)


def pick_kernel(place, v_own, v_got, u_own, u_got, *rest):
    outs, (own, got, sems) = rest[:RING], rest[RING:]
    me, core = place[0], place[1]

    def copies(first, second, k):
        at = lax.rem(me + k, RING)
        return (
            pltpu.make_async_copy(first.at[at], own.at[k], sems.at[0, k]),
            pltpu.make_async_copy(second.at[at], got.at[k], sems.at[1, k]),
        )

    order = (1, 3, 2, 0)

    @pl.when(core == 0)
    def _():
        for k in order:
            for copy in copies(v_own, v_got, k):
                copy.start()

    @pl.when(core == 1)
    def _():
        for k in order:
            for copy in copies(u_own, u_got, k):
                copy.start()

    for k in order:
        for copy in copies(v_own, v_got, k):
            copy.wait()
        outs[k][...] = (own[k].astype(F32) + got[k].astype(F32)).astype(BF16)


def pick(place, *parts):
    _, rows, rank = parts[0].shape
    return pl.pallas_call(
        pick_kernel,
        out_shape=[jax.ShapeDtypeStruct((rows, rank), BF16)] * RING,
        in_specs=[SMEM] + [HBM] * 4,
        out_specs=[VMEM] * RING,
        scratch_shapes=[
            pltpu.VMEM((RING, rows, rank), BF16),
            pltpu.VMEM((RING, rows, rank), BF16),
            pltpu.SemaphoreType.DMA((2, RING)),
        ],
        compiler_params=params(16),
    )(place, *parts)


def sum_split_kernel(place, *refs):
    ins, outs = refs[:RING], refs[RING:]
    for k in range(RING):
        at = lax.rem(place[0] + k, RING)
        total = ins[0][at].astype(F32)
        for part in ins[1:]:
            total = total + part[at].astype(F32)
        outs[k][...] = total.astype(BF16)


def sum_split(place, parts):
    rows, rank = parts[0].shape
    shaped = [p.reshape(RING, rows // RING, rank) for p in parts]
    return pl.pallas_call(
        sum_split_kernel,
        out_shape=[jax.ShapeDtypeStruct((rows // RING, rank), BF16)] * RING,
        in_specs=[SMEM] + [VMEM] * RING,
        out_specs=[VMEM] * RING,
        compiler_params=params(16),
    )(place, *shaped)


def sum_info_kernel(a, b, c, d, info, out):
    total = a[...].astype(F32) + b[...].astype(F32) + c[...].astype(F32) + d[...].astype(F32)
    out[...] = jnp.concatenate([total, info[...]], axis=0).astype(BF16)


def sum_info(parts, info):
    rows, rank = parts[0].shape
    return pl.pallas_call(
        sum_info_kernel,
        out_shape=jax.ShapeDtypeStruct((rows + INFO, rank), BF16),
        in_specs=[VMEM] * 5,
        out_specs=VMEM,
        compiler_params=params(16),
    )(*parts, info)


def couple_kernel(a, b, c, d, weight, out):
    parts = [r[...].astype(F32) for r in (a, b, c, d)]
    rows = out.shape[0] - INFO
    probe = (parts[0] + parts[1] + parts[2] + parts[3]).astype(BF16)
    inner = jnp.dot(probe, weight[...], preferred_element_type=F32)
    infos = [p[rows : rows + 1] for p in parts] + [jnp.zeros((INFO - RING, out.shape[1]), F32)]
    out[...] = jnp.concatenate([inner[:rows]] + infos, axis=0).astype(BF16)


def couple(parts, weight):
    return pl.pallas_call(
        couple_kernel,
        out_shape=jax.ShapeDtypeStruct(parts[0].shape, BF16),
        in_specs=[VMEM] * 5,
        out_specs=VMEM,
        compiler_params=params(16),
    )(*parts, weight)


def expand_kernel(flip, place, *refs):
    held, (basis, probes, leaf, out, lhs, sems) = refs[: 2 * RING], refs[2 * RING :]
    a_me, b_me, own = place[0], place[1], place[2]
    child, tile = pl.program_id(0), pl.program_id(1)

    def copies(side):
        for j in range(RING):
            for m in range(RING):
                to = lhs.at[lax.rem(a_me + RING - j, RING), lax.rem(b_me + RING - m, RING)]
                yield pltpu.make_async_copy(held[side * RING + j].at[m], to, sems.at[j, m])

    @pl.when((child == 0) & (tile == 0))
    def _():
        @pl.when(own == 1)
        def _():
            for copy in copies(0):
                copy.start()

        @pl.when(own == 0)
        def _():
            for copy in copies(1):
                copy.start()

        for copy in copies(0):
            copy.wait()

    rows = lhs.shape[2] - INFO
    rank = lhs.shape[3]
    left = lhs[pl.ds(2 * child, 2)].reshape(-1, rank)
    low = lax.dot_general(left, basis[0], (((1,), (1,)), ((), ())), preferred_element_type=F32)
    low = jnp.concatenate([low[i : i + rows] for i in range(0, low.shape[0], rows + INFO)], axis=0)
    side = 1 if flip else 0
    near = lax.dot_general(probes[...], leaf[0, 0], (((1,), (side,)), ((), ())), preferred_element_type=F32)
    out[0] = (low + near).astype(BF16)


def expand(place, held, basis, probes, leaf_blocks, flip):
    _, local, rank = basis.shape
    samples = probes.shape[0]
    leaf = leaf_blocks.shape[2]
    tiles = local // leaf
    rows = held[0].shape[1]
    return pl.pallas_call(
        functools.partial(expand_kernel, flip),
        grid=(2, tiles),
        out_shape=jax.ShapeDtypeStruct((2, samples, local), BF16),
        in_specs=[SMEM]
        + [HBM] * (2 * RING)
        + [
            pl.BlockSpec((1, leaf, rank), lambda c, t: (c, t, 0)),
            pl.BlockSpec((samples, leaf), lambda c, t: (0, c * tiles + t)),
            pl.BlockSpec((1, 1, leaf, leaf), lambda c, t: (c, t, 0, 0)),
        ],
        out_specs=pl.BlockSpec((1, samples, leaf), lambda c, t: (c, 0, t)),
        scratch_shapes=[
            pltpu.VMEM((RING, RING, rows, rank), BF16),
            pltpu.SemaphoreType.DMA((RING, RING)),
        ],
        compiler_params=params(24),
    )(place, *held, basis, probes, leaf_blocks)


GROUP = 4


def send_kernel(selector, columns, *outs):
    capacity = outs[0].shape[1]
    blocks = selector.shape[1]
    for s in range(outs[0].shape[0]):
        moved = jnp.dot(
            selector[...], columns[:, s].reshape(blocks, BLK), preferred_element_type=F32
        ).astype(BF16)
        for i, out in enumerate(outs):
            out[s] = moved[i * capacity : (i + 1) * capacity]


def send(selector, columns, capacity):
    cols, share, near, _ = columns.shape
    count = selector.shape[0] // capacity
    return pl.pallas_call(
        send_kernel,
        grid=(share // GROUP,),
        out_shape=[jax.ShapeDtypeStruct((share, capacity, BLK), BF16)] * count,
        in_specs=[
            pl.BlockSpec(selector.shape, lambda g: (0, 0)),
            pl.BlockSpec((cols, GROUP, near, BLK), lambda g: (0, g, 0, 0)),
        ],
        out_specs=[pl.BlockSpec((GROUP, capacity, BLK), lambda g: (g, 0, 0))] * count,
        compiler_params=params(24),
    )(selector, columns)


def place_kernel(placer, *refs):
    parts, out = refs[:-1], refs[-1]
    for s in range(out.shape[0]):
        arrived = jnp.concatenate([part[s] for part in parts], axis=0)
        out[s] = jnp.dot(placer[...], arrived, preferred_element_type=F32)


def place_blocks(placer, parts):
    share, capacity, _ = parts[0].shape
    return pl.pallas_call(
        place_kernel,
        grid=(share // GROUP,),
        out_shape=jax.ShapeDtypeStruct((share, placer.shape[0], BLK), F32),
        in_specs=[pl.BlockSpec(placer.shape, lambda g: (0, 0))]
        + [pl.BlockSpec((GROUP, capacity, BLK), lambda g: (g, 0, 0))] * len(parts),
        out_specs=pl.BlockSpec((GROUP, placer.shape[0], BLK), lambda g: (g, 0, 0)),
        compiler_params=params(24),
    )(placer, *parts)


def per_device(omega, u_basis, v_basis, coupling, leaf_blocks, child_map):
    y_me, core, z_me, x_me = (lax.axis_index(a) for a in ALL)
    samples = omega.shape[0]
    local = omega.shape[2]
    rank = u_basis.shape[2]
    rows = 2 * samples
    row_count, col_count = 2 * RING, RING * RING
    near = child_map.size
    owner_rows = near * col_count
    capacity = 2 * owner_rows // row_count
    share = samples // col_count
    a_me = jnp.where(core == 0, x_me, z_me)
    b_me = jnp.where(core == 0, z_me, x_me)

    mine = child_map.reshape(-1)
    mine = jnp.concatenate([mine // owner_rows, mine % owner_rows]).astype(F32)
    both = jnp.concatenate([mine, swap_core(mine)])
    info = jnp.zeros((INFO, rank), F32).at[0, : both.size].set(both)

    v_own = jnp.einsum("scn,cnr->csr", omega, v_basis, preferred_element_type=F32).astype(BF16)
    v_own = v_own.reshape(RING, rows // RING, rank)
    v_got = lax.ppermute(v_own, "core", [(1, 0)])
    u_own = jnp.einsum("scn,cnr->csr", omega, u_basis, preferred_element_type=F32).astype(BF16)
    u_own = u_own.reshape(RING, rows // RING, rank)
    u_got = lax.ppermute(u_own, "core", [(0, 1)])
    pieces = pick(jnp.stack([a_me, core]).astype(jnp.int32), v_own, v_got, u_own, u_got)
    pieces = [pieces[0]] + [ring_zx(pieces[k], True, k) for k in STEPS]
    pieces = sum_split(b_me.astype(jnp.int32).reshape(1), pieces)
    pieces = [pieces[0]] + [ring_zx(pieces[k], False, k) for k in STEPS]
    piece = sum_info(pieces, info)
    weight = lax.dynamic_index_in_dim(coupling, a_me // 2, 0, keepdims=False)
    weight = jnp.where(core == 0, weight.T, weight)
    inner = couple([piece] + [ring_y(piece, k) for k in (1, 2, 3)], weight)
    inner = jnp.stack([inner] + [ring_zx(inner, False, k) for k in (1, 2, 3)])
    held = [inner] + [ring_zx(inner, True, k) for k in (1, 2, 3)]
    swapped = [swap_core(p) for p in held]

    fields = 2 * both.size // 2
    seen = jnp.stack([p[:, rows // 16 : rows // 16 + RING, :fields] for p in held])
    at = jnp.arange(RING)
    z_step, x_step = (z_me - at) % RING, (x_me - at) % RING
    flat = jnp.where(
        core == 0, x_step[None, :] * RING + z_step[:, None], z_step[:, None] * RING + x_step[None, :]
    ).reshape(-1)
    seen = seen.reshape(col_count, RING, 2, 2, near)[flat].astype(jnp.int32)
    seen = seen.transpose(3, 2, 1, 0, 4).reshape(2, row_count, owner_rows)
    dest, home = seen[0], seen[1]
    same = (dest[:, :, None] == dest[:, None, :]).astype(jnp.int32)
    before = (jnp.arange(owner_rows)[None, :] < jnp.arange(owner_rows)[:, None]).astype(jnp.int32)
    order = jnp.sum(same * before[None], axis=2)
    to_step = (dest[0] // 2 - y_me) % RING
    to_other = jnp.where(dest[0] % 2 == core, 0, 1)
    slot = (to_other * RING + to_step) * capacity + order[0]
    selector = (jnp.arange(row_count * capacity)[:, None] == slot[None, :]).astype(BF16)
    arriving = jnp.where(dest == y_me * 2 + core, order, -1)
    spots = jnp.arange(capacity)
    ids = jnp.sum((spots[None, :, None] == arriving[:, None, :]) * (home + 1)[:, None, :], axis=2) - 1
    placer = (jnp.arange(owner_rows)[:, None] == ids.reshape(-1)[None, :]).astype(BF16)

    probes = omega.reshape(samples, 2 * local)

    def columns(samp):
        samp = samp.reshape(2, samples, local // BLK, BLK).transpose(1, 0, 2, 3).reshape(samples, near, BLK)
        got = lax.all_to_all(samp, ("z", "x"), split_axis=0, concat_axis=0, tiled=True)
        return got.reshape(col_count, share, near, BLK)

    def exchange(cols):
        out = send(selector, cols, capacity)
        here, there = out[:RING], [swap_core(p) for p in out[RING:]]
        arrived = [here[0]] + [ring_y(here[k], k) for k in (1, 2, 3)]
        arrived += [there[0]] + [ring_y(there[k], k) for k in (1, 2, 3)]
        return place_blocks(placer, arrived).transpose(1, 0, 2)

    y_place = jnp.stack([x_me, z_me, 1 - core]).astype(jnp.int32)
    z_place = jnp.stack([z_me, x_me, core]).astype(jnp.int32)
    y_cols = columns(expand(y_place, held + swapped, u_basis, probes, leaf_blocks, True))
    z_cols = columns(expand(z_place, held + swapped, v_basis, probes, leaf_blocks, False))
    return exchange(y_cols), exchange(z_cols)


def solution(mesh):
    fine = Mesh(mesh.devices.reshape(RING, 2, RING, RING), ALL)
    return jax.shard_map(
        per_device,
        mesh=fine,
        in_specs=(
            P(None, None, ALL),
            P(None, ALL, None),
            P(None, ALL, None),
            P(),
            P(None, ALL, None, None),
            P(None, ALL),
        ),
        out_specs=(P(("y", "core"), ("z", "x"), None), P(("y", "core"), ("z", "x"), None)),
        check_vma=False,
    )
```

time: 308 us -> 208 us (0.68)
  blocking collectives: 125 us -> 0 us
  Pallas kernels: 0 us -> 33.5 us
  starting transfers between devices: 36.1 us -> 67.2 us
  matrix products: 36.2 us -> 6.9 us
  waiting for transfers between devices: 84.9 us -> 63.5 us
  local copies, waits for them, and re-layouts: 22.6 us -> 29.9 us
  other arithmetic: 1.56 us -> 4.83 us
    psum x1 -> x0, blocking collectives: 105 us -> none  [per_device(): v_total, u_total = lax.psum((v_part, u_part), ('prow', 'pcol'))]
    all_to_all x5 -> x2, waiting for transfers between devices: 84.9 us -> 10.6 us  [columns(): lax.all_to_all(samp, ('z', 'x'), split_axis=0, concat_axis=0, tiled=True)]
    ppermute x0 -> x42, starting transfers between devices: none -> 59.3 us  [the longest x13 23.7 us: swap_core(): return lax.ppermute(x, 'core', [(0, 1), (1, 0)])]
    ppermute x0 -> x42, waiting for transfers between devices: none -> 52.9 us  [the longest x15 36.9 us: ring_y(): return lax.ppermute(x, 'y', [(i, (i + step) % RING) for i in range(RING)])]
    pallas_call x0 -> x10, Pallas kernels: none -> 33.5 us  [the longest x2 14.2 us: expand(): pl.pallas_call(functools.partial(expand_kernel, flip), grid=(2, tiles), o...]
    dot_general x10 -> x2, matrix products: 36.2 us -> 6.9 us  [the longest x1 4.26 us: per_device(): jnp.einsum('scn,cnr->csr', omega, v_basis, preferred_element_type=F32)]
    all_to_all x5 -> x2, starting transfers between devices: 36.1 us -> 7.86 us  [columns(): lax.all_to_all(samp, ('z', 'x'), split_axis=0, concat_axis=0, tiled=True)]
    all_gather x1 -> x0, blocking collectives: 20.2 us -> none  [per_device(): targets = lax.all_gather(child_map, 'pcol', axis=1, tiled=True).reshape(-1)]
  transfers between devices with their start and end apart: 5 -> 44, of which waited for: 4 -> 17; matrix products, arithmetic and copies ran while one was open for 18% -> 10% of each run, Pallas kernels for 0% -> 9%
where the time goes in v1:
time: 208 us; the launch traced here: 207 us
  starting transfers between devices  67.2 us (32%)
  waiting for transfers between devices  63.5 us (31%)
  Pallas kernels  33.5 us (16%)
  local copies, waits for them, and re-layouts  29.9 us (14%)
  matrix products  6.9 us (3%)
  other arithmetic  4.83 us (2%)
    ppermute x15, waiting for transfers between devices, ring_y(): return lax.ppermute(x, 'y', [(i, (i + step) % RING) for i in range(RING)])  36.9 us
    ppermute x13, starting transfers between devices, swap_core(): return lax.ppermute(x, 'core', [(0, 1), (1, 0)])  23.7 us
    unnamed x51, local copies, waits for them, and re-layouts  16.9 us
    ppermute x12, starting transfers between devices, ring_zx(): return lax.ppermute(x, ('core', 'z', 'x'), pairs)  15.9 us
    ppermute x15, starting transfers between devices, ring_y(): return lax.ppermute(x, 'y', [(i, (i + step) % RING) for i in range(RING)])  15 us
    pallas_call x2, Pallas kernels, expand(): pl.pallas_call(functools.partial(expand_kernel, flip), grid=(2, tiles), o...  14.2 us
    ppermute x12, waiting for transfers between devices, ring_zx(): return lax.ppermute(x, ('core', 'z', 'x'), pairs)  12.2 us
    all_to_all x2, waiting for transfers between devices, columns(): lax.all_to_all(samp, ('z', 'x'), split_axis=0, concat_axis=0, tiled=True)  10.6 us
  transfers between devices with their start and end apart: 44, of which 17 were waited for; matrix products, arithmetic and copies ran while one was open for 10% of the time, Pallas kernels for 9%

profile of v1, /device:TPU:1, one launch (start us, length us, event | category | flops | bytes accessed | tf_op | source)
XLA Modules:
  0.0 207.0 jit_solution(13130326957790628188)
XLA Ops:
  0.7 4.3 %convolution_convert_fusion.1 = bf16[2,320,1024]{2,1,0:T(8,128)(2,1)S(1)} fusion(bf16[2,1024,1024]{2,1,0:T(8,128)(2,1)} %refs_8_.3, bf16[320,2,1024]{2,1,0:T(2,128)(2,1)} %param.8), kind=kOutput, calls=%fused_computation.5 | convolution fusion | flops 1342832640 | bytes 6815744 | tf_op jit(solution)/shard_map/scn,cnr->csr/dot_general | solution.py:282
  4.9 3.4 %collective-permute-start = (bf16[4,160,1024]{2,1,0:T(8,128)(2,1)S(1)}, bf16[4,160,1024]{2,1,0:T(8,128)(2,1)S(1)}, u32[]{:S(2)}, u32[]{:S(2)}) collective-permute-start(bf16[4,160,1024]{2,1,0:T(8,128)(2,1)S(1)} %bitcast.80), channel_id=1, source_target_pairs={{16,0},{17,1},{18,2},{19,3},{20,4},{21,5},{22,6},{23,7},{24,8},{25... | collective-permute-start | bytes 3932168 | tf_op jit(solution)/shard_map/ppermute | solution.py:284
  12.5 3.8 %collective-permute-done.1.u_got = bf16[4,160,1024]{2,1,0:T(8,128)(2,1)} collective-permute-done((bf16[4,160,1024]{2,1,0:T(8,128)(2,1)}, bf16[4,160,1024]{2,1,0:T(8,128)(2,1)}, u32[]{:S(2)}, u32[]{:S(2)}) %collective-permute-start.1) | collective-permute-done | bytes 1310752 | tf_op jit(solution)/shard_map/ppermute | solution.py:287
  16.3 3.1 %shard_map.77 = (bf16[160,1024]{1,0:T(8,128)(2,1)S(1)}, bf16[160,1024]{1,0:T(8,128)(2,1)}, bf16[160,1024]{1,0:T(8,128)(2,1)S(1)}, bf16[160,1024]{1,0:T(8,128)(2,1)}) custom-call(s32[2]{0:T(128)S(1)} %pad_add_fusion.place, bf16[4,160,1024]{2,1,0:T(8,128)(2,1)S(1)} %bitcast.81, bf16[4,160,1024]{2,1,0:T(8,128)(2,1)S(1)} %collective-permute-done.v_got, ...), custom_call_target="tpu_custom_call" | custom-call | tf_op jit(solution)/shard_map/pallas_call | solution.py:80
  24.8 3.1 %dynamic-slice_bitcast_fusion = bf16[1024,1024]{0,1:T(8,128)(2,1)} fusion(bf16[2,1024,1024]{2,1,0:T(8,128)(2,1)} %param.11, s32[]{:T(128)S(6)} %select_n.124), kind=kLoop, calls=%fused_computation.3 | loop fusion | bytes 4194308 | tf_op jit(solution)/shard_map/transpose | solution.py:294
  27.9 3.9 %copy.36 = bf16[1024,1024]{1,0:T(8,128)(2,1)} copy(bf16[1024,1024]{0,1:T(8,128)(2,1)} %dynamic-slice_bitcast_fusion) | data formatting | bytes 4194304 | tf_op jit(solution)/shard_map/transpose | solution.py:294
  57.1 3.3 %collective-permute-start.17 = (bf16[4,48,1024]{2,1,0:T(8,128)(2,1)S(1)}, bf16[4,48,1024]{2,1,0:T(8,128)(2,1)S(1)}, u32[]{:S(2)}, u32[]{:S(2)}) collective-permute-start(bf16[4,48,1024]{2,1,0:T(8,128)(2,1)S(1)} %pad_maximum_fusion.refs_0_), channel_id=1, source_target_pairs={{0,3},{1,0},{2,1},{3,2},{4,7},{5,4},{6,5},{7,6},{8,11},{9,8},{10,9... | collective-permute-start | bytes 1179656 | tf_op jit(solution)/shard_map/ppermute | solution.py:35
  61.3 4.8 %collective-permute-start.18 = (bf16[4,48,1024]{2,1,0:T(8,128)(2,1)S(1)}, bf16[4,48,1024]{2,1,0:T(8,128)(2,1)S(1)}, u32[]{:S(2)}, u32[]{:S(2)}) collective-permute-start(bf16[4,48,1024]{2,1,0:T(8,128)(2,1)S(1)} %pad_maximum_fusion.refs_0_), channel_id=1, source_target_pairs={{0,16},{16,0},{1,17},{17,1},{2,18},{18,2},{3,19},{19,3},{4,20},{20... | collective-permute-start | bytes 1179656 | tf_op jit(solution)/shard_map/ppermute | solution.py:23
  66.1 3.3 %collective-permute-done.17.refs_3_ = bf16[4,48,1024]{2,1,0:T(8,128)(2,1)S(1)} collective-permute-done((bf16[4,48,1024]{2,1,0:T(8,128)(2,1)S(1)}, bf16[4,48,1024]{2,1,0:T(8,128)(2,1)S(1)}, u32[]{:S(2)}, u32[]{:S(2)}) %collective-permute-start.17) | collective-permute-done | bytes 393248 | tf_op jit(solution)/shard_map/ppermute | solution.py:35
  69.4 4.9 %collective-permute-start.21 = (bf16[4,48,1024]{2,1,0:T(8,128)(2,1)S(1)}, bf16[4,48,1024]{2,1,0:T(8,128)(2,1)}, u32[]{:S(2)}, u32[]{:S(2)}) collective-permute-start(bf16[4,48,1024]{2,1,0:T(8,128)(2,1)S(1)} %collective-permute-done.17.refs_3_), channel_id=1, source_target_pairs={{0,16},{16,0},{1,17},{17,1},{2,18},{18,2},{3,19},{19,3},{4,20},{20... | collective-permute-start | bytes 1179656 | tf_op jit(solution)/shard_map/ppermute | solution.py:23
  74.3 3.9 %collective-permute-start.19 = (bf16[4,48,1024]{2,1,0:T(8,128)(2,1)S(1)}, bf16[4,48,1024]{2,1,0:T(8,128)(2,1)}, u32[]{:S(2)}, u32[]{:S(2)}) collective-permute-start(bf16[4,48,1024]{2,1,0:T(8,128)(2,1)S(1)} %collective-permute-done.15.refs_1_), channel_id=1, source_target_pairs={{0,16},{16,0},{1,17},{17,1},{2,18},{18,2},{3,19},{19,3},{4,20},{20... | collective-permute-start | bytes 1179656 | tf_op jit(solution)/shard_map/ppermute | solution.py:23
  83.1 6.8 %shard_map.81 = bf16[2,320,1024]{2,1,0:T(8,128)(2,1)S(1)} custom-call(s32[3]{0:T(128)S(1)} %get-tuple-element.70.place, bf16[4,48,1024]{2,1,0:T(8,128)(2,1)S(1)} %pad_maximum_fusion.refs_0_, bf16[4,48,1024]{2,1,0:T(8,128)(2,1)S(1)} %collective-permute-done.15.refs_1_, bf16[4,48,1024]{2,1,0:T(8,128)(2,1)S(1)} %collective-permute-done.16.refs_2_, ...), custom_call_target="tpu_custom_call" | custom-call | tf_op jit(solution)/shard_map/pallas_call | solution.py:193
  91.6 3.7 %all-to-all-start = ((bf16[320,16,128]{2,1,0:T(8,128)(2,1)}), bf16[320,16,128]{2,1,0:T(8,128)(2,1)S(1)}, u32[]{:S(2)}, u32[]{:S(2)}) async-start(bf16[320,16,128]{2,1,0:T(8,128)(2,1)} %copy_bitcast_fusion.1), calls=%async_computation | async-start | bytes 2621440 | tf_op jit(solution)/shard_map/all_to_all | solution.py:326
  104.0 7.4 %shard_map.84 = bf16[2,320,1024]{2,1,0:T(8,128)(2,1)S(1)} custom-call(s32[3]{0:T(128)S(1)} %get-tuple-element.71.place, bf16[4,48,1024]{2,1,0:T(8,128)(2,1)S(1)} %pad_maximum_fusion.refs_0_, bf16[4,48,1024]{2,1,0:T(8,128)(2,1)S(1)} %copy-done.8, bf16[4,48,1024]{2,1,0:T(8,128)(2,1)S(1)} %copy-done.6, ...), custom_call_target="tpu_custom_call" | custom-call | tf_op jit(solution)/shard_map/pallas_call | solution.py:193
  115.6 4.2 %all-to-all-start.1 = ((bf16[320,16,128]{2,1,0:T(8,128)(2,1)}), bf16[320,16,128]{2,1,0:T(8,128)(2,1)S(1)}, u32[]{:S(2)}, u32[]{:S(2)}) async-start(bf16[320,16,128]{2,1,0:T(8,128)(2,1)} %copy_bitcast_fusion), calls=%async_computation.1 | async-start | bytes 2621440 | tf_op jit(solution)/shard_map/all_to_all | solution.py:326
  121.4 3.4 %shard_map.82 = (bf16[20,64,128]{2,1,0:T(8,128)(2,1)S(1)}, bf16[20,64,128]{2,1,0:T(8,128)(2,1)}, bf16[20,64,128]{2,1,0:T(8,128)(2,1)}, bf16[20,64,128]{2,1,0:T(8...) custom-call(bf16[512,256]{1,0:T(8,128)(2,1)S(1)} %fusion.3.selector,, ...), custom_call_target="tpu_custom_call" | custom-call | tf_op jit(solution)/shard_map/pallas_call | solution.py:230
  129.9 8.0 %all-to-all-done.1 = bf16[320,16,128]{2,1,0:T(8,128)(2,1)S(1)} async-done(((bf16[320,16,128]{2,1,0:T(8,128)(2,1)}), bf16[320,16,128]{2,1,0:T(8,128)(2,1)S(1)}, u32[]{:S(2)}, u32[]{:S(2)}) %all-to-all-start.1) | async-done | bytes 1310752 | tf_op jit(solution)/shard_map/all_to_all | solution.py:326
  138.0 3.1 %shard_map.85 = (bf16[20,64,128]{2,1,0:T(8,128)(2,1)S(1)}, bf16[20,64,128]{2,1,0:T(8,128)(2,1)}, bf16[20,64,128]{2,1,0:T(8,128)(2,1)}, bf16[20,64,128]{2,1,0:T(8...) custom-call(bf16[512,256]{1,0:T(8,128)(2,1)S(1)} %fusion.3.selector,, ...), custom_call_target="tpu_custom_call" | custom-call | tf_op jit(solution)/shard_map/pallas_call | solution.py:230
  142.6 3.4 %collective-permute-start.28 = (bf16[20,64,128]{2,1,0:T(8,128)(2,1)}, bf16[20,64,128]{2,1,0:T(8,128)(2,1)S(1)}, u32[]{:S(2)}, u32[]{:S(2)}) collective-permute-start(bf16[20,64,128]{2,1,0:T(8,128)(2,1)} %get-tuple-element.52), channel_id=1, source_target_pairs={{0,16},{16,0},{1,17},{17,1},{2,18},{18,2},{3,19},{19,3},{4,20},{20... | collective-permute-start | bytes 983048 | tf_op jit(solution)/shard_map/ppermute | solution.py:23
  150.3 12.5 %collective-permute-done.32.refs_1_ = bf16[20,64,128]{2,1,0:T(8,128)(2,1)S(1)} collective-permute-done((bf16[20,64,128]{2,1,0:T(8,128)(2,1)}, bf16[20,64,128]{2,1,0:T(8,128)(2,1)S(1)}, u32[]{:S(2)}, u32[]{:S(2)}) %collective-permute-start.32) | collective-permute-done | bytes 327712 | tf_op jit(solution)/shard_map/ppermute | solution.py:19
  169.8 9.9 %collective-permute-done.27.refs_5_ = bf16[20,64,128]{2,1,0:T(8,128)(2,1)S(1)} collective-permute-done((bf16[20,64,128]{2,1,0:T(8,128)(2,1)}, bf16[20,64,128]{2,1,0:T(8,128)(2,1)S(1)}, u32[]{:S(2)}, u32[]{:S(2)}) %collective-permute-start.27) | collective-permute-done | bytes 327712 | tf_op jit(solution)/shard_map/ppermute | solution.py:19
  186.7 3.7 %shard_map.83 = f32[20,256,128]{2,1,0:T(8,128)} custom-call(bf16[256,512]{1,0:T(8,128)(2,1)S(1)} %fusion.2.placer, bf16[20,64,128]{2,1,0:T(8,128)(2,1)S(1)} %get-tuple-element.46.refs_0_, bf16[20,64,128]{2,1,0:T(8,128)(2,1)S(1)} %collective-permute-done.22.refs_1_, bf16[20,64,128]{2,1,0:T(8,128)(2,1)S(1)} %collective-permute-done.23.refs_2_, ...), custom_call_target="tpu_custom_call" | custom-call | tf_op jit(solution)/shard_map/pallas_call | solution.py:252
  193.6 8.1 %collective-permute-done.41.refs_7_ = bf16[20,64,128]{2,1,0:T(8,128)(2,1)} collective-permute-done((bf16[20,64,128]{2,1,0:T(8,128)(2,1)}, bf16[20,64,128]{2,1,0:T(8,128)(2,1)}, u32[]{:S(2)}, u32[]{:S(2)}) %collective-permute-start.41) | collective-permute-done | bytes 327712 | tf_op jit(solution)/shard_map/ppermute | solution.py:19
  201.7 5.3 %shard_map.86 = f32[20,256,128]{2,1,0:T(8,128)} custom-call(bf16[256,512]{1,0:T(8,128)(2,1)S(1)} %fusion.2.placer, bf16[20,64,128]{2,1,0:T(8,128)(2,1)S(1)} %get-tuple-element.54.refs_0_, bf16[20,64,128]{2,1,0:T(8,128)(2,1)S(1)} %collective-permute-done.32.refs_1_, bf16[20,64,128]{2,1,0:T(8,128)(2,1)S(1)} %collective-permute-done.33.refs_2_, ...), custom_call_target="tpu_custom_call" | custom-call | tf_op jit(solution)/shard_map/pallas_call | solution.py:252
  (167 shorter events, 84.6 us)
Async XLA Ops:
  19.4 12.4 %collective-permute-start.2 = (bf16[160,1024]{1,0:T(8,128)(2,1)}, bf16[160,1024]{1,0:T(8,128)(2,1)S(1)}, u32[]{:S(2)}, u32[]{:S(2)}) collective-permute-start(bf16[160,1024]{1,0:T(8,128)(2,1)} %get-tuple-element.39), channel_id=1, source_target_pairs={{0,1},{1,2},{2,3},{3,0},{4,5},{5,6},{6,7},{7,4},{8,9},{9,10},{10,1... | collective-permute-start | bytes 983048 | tf_op jit(solution)/shard_map/ppermute | solution.py:35
  24.7 12.4 %collective-permute-start.8 = (f32[32]{0:T(128)S(1)}, f32[32]{0:T(128)S(1)}, u32[]{:S(2)}, u32[]{:S(2)}) collective-permute-start(f32[32]{0:T(128)S(1)} %add_convert_fusion), channel_id=1, source_target_pairs={{0,16},{16,0},{1,17},{17,1},{2,18},{18,2},{3,19},{19,3},{4,20},{20... | collective-permute-start | bytes 392 | tf_op jit(solution)/shard_map/ppermute | solution.py:23
  60.5 13.8 %collective-permute-start.16 = (bf16[4,48,1024]{2,1,0:T(8,128)(2,1)S(1)}, bf16[4,48,1024]{2,1,0:T(8,128)(2,1)S(1)}, u32[]{:S(2)}, u32[]{:S(2)}) collective-permute-start(bf16[4,48,1024]{2,1,0:T(8,128)(2,1)S(1)} %pad_maximum_fusion.refs_0_), channel_id=1, source_target_pairs={{0,2},{1,3},{2,0},{3,1},{4,6},{5,7},{6,4},{7,5},{8,10},{9,11},{10,... | collective-permute-start | bytes 1179656 | tf_op jit(solution)/shard_map/ppermute | solution.py:35
  60.7 13.6 %collective-permute-start.15 = (bf16[4,48,1024]{2,1,0:T(8,128)(2,1)S(1)}, bf16[4,48,1024]{2,1,0:T(8,128)(2,1)S(1)}, u32[]{:S(2)}, u32[]{:S(2)}) collective-permute-start(bf16[4,48,1024]{2,1,0:T(8,128)(2,1)S(1)} %pad_maximum_fusion.refs_0_), channel_id=1, source_target_pairs={{0,1},{1,2},{2,3},{3,0},{4,5},{5,6},{6,7},{7,4},{8,9},{9,10},{10,1... | collective-permute-start | bytes 1179656 | tf_op jit(solution)/shard_map/ppermute | solution.py:35
  61.3 19.5 %collective-permute-start.18 = (bf16[4,48,1024]{2,1,0:T(8,128)(2,1)S(1)}, bf16[4,48,1024]{2,1,0:T(8,128)(2,1)S(1)}, u32[]{:S(2)}, u32[]{:S(2)}) collective-permute-start(bf16[4,48,1024]{2,1,0:T(8,128)(2,1)S(1)} %pad_maximum_fusion.refs_0_), channel_id=1, source_target_pairs={{0,16},{16,0},{1,17},{17,1},{2,18},{18,2},{3,19},{19,3},{4,20},{20... | collective-permute-start | bytes 1179656 | tf_op jit(solution)/shard_map/ppermute | solution.py:23
  91.6 23.9 %all-to-all-start = ((bf16[320,16,128]{2,1,0:T(8,128)(2,1)}), bf16[320,16,128]{2,1,0:T(8,128)(2,1)S(1)}, u32[]{:S(2)}, u32[]{:S(2)}) async-start(bf16[320,16,128]{2,1,0:T(8,128)(2,1)} %copy_bitcast_fusion.1), calls=%async_computation | async-start | bytes 2621440 | tf_op jit(solution)/shard_map/all_to_all | solution.py:326
  115.6 22.4 %all-to-all-start.1 = ((bf16[320,16,128]{2,1,0:T(8,128)(2,1)}), bf16[320,16,128]{2,1,0:T(8,128)(2,1)S(1)}, u32[]{:S(2)}, u32[]{:S(2)}) async-start(bf16[320,16,128]{2,1,0:T(8,128)(2,1)} %copy_bitcast_fusion), calls=%async_computation.1 | async-start | bytes 2621440 | tf_op jit(solution)/shard_map/all_to_all | solution.py:326
  124.8 17.8 %collective-permute-start.22 = (bf16[20,64,128]{2,1,0:T(8,128)(2,1)}, bf16[20,64,128]{2,1,0:T(8,128)(2,1)S(1)}, u32[]{:S(2)}, u32[]{:S(2)}) collective-permute-start(bf16[20,64,128]{2,1,0:T(8,128)(2,1)} %get-tuple-element.47), channel_id=1, source_target_pairs={{0,32},{32,64},{64,96},{96,0},{1,33},{33,65},{65,97},{97,1},{2,34}... | collective-permute-start | bytes 983048 | tf_op jit(solution)/shard_map/ppermute | solution.py:19
  124.8 21.2 %collective-permute-start.23 = (bf16[20,64,128]{2,1,0:T(8,128)(2,1)}, bf16[20,64,128]{2,1,0:T(8,128)(2,1)S(1)}, u32[]{:S(2)}, u32[]{:S(2)}) collective-permute-start(bf16[20,64,128]{2,1,0:T(8,128)(2,1)} %get-tuple-element.48), channel_id=1, source_target_pairs={{0,64},{32,96},{64,0},{96,32},{1,65},{33,97},{65,1},{97,33},{2,66}... | collective-permute-start | bytes 983048 | tf_op jit(solution)/shard_map/ppermute | solution.py:19
  126.3 19.8 %collective-permute-start.24 = (bf16[20,64,128]{2,1,0:T(8,128)(2,1)}, bf16[20,64,128]{2,1,0:T(8,128)(2,1)S(1)}, u32[]{:S(2)}, u32[]{:S(2)}) collective-permute-start(bf16[20,64,128]{2,1,0:T(8,128)(2,1)} %get-tuple-element.49), channel_id=1, source_target_pairs={{0,96},{32,0},{64,32},{96,64},{1,97},{33,1},{65,33},{97,65},{2,98}... | collective-permute-start | bytes 983048 | tf_op jit(solution)/shard_map/ppermute | solution.py:19
  127.6 18.5 %collective-permute-start.25 = (bf16[20,64,128]{2,1,0:T(8,128)(2,1)}, bf16[20,64,128]{2,1,0:T(8,128)(2,1)S(1)}, u32[]{:S(2)}, u32[]{:S(2)}) collective-permute-start(bf16[20,64,128]{2,1,0:T(8,128)(2,1)} %get-tuple-element.50), channel_id=1, source_target_pairs={{0,16},{16,0},{1,17},{17,1},{2,18},{18,2},{3,19},{19,3},{4,20},{20... | collective-permute-start | bytes 983048 | tf_op jit(solution)/shard_map/ppermute | solution.py:23
  129.9 17.7 %collective-permute-start.26 = (bf16[20,64,128]{2,1,0:T(8,128)(2,1)}, bf16[20,64,128]{2,1,0:T(8,128)(2,1)}, u32[]{:S(2)}, u32[]{:S(2)}) collective-permute-start(bf16[20,64,128]{2,1,0:T(8,128)(2,1)} %get-tuple-element.51), channel_id=1, source_target_pairs={{0,16},{16,0},{1,17},{17,1},{2,18},{18,2},{3,19},{19,3},{4,20},{20... | collective-permute-start | bytes 983048 | tf_op jit(solution)/shard_map/ppermute | solution.py:23
  146.1 16.8 %collective-permute-start.32 = (bf16[20,64,128]{2,1,0:T(8,128)(2,1)}, bf16[20,64,128]{2,1,0:T(8,128)(2,1)S(1)}, u32[]{:S(2)}, u32[]{:S(2)}) collective-permute-start(bf16[20,64,128]{2,1,0:T(8,128)(2,1)} %get-tuple-element.55), channel_id=1, source_target_pairs={{0,32},{32,64},{64,96},{96,0},{1,33},{33,65},{65,97},{97,1},{2,34}... | collective-permute-start | bytes 983048 | tf_op jit(solution)/shard_map/ppermute | solution.py:19
  146.1 16.7 %collective-permute-start.33 = (bf16[20,64,128]{2,1,0:T(8,128)(2,1)}, bf16[20,64,128]{2,1,0:T(8,128)(2,1)S(1)}, u32[]{:S(2)}, u32[]{:S(2)}) collective-permute-start(bf16[20,64,128]{2,1,0:T(8,128)(2,1)} %get-tuple-element.56), channel_id=1, source_target_pairs={{0,64},{32,96},{64,0},{96,32},{1,65},{33,97},{65,1},{97,33},{2,66}... | collective-permute-start | bytes 983048 | tf_op jit(solution)/shard_map/ppermute | solution.py:19
  147.7 16.4 %collective-permute-start.36 = (bf16[20,64,128]{2,1,0:T(8,128)(2,1)}, bf16[20,64,128]{2,1,0:T(8,128)(2,1)S(1)}, u32[]{:S(2)}, u32[]{:S(2)}) collective-permute-start(bf16[20,64,128]{2,1,0:T(8,128)(2,1)} %get-tuple-element.59), channel_id=1, source_target_pairs={{0,16},{16,0},{1,17},{17,1},{2,18},{18,2},{3,19},{19,3},{4,20},{20... | collective-permute-start | bytes 983048 | tf_op jit(solution)/shard_map/ppermute | solution.py:23
  149.6 16.9 %collective-permute-start.38 = (bf16[20,64,128]{2,1,0:T(8,128)(2,1)}, bf16[20,64,128]{2,1,0:T(8,128)(2,1)}, u32[]{:S(2)}, u32[]{:S(2)}) collective-permute-start(bf16[20,64,128]{2,1,0:T(8,128)(2,1)} %copy-done.18), channel_id=1, source_target_pairs={{0,16},{16,0},{1,17},{17,1},{2,18},{18,2},{3,19},{19,3},{4,20},{20... | collective-permute-start | bytes 983048 | tf_op jit(solution)/shard_map/ppermute | solution.py:23
  149.7 17.5 %collective-permute-start.40 = (bf16[20,64,128]{2,1,0:T(8,128)(2,1)}, bf16[20,64,128]{2,1,0:T(8,128)(2,1)}, u32[]{:S(2)}, u32[]{:S(2)}) collective-permute-start(bf16[20,64,128]{2,1,0:T(8,128)(2,1)} %copy-done.17), channel_id=1, source_target_pairs={{0,16},{16,0},{1,17},{17,1},{2,18},{18,2},{3,19},{19,3},{4,20},{20... | collective-permute-start | bytes 983048 | tf_op jit(solution)/shard_map/ppermute | solution.py:23
  162.8 16.8 %collective-permute-start.27 = (bf16[20,64,128]{2,1,0:T(8,128)(2,1)}, bf16[20,64,128]{2,1,0:T(8,128)(2,1)S(1)}, u32[]{:S(2)}, u32[]{:S(2)}) collective-permute-start(bf16[20,64,128]{2,1,0:T(8,128)(2,1)} %collective-permute-done.26), channel_id=1, source_target_pairs={{0,32},{32,64},{64,96},{96,0},{1,33},{33,65},{65,97},{97,1},{2,34}... | collective-permute-start | bytes 983048 | tf_op jit(solution)/shard_map/ppermute | solution.py:19
  162.9 16.8 %collective-permute-start.29 = (bf16[20,64,128]{2,1,0:T(8,128)(2,1)}, bf16[20,64,128]{2,1,0:T(8,128)(2,1)S(1)}, u32[]{:S(2)}, u32[]{:S(2)}) collective-permute-start(bf16[20,64,128]{2,1,0:T(8,128)(2,1)} %copy-done.22), channel_id=1, source_target_pairs={{0,64},{32,96},{64,0},{96,32},{1,65},{33,97},{65,1},{97,33},{2,66}... | collective-permute-start | bytes 983048 | tf_op jit(solution)/shard_map/ppermute | solution.py:19
  164.8 16.1 %collective-permute-start.31 = (bf16[20,64,128]{2,1,0:T(8,128)(2,1)}, bf16[20,64,128]{2,1,0:T(8,128)(2,1)S(1)}, u32[]{:S(2)}, u32[]{:S(2)}) collective-permute-start(bf16[20,64,128]{2,1,0:T(8,128)(2,1)} %collective-permute-done.30), channel_id=1, source_target_pairs={{0,96},{32,0},{64,32},{96,64},{1,97},{33,1},{65,33},{97,65},{2,98}... | collective-permute-start | bytes 983048 | tf_op jit(solution)/shard_map/ppermute | solution.py:19
  166.5 23.9 %collective-permute-start.34 = (bf16[20,64,128]{2,1,0:T(8,128)(2,1)}, bf16[20,64,128]{2,1,0:T(8,128)(2,1)S(1)}, u32[]{:S(2)}, u32[]{:S(2)}) collective-permute-start(bf16[20,64,128]{2,1,0:T(8,128)(2,1)} %copy-done.16), channel_id=1, source_target_pairs={{0,96},{32,0},{64,32},{96,64},{1,97},{33,1},{65,33},{97,65},{2,98}... | collective-permute-start | bytes 983048 | tf_op jit(solution)/shard_map/ppermute | solution.py:19
  167.2 23.2 %collective-permute-start.35 = (bf16[20,64,128]{2,1,0:T(8,128)(2,1)}, bf16[20,64,128]{2,1,0:T(8,128)(2,1)}, u32[]{:S(2)}, u32[]{:S(2)}) collective-permute-start(bf16[20,64,128]{2,1,0:T(8,128)(2,1)} %copy-done.15), channel_id=1, source_target_pairs={{0,16},{16,0},{1,17},{17,1},{2,18},{18,2},{3,19},{19,3},{4,20},{20... | collective-permute-start | bytes 983048 | tf_op jit(solution)/shard_map/ppermute | solution.py:23
  180.4 13.2 %collective-permute-start.39 = (bf16[20,64,128]{2,1,0:T(8,128)(2,1)}, bf16[20,64,128]{2,1,0:T(8,128)(2,1)}, u32[]{:S(2)}, u32[]{:S(2)}) collective-permute-start(bf16[20,64,128]{2,1,0:T(8,128)(2,1)} %collective-permute-done.38), channel_id=1, source_target_pairs={{0,64},{32,96},{64,0},{96,32},{1,65},{33,97},{65,1},{97,33},{2,66}... | collective-permute-start | bytes 983048 | tf_op jit(solution)/shard_map/ppermute | solution.py:19
  181.7 20.0 %collective-permute-start.41 = (bf16[20,64,128]{2,1,0:T(8,128)(2,1)}, bf16[20,64,128]{2,1,0:T(8,128)(2,1)}, u32[]{:S(2)}, u32[]{:S(2)}) collective-permute-start(bf16[20,64,128]{2,1,0:T(8,128)(2,1)} %collective-permute-done.40), channel_id=1, source_target_pairs={{0,96},{32,0},{64,32},{96,64},{1,97},{33,1},{65,33},{97,65},{2,98}... | collective-permute-start | bytes 983048 | tf_op jit(solution)/shard_map/ppermute | solution.py:19
  (44 other events, 221.3 us)

commit v2 on v1

v2 whole, which is shorter than its diff:
```python
import functools

import jax
import jax.numpy as jnp
from jax import lax
from jax.experimental import pallas as pl
from jax.experimental.pallas import tpu as pltpu
from jax.sharding import Mesh, PartitionSpec as P

BLK = 128
ALL = ("y", "core", "z", "x")
RING = 4
STEPS = (1, 3, 2)
INFO = 8
BF16, F32 = jnp.bfloat16, jnp.float32


def ring_y(x, step):
    return lax.ppermute(x, "y", [(i, (i + step) % RING) for i in range(RING)])


def swap_core(x):
    return lax.ppermute(x, "core", [(0, 1), (1, 0)])


def ring_zx(x, first, step):
    pairs = []
    for core in range(2):
        for zz in range(RING):
            for xx in range(RING):
                along_x = (core == 0) == first
                to_z = zz if along_x else (zz + step) % RING
                to_x = (xx + step) % RING if along_x else xx
                pairs.append(((core * RING + zz) * RING + xx, (core * RING + to_z) * RING + to_x))
    return lax.ppermute(x, ("core", "z", "x"), pairs)


VMEM = pl.BlockSpec(memory_space=pltpu.VMEM)
SMEM = pl.BlockSpec(memory_space=pltpu.SMEM)
HBM = pl.BlockSpec(memory_space=pltpu.HBM)
ANY = pl.BlockSpec(memory_space=pl.ANY)


def cost(flops, moved):
    return pl.CostEstimate(flops=flops, bytes_accessed=moved, transcendentals=0)


def params(mib):
    return pltpu.CompilerParams(vmem_limit_bytes=mib * 2**20)


CORE, OTHER, FIRST, SECOND, KIND = range(5)


def merge_kernel(place, v, u, v_got, u_got, *outs):
    rows = outs[0].shape[0]
    child = place[CORE]
    for k, out in enumerate(outs):
        part = lax.rem(place[FIRST] + k, RING)
        at = pl.ds(pl.multiple_of(lax.rem(part, 2) * rows, rows), rows)

        @pl.when(part < 2)
        def _():
            out[...] = (v[child, at].astype(F32) + v_got[at].astype(F32)).astype(BF16)

        @pl.when(part >= 2)
        def _():
            out[...] = (u[child, at].astype(F32) + u_got[at].astype(F32)).astype(BF16)


def merge(place, v, u, v_got, u_got):
    _, samples, rank = v.shape
    return pl.pallas_call(
        merge_kernel,
        out_shape=[jax.ShapeDtypeStruct((samples // 2, rank), BF16)] * RING,
        in_specs=[SMEM] + [VMEM] * 4,
        out_specs=[VMEM] * RING,
        compiler_params=params(16),
    )(place, v, u, v_got, u_got)


def sum_split_kernel(place, *refs):
    ins, outs = refs[:RING], refs[RING:]
    for k in range(RING):
        at = lax.rem(place[SECOND] + k, RING)
        total = ins[0][at].astype(F32)
        for part in ins[1:]:
            total = total + part[at].astype(F32)
        outs[k][...] = total.astype(BF16)


def sum_split(place, parts):
    parts = [p.reshape(RING, -1, p.shape[-1]) for p in parts]
    return pl.pallas_call(
        sum_split_kernel,
        out_shape=[jax.ShapeDtypeStruct(parts[0].shape[1:], BF16)] * RING,
        in_specs=[SMEM] + [VMEM] * RING,
        out_specs=[VMEM] * RING,
        compiler_params=params(16),
    )(place, *parts)


def sum_info_kernel(a, b, c, d, info, out):
    total = a[...].astype(F32) + b[...].astype(F32) + c[...].astype(F32) + d[...].astype(F32)
    out[...] = jnp.concatenate([total, info[...]], axis=0).astype(BF16)


def sum_info(parts, info):
    rows, rank = parts[0].shape
    return pl.pallas_call(
        sum_info_kernel,
        out_shape=jax.ShapeDtypeStruct((rows + INFO, rank), BF16),
        in_specs=[VMEM] * 5,
        out_specs=VMEM,
        compiler_params=params(16),
    )(*parts, info)


def couple_kernel(place, a, b, c, d, weight, out):
    parts = [r[...].astype(F32) for r in (a, b, c, d)]
    rows = out.shape[0] - INFO
    probe = (parts[0] + parts[1] + parts[2] + parts[3]).astype(BF16)
    infos = [p[rows : rows + 1] for p in parts] + [jnp.zeros((INFO - RING, out.shape[1]), F32)]

    def store(side):
        inner = lax.dot_general(probe, weight[...], (((1,), (side,)), ((), ())), preferred_element_type=F32)
        out[...] = jnp.concatenate([inner[:rows]] + infos, axis=0).astype(BF16)

    @pl.when(place[KIND] == 0)
    def _():
        store(1)

    @pl.when(place[KIND] == 1)
    def _():
        store(0)


def couple(place, parts, weight):
    return pl.pallas_call(
        couple_kernel,
        out_shape=jax.ShapeDtypeStruct(parts[0].shape, BF16),
        in_specs=[SMEM] + [VMEM] * 5,
        out_specs=VMEM,
        compiler_params=params(16),
    )(place, *parts, weight)


def expand_kernel(kind, own, place, *refs):
    held, (basis, probes, leaf), rest = refs[:RING], refs[RING : RING + 3], refs[RING + 3 :]
    out, lhs = rest[-2:]
    if own and kind == 0:
        out, seen, lhs = rest[-3:]
        for j in range(RING):
            for m in range(RING):
                seen[j, m] = held[j][m, -2 * INFO :, :BLK]
    child = place[CORE if own else OTHER]
    a_me, b_me = (place[FIRST], place[SECOND]) if own else (place[SECOND], place[FIRST])
    for j in range(RING):
        a = lax.rem(a_me + RING - j, RING)

        @pl.when(a // 2 == kind)
        def _():
            for m in range(RING):
                lhs[lax.rem(a, 2), lax.rem(b_me + RING - m, RING)] = held[j][m]

    rows = lhs.shape[2] - INFO
    rank = lhs.shape[3]
    _, count, size, _ = leaf.shape
    done = []
    for t in range(count):
        at = slice(t * size, (t + 1) * size)
        low = lax.dot_general(
            lhs[...].reshape(-1, rank), basis[at], (((1,), (1,)), ((), ())), preferred_element_type=F32
        )
        low = jnp.concatenate([low[i : i + rows] for i in range(0, low.shape[0], rows + INFO)], axis=0)
        near = lax.dot_general(
            probes[child, :, at], leaf[child, t], (((1,), (1 - kind,)), ((), ())), preferred_element_type=F32
        )
        done.append(low + near)
    done = jnp.concatenate(done, axis=1).reshape(done[0].shape[0], -1, BLK)
    if not own:
        done = jnp.concatenate([rest[0][...].astype(F32), done], axis=1)
    out[...] = done.astype(BF16)


def expand(kind, place, held, basis, probes, leaf_blocks, before=None):
    local, rank = basis.shape
    samples = probes.shape[1]
    own = before is None
    blocks = local // BLK * (1 if own else 2)
    rest = [] if own else [before]
    shapes = [jax.ShapeDtypeStruct((samples, blocks, BLK), BF16)]
    if own and kind == 0:
        shapes.append(jax.ShapeDtypeStruct((RING, RING, 2 * INFO, BLK), BF16))
    got = pl.pallas_call(
        functools.partial(expand_kernel, kind, own),
        in_specs=[SMEM] + [VMEM] * (RING + 3 + len(rest)),
        out_specs=[VMEM] * len(shapes),
        scratch_shapes=[pltpu.VMEM((2, RING) + held[0].shape[1:], BF16)],
        out_shape=shapes,
        compiler_params=params(24),
        cost_estimate=cost(2 * samples * local * (rank + 256), 6 * 2**20),
    )(place, *held, basis, probes, leaf_blocks, *rest)
    return got if len(got) > 1 else got[0]


GROUP = 10


def send_kernel(selector, columns, *outs):
    _, share, capacity, _ = outs[0].shape
    blocks = selector.shape[1]
    for s in range(0, share, 2):
        pair = jnp.concatenate([columns[:, s + i].reshape(blocks, BLK) for i in range(2)], axis=1)
        moved = jnp.dot(selector[...], pair, preferred_element_type=F32).astype(BF16)
        for i in range(2 * RING):
            for h in range(2):
                outs[i % RING][i // RING, s + h] = moved[
                    i * capacity : (i + 1) * capacity, h * BLK : (h + 1) * BLK
                ]


def send(selector, columns, capacity):
    cols, share, near, _ = columns.shape
    return pl.pallas_call(
        send_kernel,
        grid=(share // GROUP,),
        out_shape=[jax.ShapeDtypeStruct((2, share, capacity, BLK), BF16)] * RING,
        in_specs=[
            pl.BlockSpec(selector.shape, lambda g: (0, 0)),
            pl.BlockSpec((cols, GROUP, near, BLK), lambda g: (0, g, 0, 0)),
        ],
        out_specs=[pl.BlockSpec((2, GROUP, capacity, BLK), lambda g: (0, g, 0, 0))] * RING,
        compiler_params=params(32),
        cost_estimate=cost(2 * selector.size * share * BLK, 8 * 2**20),
    )(selector, columns)


def place_kernel(placer, *refs):
    parts, out = refs[:-1], refs[-1]
    for s in range(0, out.shape[0], 2):
        arrived = jnp.concatenate(
            [jnp.concatenate([part[0, s], part[0, s + 1]], axis=1) for part in parts], axis=0
        )
        got = jnp.dot(placer[...], arrived, preferred_element_type=F32)
        out[s] = got[:, :BLK]
        out[s + 1] = got[:, BLK:]


def place_blocks(placer, near):
    far = [swap_core(p) for p in near]
    _, share, capacity, _ = near[0].shape
    spec = lambda half: pl.BlockSpec((1, GROUP, capacity, BLK), lambda g: (half, g, 0, 0))
    return pl.pallas_call(
        place_kernel,
        grid=(share // GROUP,),
        out_shape=jax.ShapeDtypeStruct((share, placer.shape[0], BLK), F32),
        in_specs=[pl.BlockSpec(placer.shape, lambda g: (0, 0))] + [spec(0)] * RING + [spec(1)] * RING,
        out_specs=pl.BlockSpec((GROUP, placer.shape[0], BLK), lambda g: (g, 0, 0)),
        compiler_params=params(32),
        cost_estimate=cost(2 * placer.size * share * BLK, 10 * 2**20),
    )(placer, *near, *far).transpose(1, 0, 2)


def whole(*values):
    return jnp.stack(values).astype(jnp.int32)


def per_device(omega, u_basis, v_basis, coupling, leaf_blocks, child_map):
    y_me, core, z_me, x_me = (lax.axis_index(a) for a in ALL)
    samples = omega.shape[0]
    rank = u_basis.shape[2]
    rows = 2 * samples
    row_count, col_count = 2 * RING, RING * RING
    near = child_map.size
    owner_rows = near * col_count
    capacity = 2 * owner_rows // row_count
    share = samples // col_count
    a_me = jnp.where(core == 0, x_me, z_me)
    b_me = jnp.where(core == 0, z_me, x_me)

    mine = jnp.where(core == 0, child_map, child_map[::-1]).reshape(-1)
    mine = jnp.concatenate([mine // owner_rows, mine % owner_rows]).astype(F32)
    both = jnp.concatenate([mine, swap_core(mine)])
    info = jnp.zeros((INFO, rank), F32).at[0, : both.size].set(both)

    spot = whole(core, 1 - core, a_me, b_me, a_me // 2)
    probes = omega.transpose(1, 0, 2)
    own, got = [], []
    for basis in (v_basis, u_basis):
        own.append(jnp.einsum("scn,cnr->csr", omega, basis, preferred_element_type=F32).astype(BF16))
        got.append(swap_core(lax.dynamic_index_in_dim(own[-1], 1 - core, 0, keepdims=False)))
    pieces = merge(spot, *own, *got)
    coupling, u_late, pieces = lax.optimization_barrier((coupling, u_basis, pieces))
    weight = lax.dynamic_index_in_dim(coupling, core, 0, keepdims=False)
    u_parts = [lax.dynamic_index_in_dim(u_late, c, 0, keepdims=False) for c in (core, 1 - core)]
    pieces = [pieces[0]] + [ring_zx(pieces[k], True, k) for k in STEPS]
    pieces = sum_split(spot, pieces)
    pieces = [pieces[0]] + [ring_zx(pieces[k], False, k) for k in STEPS]
    piece = sum_info(pieces, info)
    inner = couple(spot, [piece] + [ring_y(piece, k) for k in (1, 2, 3)], weight)
    inner = jnp.stack([inner] + [ring_zx(inner, False, k) for k in (1, 2, 3)])
    u_parts, probes, inner = lax.optimization_barrier((u_parts, probes, inner))
    held = [inner] + [ring_zx(inner, True, k) for k in (1, 2, 3)]
    swapped = [swap_core(p) for p in held]

    first, seen = expand(0, spot, held, u_parts[0], probes, leaf_blocks)
    y_samp = expand(0, spot, swapped, u_parts[1], probes, leaf_blocks, first)
    seen, y_samp, v_late = lax.optimization_barrier((seen, y_samp, v_basis))
    v_parts = [lax.dynamic_index_in_dim(v_late, c, 0, keepdims=False) for c in (core, 1 - core)]
    first = expand(1, spot, held, v_parts[0], probes, leaf_blocks)
    z_samp = expand(1, spot, swapped, v_parts[1], probes, leaf_blocks, first)

    fields = both.size
    seen = seen[:, :, INFO : INFO + RING, :fields]
    at = jnp.arange(RING)
    z_step, x_step = (z_me - at) % RING, (x_me - at) % RING
    flat = jnp.where(
        core == 0, x_step[None, :] * RING + z_step[:, None], z_step[:, None] * RING + x_step[None, :]
    ).reshape(-1)
    seen = seen.reshape(col_count, RING, 2, 2, near)[flat].astype(jnp.int32)
    seen = seen.transpose(3, 2, 1, 0, 4).reshape(2, row_count, owner_rows)
    dest, home = seen[0], seen[1]
    same = (dest[:, :, None] == dest[:, None, :]).astype(jnp.int32)
    before = (jnp.arange(owner_rows)[None, :] < jnp.arange(owner_rows)[:, None]).astype(jnp.int32)
    order = jnp.sum(same * before[None], axis=2)

    step = (dest[0] // 2 - y_me) % RING
    slot = (jnp.where(dest[0] % 2 == core, 0, RING) + step) * capacity + order[0]
    selector = (jnp.arange(row_count * capacity)[:, None] == slot[None, :]).astype(BF16)
    arriving = jnp.where(dest == y_me * 2 + core, order, -1)
    spots = jnp.arange(capacity)
    ids = jnp.sum((spots[None, :, None] == arriving[:, None, :]) * (home + 1)[:, None, :], axis=2) - 1
    placer = (jnp.arange(owner_rows)[:, None] == ids.reshape(-1)[None, :]).astype(BF16)

    def columns(samp):
        got = lax.all_to_all(samp, ("z", "x"), split_axis=0, concat_axis=0, tiled=True)
        return got.reshape(col_count, share, near, BLK)

    y_cols = columns(y_samp)
    z_samp, y_cols = lax.optimization_barrier((z_samp, y_cols))
    y_out = send(selector, y_cols, capacity)
    y_out = [y_out[0]] + [ring_y(y_out[k], k) for k in (1, 2, 3)]
    z_out = list(send(selector, columns(z_samp), capacity))
    parent_y = place_blocks(placer, y_out)
    z_out[2], parent_y = lax.optimization_barrier((z_out[2], parent_y))
    z_out = [z_out[0]] + [ring_y(z_out[k], k) for k in (1, 2, 3)]
    return parent_y, place_blocks(placer, z_out)


def solution(mesh):
    fine = Mesh(mesh.devices.reshape(RING, 2, RING, RING), ALL)
    return jax.shard_map(
        per_device,
        mesh=fine,
        in_specs=(
            P(None, None, ALL),
            P(None, ALL, None),
            P(None, ALL, None),
            P(),
            P(None, ALL, None, None),
            P(None, ALL),
        ),
        out_specs=(P(("y", "core"), ("z", "x"), None), P(("y", "core"), ("z", "x"), None)),
        check_vma=False,
    )
```

time: 208 us -> 190 us (0.913)
  Pallas kernels: 33.5 us -> 25.8 us
  starting transfers between devices: 67.2 us -> 62.7 us
  local copies, waits for them, and re-layouts: 29.9 us -> 25.8 us
    ppermute x15 -> x9, waiting for transfers between devices: 36.9 us -> 46.7 us  [ring_y(): return lax.ppermute(x, 'y', [(i, (i + step) % RING) for i in range(RING)])]
    squeeze x0 -> x5, local copies, waits for them, and re-layouts: none -> 8.83 us  [the longest x1 2.67 us: per_device(): lax.dynamic_index_in_dim(v_late, c, 0, keepdims=False)]
    all_to_all x2, waiting for transfers between devices: 10.6 us -> 2.86 us  [columns(): lax.all_to_all(samp, ('z', 'x'), split_axis=0, concat_axis=0, tiled=True)]
    unnamed x51 -> x31, local copies, waits for them, and re-layouts: 16.9 us -> 9.21 us
    transpose x2 -> x0, local copies, waits for them, and re-layouts: 7.02 us -> none  [per_device(): weight = jnp.where(core == 0, weight.T, weight)]
    ppermute x2 -> x0, starting transfers between devices: 4.69 us -> none  [the longest x1 3.41 us: per_device(): v_got = lax.ppermute(v_own, 'core', [(1, 0)])]
    ppermute x15 -> x9, starting transfers between devices: 15 us -> 10.7 us  [ring_y(): return lax.ppermute(x, 'y', [(i, (i + step) % RING) for i in range(RING)])]
    ppermute x13 -> x15, waiting for transfers between devices: 0.03 us -> 4.32 us  [swap_core(): return lax.ppermute(x, 'core', [(0, 1), (1, 0)])]
  transfers between devices with their start and end apart: 44 -> 38, of which waited for: 17 -> 16; matrix products, arithmetic and copies ran while one was open for 10% -> 12% of each run, Pallas kernels for 9% -> 8%
where the time goes in v2:
time: 190 us; the launch traced here: 189 us
  waiting for transfers between devices  64 us (34%)
  starting transfers between devices  62.7 us (33%)
  local copies, waits for them, and re-layouts  25.8 us (14%)
  Pallas kernels  25.8 us (14%)
  matrix products  5.84 us (3%)
  other arithmetic  3.7 us (2%)
    ppermute x9, waiting for transfers between devices, ring_y(): return lax.ppermute(x, 'y', [(i, (i + step) % RING) for i in range(RING)])  46.7 us
    ppermute x15, starting transfers between devices, swap_core(): return lax.ppermute(x, 'core', [(0, 1), (1, 0)])  25.1 us
    ppermute x12, starting transfers between devices, ring_zx(): return lax.ppermute(x, ('core', 'z', 'x'), pairs)  15.9 us
    pallas_call x4, Pallas kernels, expand(): pl.pallas_call(functools.partial(expand_kernel, kind, own), in_specs=[SME...  12 us
    all_to_all x2, starting transfers between devices, columns(): lax.all_to_all(samp, ('z', 'x'), split_axis=0, concat_axis=0, tiled=True)  11.1 us
    ppermute x9, starting transfers between devices, ring_y(): return lax.ppermute(x, 'y', [(i, (i + step) % RING) for i in range(RING)])  10.7 us
    ppermute x12, waiting for transfers between devices, ring_zx(): return lax.ppermute(x, ('core', 'z', 'x'), pairs)  10 us
    unnamed x31, local copies, waits for them, and re-layouts  9.21 us
  transfers between devices with their start and end apart: 38, of which 16 were waited for; matrix products, arithmetic and copies ran while one was open for 12% of the time, Pallas kernels for 8%

profile of v2, /device:TPU:1, one launch (start us, length us, event | category | flops | bytes accessed | tf_op | source)
XLA Modules:
  0.0 188.8 jit_solution(17890439421799738611)
XLA Ops:
  0.7 4.3 %convolution_convert_fusion.1.v = bf16[2,320,1024]{2,1,0:T(8,128)(2,1)S(1)} fusion(bf16[2,1024,1024]{2,1,0:T(8,128)(2,1)} %param.10, bf16[320,2,1024]{2,1,0:T(2,128)(2,1)} %param.8), kind=kOutput, calls=%fused_computation.8 | convolution fusion | flops 1342832640 | bytes 6815744 | tf_op jit(solution)/shard_map/scn,cnr->csr/dot_general | solution.py:291
  24.8 3.2 %collective-permute-done.3 = bf16[160,1024]{1,0:T(8,128)(2,1)S(1)} collective-permute-done((bf16[160,1024]{1,0:T(8,128)(2,1)}, bf16[160,1024]{1,0:T(8,128)(2,1)S(1)}, u32[]{:S(2)}, u32[]{:S(2)}) %collective-permute-start.3) | collective-permute-done | bytes 327712 | tf_op jit(solution)/shard_map/ppermute | solution.py:35
  34.8 3.0 %collective-permute-done.7.d = bf16[40,1024]{1,0:T(8,128)(2,1)S(1)} collective-permute-done((bf16[40,1024]{1,0:T(8,128)(2,1)S(1)}, bf16[40,1024]{1,0:T(8,128)(2,1)S(1)}, u32[]{:S(2)}, u32[]{:S(2)}) %collective-permute-start.7) | collective-permute-done | bytes 81952 | tf_op jit(solution)/shard_map/ppermute | solution.py:35
  37.8 3.0 %collective-permute-start.10 = (bf16[48,1024]{1,0:T(8,128)(2,1)S(1)}, bf16[48,1024]{1,0:T(8,128)(2,1)S(1)}, u32[]{:S(2)}, u32[]{:S(2)}) collective-permute-start(bf16[48,1024]{1,0:T(8,128)(2,1)S(1)} %shard_map.79.a), channel_id=1, source_target_pairs={{0,64},{32,96},{64,0},{96,32},{1,65},{33,97},{65,1},{97,33},{2,66}... | collective-permute-start | bytes 294920 | tf_op jit(solution)/shard_map/ppermute | solution.py:19
  44.2 2.8 %collective-permute-done.9.b = bf16[48,1024]{1,0:T(8,128)(2,1)S(1)} collective-permute-done((bf16[48,1024]{1,0:T(8,128)(2,1)S(1)}, bf16[48,1024]{1,0:T(8,128)(2,1)S(1)}, u32[]{:S(2)}, u32[]{:S(2)}) %collective-permute-start.9) | collective-permute-done | bytes 98336 | tf_op jit(solution)/shard_map/ppermute | solution.py:19
  51.6 2.5 %dynamic-slice_bitcast_fusion.3 = (bf16[1024,1024]{1,0:T(8,128)(2,1)}, bf16[1024,1024]{1,0:T(8,128)(2,1)}) fusion(bf16[2,1024,1024]{2,1,0:T(8,128)(2,1)S(1)} %copy-done.10, s32[]{:T(128)S(6)} %select_n.130, s32[]{:T(128)S(6)} %select_n.131), kind=kLoop, calls=%fused_computation.5 | loop fusion | bytes 8388616 | tf_op jit(solution)/shard_map/jit(dynamic_index_in_dim)/squeeze | solution.py:296
  58.3 7.2 %collective-permute-start.18 = (bf16[4,48,1024]{2,1,0:T(8,128)(2,1)S(1)}, bf16[4,48,1024]{2,1,0:T(8,128)(2,1)S(1)}, u32[]{:S(2)}, u32[]{:S(2)}) collective-permute-start(bf16[4,48,1024]{2,1,0:T(8,128)(2,1)S(1)} %pad_maximum_fusion.refs_0_), channel_id=1, source_target_pairs={{0,16},{16,0},{1,17},{17,1},{2,18},{18,2},{3,19},{19,3},{4,20},{20... | collective-permute-start | bytes 1179656 | tf_op jit(solution)/shard_map/ppermute | solution.py:23
  65.5 3.9 %collective-permute-start.19 = (bf16[4,48,1024]{2,1,0:T(8,128)(2,1)}, bf16[4,48,1024]{2,1,0:T(8,128)(2,1)S(1)}, u32[]{:S(2)}, u32[]{:S(2)}) collective-permute-start(bf16[4,48,1024]{2,1,0:T(8,128)(2,1)} %collective-permute-done.15.refs_1_), channel_id=1, source_target_pairs={{0,16},{16,0},{1,17},{17,1},{2,18},{18,2},{3,19},{19,3},{4,20},{20... | collective-permute-start | bytes 1179656 | tf_op jit(solution)/shard_map/ppermute | solution.py:23
  69.4 4.3 %collective-permute-start.20 = (bf16[4,48,1024]{2,1,0:T(8,128)(2,1)}, bf16[4,48,1024]{2,1,0:T(8,128)(2,1)}, u32[]{:S(2)}, u32[]{:S(2)}) collective-permute-start(bf16[4,48,1024]{2,1,0:T(8,128)(2,1)} %collective-permute-done.16.refs_2_), channel_id=1, source_target_pairs={{0,16},{16,0},{1,17},{17,1},{2,18},{18,2},{3,19},{19,3},{4,20},{20... | collective-permute-start | bytes 1179656 | tf_op jit(solution)/shard_map/ppermute | solution.py:23
  76.8 2.8 %shard_map.81 = (bf16[320,8,128]{2,1,0:T(8,128)(2,1)S(1)}, bf16[4,4,16,128]{3,2,1,0:T(8,128)(2,1)S(1)}) custom-call(s32[5]{0:T(128)S(1)} %stack.38.place, bf16[4,48,1024]{2,1,0:T(8,128)(2,1)S(1)} %pad_maximum_fusion.refs_0_, bf16[4,48,1024]{2,1,0:T(8,128)(2,1)} %collective-permute-done.15.refs_1_, bf16[4,48,1024]{2,1,0:T(8,128)(2,1)} %collective-permute-done.16.refs_2_, ...), custom_call_target="tpu_custom_call" | custom-call | flops 838860800 | bytes 6291456 | tf_op jit(solution)/shard_map/pallas_call | solution.py:195
  80.3 2.6 %shard_map.82 = bf16[320,16,128]{2,1,0:T(8,128)(2,1)S(1)} custom-call(s32[5]{0:T(128)S(1)} %stack.38.place, bf16[4,48,1024]{2,1,0:T(8,128)(2,1)S(1)} %collective-permute-done.18.refs_0_, bf16[4,48,1024]{2,1,0:T(8,128)(2,1)S(1)} %collective-permute-done.19.refs_1_, bf16[4,48,1024]{2,1,0:T(8,128)(2,1)} %collective-permute-done.20.refs_2_, ...), custom_call_target="tpu_custom_call" | custom-call | flops 838860800 | bytes 6291456 | tf_op jit(solution)/shard_map/pallas_call | solution.py:195
  84.0 7.3 %all-to-all-start = ((bf16[320,16,128]{2,1,0:T(8,128)(2,1)}), bf16[320,16,128]{2,1,0:T(8,128)(2,1)}, u32[]{:S(2)}, u32[]{:S(2)}) async-start(bf16[320,16,128]{2,1,0:T(8,128)(2,1)} %copy-done.3), calls=%async_computation | async-start | bytes 2621440 | tf_op jit(solution)/shard_map/all_to_all | solution.py:337
  100.1 2.7 %dynamic-slice_bitcast_fusion = (bf16[1024,1024]{1,0:T(8,128)(2,1)S(1)}, bf16[1024,1024]{1,0:T(8,128)(2,1)S(1)}) fusion(bf16[2,1024,1024]{2,1,0:T(8,128)(2,1)} %param.10, s32[]{:T(128)S(6)} %select_n.131, s32[]{:T(128)S(6)} %select_n.130), kind=kLoop, calls=%fused_computation.1 | loop fusion | bytes 8388616 | tf_op jit(solution)/shard_map/jit(dynamic_index_in_dim)/squeeze | solution.py:310
  102.8 2.7 %shard_map.83.refs_7_ = bf16[320,8,128]{2,1,0:T(8,128)(2,1)S(1)} custom-call(s32[5]{0:T(128)S(1)} %stack.38.place, bf16[4,48,1024]{2,1,0:T(8,128)(2,1)S(1)} %pad_maximum_fusion.refs_0_, bf16[4,48,1024]{2,1,0:T(8,128)(2,1)} %collective-permute-done.15.refs_1_, bf16[4,48,1024]{2,1,0:T(8,128)(2,1)} %collective-permute-done.16.refs_2_, ...), custom_call_target="tpu_custom_call" | custom-call | flops 838860800 | bytes 6291456 | tf_op jit(solution)/shard_map/pallas_call | solution.py:195
  105.5 3.8 %shard_map.84 = bf16[320,16,128]{2,1,0:T(8,128)(2,1)} custom-call(s32[5]{0:T(128)S(1)} %stack.38.place, bf16[4,48,1024]{2,1,0:T(8,128)(2,1)S(1)} %collective-permute-done.18.refs_0_, bf16[4,48,1024]{2,1,0:T(8,128)(2,1)S(1)} %collective-permute-done.19.refs_1_, bf16[4,48,1024]{2,1,0:T(8,128)(2,1)} %collective-permute-done.20.refs_2_, ...), custom_call_target="tpu_custom_call" | custom-call | flops 838860800 | bytes 6291456 | tf_op jit(solution)/shard_map/pallas_call | solution.py:195
  110.2 2.9 %all-to-all-done = bf16[320,16,128]{2,1,0:T(8,128)(2,1)} async-done(((bf16[320,16,128]{2,1,0:T(8,128)(2,1)}), bf16[320,16,128]{2,1,0:T(8,128)(2,1)}, u32[]{:S(2)}, u32[]{:S(2)}) %all-to-all-start) | async-done | bytes 1310752 | tf_op jit(solution)/shard_map/all_to_all | solution.py:337
  113.0 3.1 %shard_map.86 = (bf16[2,20,64,128]{3,2,1,0:T(8,128)(2,1)S(1)}, bf16[2,20,64,128]{3,2,1,0:T(8,128)(2,1)}, bf16[2,20,64,128]{3,2,1,0:T(8,128)(2,1)}, bf16[2,20,64,128]{3,2,1,0:T(8,128)(2,1)}) custom-call(bf16[512,256]{1,0:T(8,128)(2,1)S(1)} %fusion.2.selector, bf16[16,20,16,128]{3,2,1,0:T(8,128)(2,1)} %bitcast.25.columns), custom_call_target="tpu_custom_call" | custom-call | flops 671088640 | bytes 8388608 | tf_op jit(solution)/shard_map/pallas_call | solution.py:225
  116.2 2.7 %collective-permute-start.24 = (bf16[2,20,64,128]{3,2,1,0:T(8,128)(2,1)}, bf16[2,20,64,128]{3,2,1,0:T(8,128)(2,1)}, u32[]{:S(2)}, u32[]{:S(2)}) collective-permute-start(bf16[2,20,64,128]{3,2,1,0:T(8,128)(2,1)} %get-tuple-element.78), channel_id=1, source_target_pairs={{0,96},{32,0},{64,32},{96,64},{1,97},{33,1},{65,33},{97,65},{2,98}... | collective-permute-start | bytes 1966088 | tf_op jit(solution)/shard_map/ppermute | solution.py:19
  118.8 3.8 %all-to-all-start.1 = ((bf16[320,16,128]{2,1,0:T(8,128)(2,1)}), bf16[320,16,128]{2,1,0:T(8,128)(2,1)S(1)}, u32[]{:S(2)}, u32[]{:S(2)}) async-start(bf16[320,16,128]{2,1,0:T(8,128)(2,1)} %shard_map.84), calls=%async_computation.1 | async-start | bytes 2621440 | tf_op jit(solution)/shard_map/all_to_all | solution.py:337
  124.3 22.5 %collective-permute-done.22.refs_1_ = bf16[2,20,64,128]{3,2,1,0:T(8,128)(2,1)} collective-permute-done((bf16[2,20,64,128]{3,2,1,0:T(8,128)(2,1)}, bf16[2,20,64,128]{3,2,1,0:T(8,128)(2,1)}, u32[]{:S(2)}, u32[]{:S(2)}) %collective-permute-start.22) | collective-permute-done | bytes 655392 | tf_op jit(solution)/shard_map/ppermute | solution.py:19
  152.4 2.7 %collective-permute-start.31 = (bf16[2,20,64,128]{3,2,1,0:T(8,128)(2,1)S(1)}, bf16[2,20,64,128]{3,2,1,0:T(8,128)(2,1)S(1)}, u32[]{:S(2)}, u32[]{:S(2)}) collective-permute-start(bf16[2,20,64,128]{3,2,1,0:T(8,128)(2,1)S(1)} %get-tuple-element.83), channel_id=1, source_target_pairs={{0,96},{32,0},{64,32},{96,64},{1,97},{33,1},{65,33},{97,65},{2,98}... | collective-permute-start | bytes 1966088 | tf_op jit(solution)/shard_map/ppermute | solution.py:19
  156.2 3.4 %shard_map.87 = f32[20,256,128]{2,1,0:T(8,128)} custom-call(bf16[256,512]{1,0:T(8,128)(2,1)S(1)} %fusion.3.placer, bf16[2,20,64,128]{3,2,1,0:T(8,128)(2,1)S(1)} %get-tuple-element.75.refs_0_, bf16[2,20,64,128]{3,2,1,0:T(8,128)(2,1)} %collective-permute-done.22.refs_1_, bf16[2,20,64,128]{3,2,1,0:T(8,128)(2,1)} %collective-permute-done.23.refs_2_, ...), custom_call_target="tpu_custom_call" | custom-call | flops 671088640 | bytes 10485760 | tf_op jit(solution)/shard_map/pallas_call | solution.py:254
  160.8 8.4 %collective-permute-done.29.refs_1_ = bf16[2,20,64,128]{3,2,1,0:T(8,128)(2,1)S(1)} collective-permute-done((bf16[2,20,64,128]{3,2,1,0:T(8,128)(2,1)S(1)}, bf16[2,20,64,128]{3,2,1,0:T(8,128)(2,1)S(1)}, u32[]{:S(2)}, u32[]{:S(2)}) %collective-permute-start.29) | collective-permute-done | bytes 655392 | tf_op jit(solution)/shard_map/ppermute | solution.py:19
  169.9 12.9 %collective-permute-done.31.refs_3_ = bf16[2,20,64,128]{3,2,1,0:T(8,128)(2,1)S(1)} collective-permute-done((bf16[2,20,64,128]{3,2,1,0:T(8,128)(2,1)S(1)}, bf16[2,20,64,128]{3,2,1,0:T(8,128)(2,1)S(1)}, u32[]{:S(2)}, u32[]{:S(2)}) %collective-permute-start.31) | collective-permute-done | bytes 655392 | tf_op jit(solution)/shard_map/ppermute | solution.py:19
  (134 shorter events, 69.5 us)
Async XLA Ops:
  16.3 8.5 %collective-permute-start.2 = (bf16[160,1024]{1,0:T(8,128)(2,1)}, bf16[160,1024]{1,0:T(8,128)(2,1)S(1)}, u32[]{:S(2)}, u32[]{:S(2)}) collective-permute-start(bf16[160,1024]{1,0:T(8,128)(2,1)} %get-tuple-element.55), channel_id=1, source_target_pairs={{0,1},{1,2},{2,3},{3,0},{4,5},{5,6},{6,7},{7,4},{8,9},{9,10},{10,1... | collective-permute-start | bytes 983048 | tf_op jit(solution)/shard_map/ppermute | solution.py:35
  18.0 10.0 %collective-permute-start.3 = (bf16[160,1024]{1,0:T(8,128)(2,1)}, bf16[160,1024]{1,0:T(8,128)(2,1)S(1)}, u32[]{:S(2)}, u32[]{:S(2)}) collective-permute-start(bf16[160,1024]{1,0:T(8,128)(2,1)} %get-tuple-element.56), channel_id=1, source_target_pairs={{0,3},{1,0},{2,1},{3,2},{4,7},{5,4},{6,5},{7,6},{8,11},{9,8},{10,9... | collective-permute-start | bytes 983048 | tf_op jit(solution)/shard_map/ppermute | solution.py:35
  20.1 9.4 %collective-permute-start.4 = (bf16[160,1024]{1,0:T(8,128)(2,1)}, bf16[160,1024]{1,0:T(8,128)(2,1)S(1)}, u32[]{:S(2)}, u32[]{:S(2)}) collective-permute-start(bf16[160,1024]{1,0:T(8,128)(2,1)} %get-tuple-element.57), channel_id=1, source_target_pairs={{0,2},{1,3},{2,0},{3,1},{4,6},{5,7},{6,4},{7,5},{8,10},{9,11},{10,... | collective-permute-start | bytes 983048 | tf_op jit(solution)/shard_map/ppermute | solution.py:35
  21.5 13.0 %collective-permute-start.8 = (f32[32]{0:T(128)S(1)}, f32[32]{0:T(128)S(1)}, u32[]{:S(2)}, u32[]{:S(2)}) collective-permute-start(f32[32]{0:T(128)S(1)} %add_convert_fusion), channel_id=1, source_target_pairs={{0,16},{16,0},{1,17},{17,1},{2,18},{18,2},{3,19},{19,3},{4,20},{20... | collective-permute-start | bytes 392 | tf_op jit(solution)/shard_map/ppermute | solution.py:23
  37.8 6.4 %collective-permute-start.10 = (bf16[48,1024]{1,0:T(8,128)(2,1)S(1)}, bf16[48,1024]{1,0:T(8,128)(2,1)S(1)}, u32[]{:S(2)}, u32[]{:S(2)}) collective-permute-start(bf16[48,1024]{1,0:T(8,128)(2,1)S(1)} %shard_map.79.a), channel_id=1, source_target_pairs={{0,64},{32,96},{64,0},{96,32},{1,65},{33,97},{65,1},{97,33},{2,66}... | collective-permute-start | bytes 294920 | tf_op jit(solution)/shard_map/ppermute | solution.py:19
  54.8 10.7 %collective-permute-start.15 = (bf16[4,48,1024]{2,1,0:T(8,128)(2,1)S(1)}, bf16[4,48,1024]{2,1,0:T(8,128)(2,1)}, u32[]{:S(2)}, u32[]{:S(2)}) collective-permute-start(bf16[4,48,1024]{2,1,0:T(8,128)(2,1)S(1)} %pad_maximum_fusion.refs_0_), channel_id=1, source_target_pairs={{0,1},{1,2},{2,3},{3,0},{4,5},{5,6},{6,7},{7,4},{8,9},{9,10},{10,1... | collective-permute-start | bytes 1179656 | tf_op jit(solution)/shard_map/ppermute | solution.py:35
  55.6 13.7 %collective-permute-start.16 = (bf16[4,48,1024]{2,1,0:T(8,128)(2,1)S(1)}, bf16[4,48,1024]{2,1,0:T(8,128)(2,1)}, u32[]{:S(2)}, u32[]{:S(2)}) collective-permute-start(bf16[4,48,1024]{2,1,0:T(8,128)(2,1)S(1)} %pad_maximum_fusion.refs_0_), channel_id=1, source_target_pairs={{0,2},{1,3},{2,0},{3,1},{4,6},{5,7},{6,4},{7,5},{8,10},{9,11},{10,... | collective-permute-start | bytes 1179656 | tf_op jit(solution)/shard_map/ppermute | solution.py:35
  57.6 16.0 %collective-permute-start.17 = (bf16[4,48,1024]{2,1,0:T(8,128)(2,1)S(1)}, bf16[4,48,1024]{2,1,0:T(8,128)(2,1)}, u32[]{:S(2)}, u32[]{:S(2)}) collective-permute-start(bf16[4,48,1024]{2,1,0:T(8,128)(2,1)S(1)} %pad_maximum_fusion.refs_0_), channel_id=1, source_target_pairs={{0,3},{1,0},{2,1},{3,2},{4,7},{5,4},{6,5},{7,6},{8,11},{9,8},{10,9... | collective-permute-start | bytes 1179656 | tf_op jit(solution)/shard_map/ppermute | solution.py:35
  58.3 21.4 %collective-permute-start.18 = (bf16[4,48,1024]{2,1,0:T(8,128)(2,1)S(1)}, bf16[4,48,1024]{2,1,0:T(8,128)(2,1)S(1)}, u32[]{:S(2)}, u32[]{:S(2)}) collective-permute-start(bf16[4,48,1024]{2,1,0:T(8,128)(2,1)S(1)} %pad_maximum_fusion.refs_0_), channel_id=1, source_target_pairs={{0,16},{16,0},{1,17},{17,1},{2,18},{18,2},{3,19},{19,3},{4,20},{20... | collective-permute-start | bytes 1179656 | tf_op jit(solution)/shard_map/ppermute | solution.py:23
  65.5 14.2 %collective-permute-start.19 = (bf16[4,48,1024]{2,1,0:T(8,128)(2,1)}, bf16[4,48,1024]{2,1,0:T(8,128)(2,1)S(1)}, u32[]{:S(2)}, u32[]{:S(2)}) collective-permute-start(bf16[4,48,1024]{2,1,0:T(8,128)(2,1)} %collective-permute-done.15.refs_1_), channel_id=1, source_target_pairs={{0,16},{16,0},{1,17},{17,1},{2,18},{18,2},{3,19},{19,3},{4,20},{20... | collective-permute-start | bytes 1179656 | tf_op jit(solution)/shard_map/ppermute | solution.py:23
  69.4 10.3 %collective-permute-start.20 = (bf16[4,48,1024]{2,1,0:T(8,128)(2,1)}, bf16[4,48,1024]{2,1,0:T(8,128)(2,1)}, u32[]{:S(2)}, u32[]{:S(2)}) collective-permute-start(bf16[4,48,1024]{2,1,0:T(8,128)(2,1)} %collective-permute-done.16.refs_2_), channel_id=1, source_target_pairs={{0,16},{16,0},{1,17},{17,1},{2,18},{18,2},{3,19},{19,3},{4,20},{20... | collective-permute-start | bytes 1179656 | tf_op jit(solution)/shard_map/ppermute | solution.py:23
  84.0 29.0 %all-to-all-start = ((bf16[320,16,128]{2,1,0:T(8,128)(2,1)}), bf16[320,16,128]{2,1,0:T(8,128)(2,1)}, u32[]{:S(2)}, u32[]{:S(2)}) async-start(bf16[320,16,128]{2,1,0:T(8,128)(2,1)} %copy-done.3), calls=%async_computation | async-start | bytes 2621440 | tf_op jit(solution)/shard_map/all_to_all | solution.py:337
  116.2 30.7 %collective-permute-start.22 = (bf16[2,20,64,128]{3,2,1,0:T(8,128)(2,1)}, bf16[2,20,64,128]{3,2,1,0:T(8,128)(2,1)}, u32[]{:S(2)}, u32[]{:S(2)}) collective-permute-start(bf16[2,20,64,128]{3,2,1,0:T(8,128)(2,1)} %get-tuple-element.76), channel_id=1, source_target_pairs={{0,32},{32,64},{64,96},{96,0},{1,33},{33,65},{65,97},{97,1},{2,34}... | collective-permute-start | bytes 1966088 | tf_op jit(solution)/shard_map/ppermute | solution.py:19
  116.2 32.7 %collective-permute-start.23 = (bf16[2,20,64,128]{3,2,1,0:T(8,128)(2,1)}, bf16[2,20,64,128]{3,2,1,0:T(8,128)(2,1)}, u32[]{:S(2)}, u32[]{:S(2)}) collective-permute-start(bf16[2,20,64,128]{3,2,1,0:T(8,128)(2,1)} %get-tuple-element.77), channel_id=1, source_target_pairs={{0,64},{32,96},{64,0},{96,32},{1,65},{33,97},{65,1},{97,33},{2,66}... | collective-permute-start | bytes 1966088 | tf_op jit(solution)/shard_map/ppermute | solution.py:19
  116.2 32.7 %collective-permute-start.24 = (bf16[2,20,64,128]{3,2,1,0:T(8,128)(2,1)}, bf16[2,20,64,128]{3,2,1,0:T(8,128)(2,1)}, u32[]{:S(2)}, u32[]{:S(2)}) collective-permute-start(bf16[2,20,64,128]{3,2,1,0:T(8,128)(2,1)} %get-tuple-element.78), channel_id=1, source_target_pairs={{0,96},{32,0},{64,32},{96,64},{1,97},{33,1},{65,33},{97,65},{2,98}... | collective-permute-start | bytes 1966088 | tf_op jit(solution)/shard_map/ppermute | solution.py:19
  118.8 31.1 %all-to-all-start.1 = ((bf16[320,16,128]{2,1,0:T(8,128)(2,1)}), bf16[320,16,128]{2,1,0:T(8,128)(2,1)S(1)}, u32[]{:S(2)}, u32[]{:S(2)}) async-start(bf16[320,16,128]{2,1,0:T(8,128)(2,1)} %shard_map.84), calls=%async_computation.1 | async-start | bytes 2621440 | tf_op jit(solution)/shard_map/all_to_all | solution.py:337
  122.6 29.0 %collective-permute-start.25 = (bf16[2,20,64,128]{3,2,1,0:T(8,128)(2,1)S(1)}, bf16[2,20,64,128]{3,2,1,0:T(8,128)(2,1)S(1)}, u32[]{:S(2)}, u32[]{:S(2)}) collective-permute-start(bf16[2,20,64,128]{3,2,1,0:T(8,128)(2,1)S(1)} %get-tuple-element.75.refs_0_), channel_id=1, source_target_pairs={{0,16},{16,0},{1,17},{17,1},{2,18},{18,2},{3,19},{19,3},{4,20},{20... | collective-permute-start | bytes 1966088 | tf_op jit(solution)/shard_map/ppermute | solution.py:23
  146.8 8.3 %collective-permute-start.26 = (bf16[2,20,64,128]{3,2,1,0:T(8,128)(2,1)}, bf16[2,20,64,128]{3,2,1,0:T(8,128)(2,1)}, u32[]{:S(2)}, u32[]{:S(2)}) collective-permute-start(bf16[2,20,64,128]{3,2,1,0:T(8,128)(2,1)} %collective-permute-done.22.refs_1_), channel_id=1, source_target_pairs={{0,16},{16,0},{1,17},{17,1},{2,18},{18,2},{3,19},{19,3},{4,20},{20... | collective-permute-start | bytes 1966088 | tf_op jit(solution)/shard_map/ppermute | solution.py:23
  148.9 6.2 %collective-permute-start.27 = (bf16[2,20,64,128]{3,2,1,0:T(8,128)(2,1)}, bf16[2,20,64,128]{3,2,1,0:T(8,128)(2,1)}, u32[]{:S(2)}, u32[]{:S(2)}) collective-permute-start(bf16[2,20,64,128]{3,2,1,0:T(8,128)(2,1)} %collective-permute-done.23.refs_2_), channel_id=1, source_target_pairs={{0,16},{16,0},{1,17},{17,1},{2,18},{18,2},{3,19},{19,3},{4,20},{20... | collective-permute-start | bytes 1966088 | tf_op jit(solution)/shard_map/ppermute | solution.py:23
  151.3 17.9 %collective-permute-start.29 = (bf16[2,20,64,128]{3,2,1,0:T(8,128)(2,1)S(1)}, bf16[2,20,64,128]{3,2,1,0:T(8,128)(2,1)S(1)}, u32[]{:S(2)}, u32[]{:S(2)}) collective-permute-start(bf16[2,20,64,128]{3,2,1,0:T(8,128)(2,1)S(1)} %get-tuple-element.81), channel_id=1, source_target_pairs={{0,32},{32,64},{64,96},{96,0},{1,33},{33,65},{65,97},{97,1},{2,34}... | collective-permute-start | bytes 1966088 | tf_op jit(solution)/shard_map/ppermute | solution.py:19
  152.4 30.4 %collective-permute-start.31 = (bf16[2,20,64,128]{3,2,1,0:T(8,128)(2,1)S(1)}, bf16[2,20,64,128]{3,2,1,0:T(8,128)(2,1)S(1)}, u32[]{:S(2)}, u32[]{:S(2)}) collective-permute-start(bf16[2,20,64,128]{3,2,1,0:T(8,128)(2,1)S(1)} %get-tuple-element.83), channel_id=1, source_target_pairs={{0,96},{32,0},{64,32},{96,64},{1,97},{33,1},{65,33},{97,65},{2,98}... | collective-permute-start | bytes 1966088 | tf_op jit(solution)/shard_map/ppermute | solution.py:19
  159.6 24.5 %collective-permute-start.30 = (bf16[2,20,64,128]{3,2,1,0:T(8,128)(2,1)S(1)}, bf16[2,20,64,128]{3,2,1,0:T(8,128)(2,1)S(1)}, u32[]{:S(2)}, u32[]{:S(2)}) collective-permute-start(bf16[2,20,64,128]{3,2,1,0:T(8,128)(2,1)S(1)} %get-tuple-element.82), channel_id=1, source_target_pairs={{0,64},{32,96},{64,0},{96,32},{1,65},{33,97},{65,1},{97,33},{2,66}... | collective-permute-start | bytes 1966088 | tf_op jit(solution)/shard_map/ppermute | solution.py:19
  160.2 24.4 %collective-permute-start.32 = (bf16[2,20,64,128]{3,2,1,0:T(8,128)(2,1)S(1)}, bf16[2,20,64,128]{3,2,1,0:T(8,128)(2,1)S(1)}, u32[]{:S(2)}, u32[]{:S(2)}) collective-permute-start(bf16[2,20,64,128]{3,2,1,0:T(8,128)(2,1)S(1)} %get-tuple-element.80.refs_0_), channel_id=1, source_target_pairs={{0,16},{16,0},{1,17},{17,1},{2,18},{18,2},{3,19},{19,3},{4,20},{20... | collective-permute-start | bytes 1966088 | tf_op jit(solution)/shard_map/ppermute | solution.py:23
  169.2 15.4 %collective-permute-start.33 = (bf16[2,20,64,128]{3,2,1,0:T(8,128)(2,1)S(1)}, bf16[2,20,64,128]{3,2,1,0:T(8,128)(2,1)S(1)}, u32[]{:S(2)}, u32[]{:S(2)}) collective-permute-start(bf16[2,20,64,128]{3,2,1,0:T(8,128)(2,1)S(1)} %collective-permute-done.29.refs_1_), channel_id=1, source_target_pairs={{0,16},{16,0},{1,17},{17,1},{2,18},{18,2},{3,19},{19,3},{4,20},{20... | collective-permute-start | bytes 1966088 | tf_op jit(solution)/shard_map/ppermute | solution.py:23
  (29 other events, 167.5 us)

commit v3 on v2

--- a/solution.py
+++ b/solution.py
@@ -54,22 +54,21 @@
 
 def merge_kernel(place, v, u, v_got, u_got, *outs):
     rows = outs[0].shape[0]
-    child = place[CORE]
     for k, out in enumerate(outs):
         part = lax.rem(place[FIRST] + k, RING)
         at = pl.ds(pl.multiple_of(lax.rem(part, 2) * rows, rows), rows)
 
         @pl.when(part < 2)
         def _():
-            out[...] = (v[child, at].astype(F32) + v_got[at].astype(F32)).astype(BF16)
+            out[...] = (v[at].astype(F32) + v_got[at].astype(F32)).astype(BF16)
 
         @pl.when(part >= 2)
         def _():
-            out[...] = (u[child, at].astype(F32) + u_got[at].astype(F32)).astype(BF16)
+            out[...] = (u[at].astype(F32) + u_got[at].astype(F32)).astype(BF16)
 
 
 def merge(place, v, u, v_got, u_got):
-    _, samples, rank = v.shape
+    samples, rank = v.shape
     return pl.pallas_call(
         merge_kernel,
         out_shape=[jax.ShapeDtypeStruct((samples // 2, rank), BF16)] * RING,
@@ -247,8 +246,8 @@
         out[s + 1] = got[:, BLK:]
 
 
-def place_blocks(placer, near):
-    far = [swap_core(p) for p in near]
+def place_blocks(placer, near, far_first):
+    far = [far_first] + [swap_core(p) for p in near[1:]]
     _, share, capacity, _ = near[0].shape
     spec = lambda half: pl.BlockSpec((1, GROUP, capacity, BLK), lambda g: (half, g, 0, 0))
     return pl.pallas_call(
@@ -288,25 +287,28 @@
     probes = omega.transpose(1, 0, 2)
     own, got = [], []
     for basis in (v_basis, u_basis):
-        own.append(jnp.einsum("scn,cnr->csr", omega, basis, preferred_element_type=F32).astype(BF16))
-        got.append(swap_core(lax.dynamic_index_in_dim(own[-1], 1 - core, 0, keepdims=False)))
+        both_parts = jnp.einsum("scn,cnr->csr", omega, basis, preferred_element_type=F32).astype(BF16)
+        own.append(lax.dynamic_index_in_dim(both_parts, core, 0, keepdims=False))
+        got.append(swap_core(lax.dynamic_index_in_dim(both_parts, 1 - core, 0, keepdims=False)))
     pieces = merge(spot, *own, *got)
     coupling, u_late, pieces = lax.optimization_barrier((coupling, u_basis, pieces))
     weight = lax.dynamic_index_in_dim(coupling, core, 0, keepdims=False)
-    u_parts = [lax.dynamic_index_in_dim(u_late, c, 0, keepdims=False) for c in (core, 1 - core)]
+    u_own = lax.dynamic_index_in_dim(u_late, core, 0, keepdims=False)
     pieces = [pieces[0]] + [ring_zx(pieces[k], True, k) for k in STEPS]
     pieces = sum_split(spot, pieces)
     pieces = [pieces[0]] + [ring_zx(pieces[k], False, k) for k in STEPS]
     piece = sum_info(pieces, info)
+    u_own, probes, piece, u_late = lax.optimization_barrier((u_own, probes, piece, u_late))
+    u_other = lax.dynamic_index_in_dim(u_late, 1 - core, 0, keepdims=False)
     inner = couple(spot, [piece] + [ring_y(piece, k) for k in (1, 2, 3)], weight)
     inner = jnp.stack([inner] + [ring_zx(inner, False, k) for k in (1, 2, 3)])
-    u_parts, probes, inner = lax.optimization_barrier((u_parts, probes, inner))
+    u_other, inner = lax.optimization_barrier((u_other, inner))
     held = [inner] + [ring_zx(inner, True, k) for k in (1, 2, 3)]
     swapped = [swap_core(p) for p in held]
 
-    first, seen = expand(0, spot, held, u_parts[0], probes, leaf_blocks)
-    y_samp = expand(0, spot, swapped, u_parts[1], probes, leaf_blocks, first)
-    seen, y_samp, v_late = lax.optimization_barrier((seen, y_samp, v_basis))
+    first, seen = expand(0, spot, held, u_own, probes, leaf_blocks)
+    y_samp = expand(0, spot, swapped, u_other, probes, leaf_blocks, first)
+    seen, y_samp, v_late, count = lax.optimization_barrier((seen, y_samp, v_basis, jnp.arange(owner_rows)))
     v_parts = [lax.dynamic_index_in_dim(v_late, c, 0, keepdims=False) for c in (core, 1 - core)]
     first = expand(1, spot, held, v_parts[0], probes, leaf_blocks)
     z_samp = expand(1, spot, swapped, v_parts[1], probes, leaf_blocks, first)
@@ -322,7 +324,7 @@
     seen = seen.transpose(3, 2, 1, 0, 4).reshape(2, row_count, owner_rows)
     dest, home = seen[0], seen[1]
     same = (dest[:, :, None] == dest[:, None, :]).astype(jnp.int32)
-    before = (jnp.arange(owner_rows)[None, :] < jnp.arange(owner_rows)[:, None]).astype(jnp.int32)
+    before = (count[None, :] < count[:, None]).astype(jnp.int32)
     order = jnp.sum(same * before[None], axis=2)
 
     step = (dest[0] // 2 - y_me) % RING
@@ -342,10 +344,12 @@
     y_out = send(selector, y_cols, capacity)
     y_out = [y_out[0]] + [ring_y(y_out[k], k) for k in (1, 2, 3)]
     z_out = list(send(selector, columns(z_samp), capacity))
-    parent_y = place_blocks(placer, y_out)
+    z_far = swap_core(z_out[0])
+    y_out[1:], z_far = lax.optimization_barrier((y_out[1:], z_far))
+    parent_y = place_blocks(placer, y_out, swap_core(y_out[0]))
     z_out[2], parent_y = lax.optimization_barrier((z_out[2], parent_y))
     z_out = [z_out[0]] + [ring_y(z_out[k], k) for k in (1, 2, 3)]
-    return parent_y, place_blocks(placer, z_out)
+    return parent_y, place_blocks(placer, z_out, z_far)
 
 
 def solution(mesh):

time: 190 us -> 189 us (level)
  waiting for transfers between devices: 64 us -> 73.5 us
  local copies, waits for them, and re-layouts: 25.8 us -> 17.1 us
  Pallas kernels: 25.8 us -> 21 us
  starting transfers between devices: 62.7 us -> 67.4 us
    all_to_all x2, waiting for transfers between devices: 2.86 us -> 18.2 us  [columns(): lax.all_to_all(samp, ('z', 'x'), split_axis=0, concat_axis=0, tiled=True)]
    ppermute x9, waiting for transfers between devices: 46.7 us -> 38.8 us  [ring_y(): return lax.ppermute(x, 'y', [(i, (i + step) % RING) for i in range(RING)])]
    unnamed x31 -> x51, local copies, waits for them, and re-layouts: 9.21 us -> 5.12 us
    pallas_call x4, Pallas kernels: 12 us -> 8.14 us  [expand(): pl.pallas_call(functools.partial(expand_kernel, kind, own), in_specs=[SME...]
    ppermute x15, starting transfers between devices: 25.1 us -> 28 us  [swap_core(): return lax.ppermute(x, 'core', [(0, 1), (1, 0)])]
    squeeze x3 -> x4, local copies, waits for them, and re-layouts: 4.25 us -> 1.39 us  [the longest x2 1.04 us: per_device(): lax.dynamic_index_in_dim(both_parts, 1 - core, 0, keepdims=False)]
    ppermute x12, waiting for transfers between devices: 10 us -> 12.5 us  [ring_zx(): return lax.ppermute(x, ('core', 'z', 'x'), pairs)]
  transfers between devices with their start and end apart: 38 -> 38, of which waited for: 16 -> 21; matrix products, arithmetic and copies ran while one was open for 12% -> 9% of each run, Pallas kernels for 8% -> 7%
where the time goes in v3:
time: 189 us; the launch traced here: 188 us
  waiting for transfers between devices  73.5 us (39%)
  starting transfers between devices  67.4 us (36%)
  Pallas kernels  21 us (11%)
  local copies, waits for them, and re-layouts  17.1 us (9%)
  matrix products  5.84 us (3%)
  other arithmetic  2.23 us (1%)
    ppermute x9, waiting for transfers between devices, ring_y(): return lax.ppermute(x, 'y', [(i, (i + step) % RING) for i in range(RING)])  38.8 us
    ppermute x15, starting transfers between devices, swap_core(): return lax.ppermute(x, 'core', [(0, 1), (1, 0)])  28 us
    all_to_all x2, waiting for transfers between devices, columns(): lax.all_to_all(samp, ('z', 'x'), split_axis=0, concat_axis=0, tiled=True)  18.2 us
    ppermute x12, starting transfers between devices, ring_zx(): return lax.ppermute(x, ('core', 'z', 'x'), pairs)  16.1 us
    all_to_all x2, starting transfers between devices, columns(): lax.all_to_all(samp, ('z', 'x'), split_axis=0, concat_axis=0, tiled=True)  12.7 us
    ppermute x12, waiting for transfers between devices, ring_zx(): return lax.ppermute(x, ('core', 'z', 'x'), pairs)  12.5 us
    ppermute x9, starting transfers between devices, ring_y(): return lax.ppermute(x, 'y', [(i, (i + step) % RING) for i in range(RING)])  10.5 us
    pallas_call x4, Pallas kernels, expand(): pl.pallas_call(functools.partial(expand_kernel, kind, own), in_specs=[SME...  8.14 us
  transfers between devices with their start and end apart: 38, of which 21 were waited for; matrix products, arithmetic and copies ran while one was open for 9% of the time, Pallas kernels for 7%

profile of v3, /device:TPU:1, one launch (start us, length us, event | category | flops | bytes accessed | tf_op | source)
XLA Modules:
  0.0 188.2 jit_solution(14538733602636538126)
XLA Ops:
  0.6 4.3 %convolution_convert_fusion.1 = bf16[2,320,1024]{2,1,0:T(8,128)(2,1)S(1)} fusion(bf16[2,1024,1024]{2,1,0:T(8,128)(2,1)} %param.10, bf16[320,2,1024]{2,1,0:T(2,128)(2,1)} %param.8), kind=kOutput, calls=%fused_computation.8 | convolution fusion | flops 1342832640 | bytes 6815744 | tf_op jit(solution)/shard_map/scn,cnr->csr/dot_general | solution.py:290
  21.4 3.1 %collective-permute-done.3 = bf16[160,1024]{1,0:T(8,128)(2,1)S(1)} collective-permute-done((bf16[160,1024]{1,0:T(8,128)(2,1)S(1)}, bf16[160,1024]{1,0:T(8,128)(2,1)S(1)}, u32[]{:S(2)}, u32[]{:S(2)}) %collective-permute-start.3) | collective-permute-done | bytes 327712 | tf_op jit(solution)/shard_map/ppermute | solution.py:35
  31.4 3.0 %collective-permute-done.7.d = bf16[40,1024]{1,0:T(8,128)(2,1)S(1)} collective-permute-done((bf16[40,1024]{1,0:T(8,128)(2,1)S(1)}, bf16[40,1024]{1,0:T(8,128)(2,1)S(1)}, u32[]{:S(2)}, u32[]{:S(2)}) %collective-permute-start.7) | collective-permute-done | bytes 81952 | tf_op jit(solution)/shard_map/ppermute | solution.py:35
  34.4 3.0 %collective-permute-start.10 = (bf16[48,1024]{1,0:T(8,128)(2,1)S(1)}, bf16[48,1024]{1,0:T(8,128)(2,1)S(1)}, u32[]{:S(2)}, u32[]{:S(2)}) collective-permute-start(bf16[48,1024]{1,0:T(8,128)(2,1)S(1)} %shard_map.79.a), channel_id=1, source_target_pairs={{0,64},{32,96},{64,0},{96,32},{1,65},{33,97},{65,1},{97,33},{2,66}... | collective-permute-start | bytes 294920 | tf_op jit(solution)/shard_map/ppermute | solution.py:19
  40.9 2.9 %collective-permute-done.9.b = bf16[48,1024]{1,0:T(8,128)(2,1)S(1)} collective-permute-done((bf16[48,1024]{1,0:T(8,128)(2,1)S(1)}, bf16[48,1024]{1,0:T(8,128)(2,1)S(1)}, u32[]{:S(2)}, u32[]{:S(2)}) %collective-permute-start.9) | collective-permute-done | bytes 98336 | tf_op jit(solution)/shard_map/ppermute | solution.py:19
  45.2 2.5 %collective-permute-start.13 = (bf16[48,1024]{1,0:T(8,128)(2,1)S(1)}, bf16[48,1024]{1,0:T(8,128)(2,1)S(1)}, u32[]{:S(2)}, u32[]{:S(2)}) collective-permute-start(bf16[48,1024]{1,0:T(8,128)(2,1)S(1)} %shard_map.80), channel_id=1, source_target_pairs={{0,8},{1,9},{2,10},{3,11},{4,12},{5,13},{6,14},{7,15},{8,0},{9,1},... | collective-permute-start | bytes 294920 | tf_op jit(solution)/shard_map/ppermute | solution.py:35
  48.6 2.4 %collective-permute-done.12 = bf16[48,1024]{1,0:T(8,128)(2,1)S(1)} collective-permute-done((bf16[48,1024]{1,0:T(8,128)(2,1)S(1)}, bf16[48,1024]{1,0:T(8,128)(2,1)S(1)}, u32[]{:S(2)}, u32[]{:S(2)}) %collective-permute-start.12) | collective-permute-done | bytes 98336 | tf_op jit(solution)/shard_map/ppermute | solution.py:35
  54.9 7.2 %collective-permute-start.18 = (bf16[4,48,1024]{2,1,0:T(8,128)(2,1)S(1)}, bf16[4,48,1024]{2,1,0:T(8,128)(2,1)S(1)}, u32[]{:S(2)}, u32[]{:S(2)}) collective-permute-start(bf16[4,48,1024]{2,1,0:T(8,128)(2,1)S(1)} %pad_maximum_fusion.refs_0_), channel_id=1, source_target_pairs={{0,16},{16,0},{1,17},{17,1},{2,18},{18,2},{3,19},{19,3},{4,20},{20... | collective-permute-start | bytes 1179656 | tf_op jit(solution)/shard_map/ppermute | solution.py:23
  62.1 4.2 %collective-permute-start.19 = (bf16[4,48,1024]{2,1,0:T(8,128)(2,1)S(1)}, bf16[4,48,1024]{2,1,0:T(8,128)(2,1)S(1)}, u32[]{:S(2)}, u32[]{:S(2)}) collective-permute-start(bf16[4,48,1024]{2,1,0:T(8,128)(2,1)S(1)} %collective-permute-done.15.refs_1_), channel_id=1, source_target_pairs={{0,16},{16,0},{1,17},{17,1},{2,18},{18,2},{3,19},{19,3},{4,20},{20... | collective-permute-start | bytes 1179656 | tf_op jit(solution)/shard_map/ppermute | solution.py:23
  66.3 4.2 %collective-permute-start.20 = (bf16[4,48,1024]{2,1,0:T(8,128)(2,1)S(1)}, bf16[4,48,1024]{2,1,0:T(8,128)(2,1)S(1)}, u32[]{:S(2)}, u32[]{:S(2)}) collective-permute-start(bf16[4,48,1024]{2,1,0:T(8,128)(2,1)S(1)} %collective-permute-done.16.refs_2_), channel_id=1, source_target_pairs={{0,16},{16,0},{1,17},{17,1},{2,18},{18,2},{3,19},{19,3},{4,20},{20... | collective-permute-start | bytes 1179656 | tf_op jit(solution)/shard_map/ppermute | solution.py:23
  76.6 9.0 %all-to-all-start = ((bf16[320,16,128]{2,1,0:T(8,128)(2,1)}), bf16[320,16,128]{2,1,0:T(8,128)(2,1)}, u32[]{:S(2)}, u32[]{:S(2)}) async-start(bf16[320,16,128]{2,1,0:T(8,128)(2,1)} %copy-done.1), calls=%async_computation | async-start | bytes 2621440 | tf_op jit(solution)/shard_map/all_to_all | solution.py:339
  92.2 2.8 %dynamic-slice_bitcast_fusion = (bf16[1024,1024]{1,0:T(8,128)(2,1)S(1)}, bf16[1024,1024]{1,0:T(8,128)(2,1)S(1)}) fusion(bf16[2,1024,1024]{2,1,0:T(8,128)(2,1)} %param.10, s32[]{:T(128)S(6)} %select_n.132, s32[]{:T(128)S(6)} %select_n.133), kind=kLoop, calls=%fused_computation.1 | loop fusion | bytes 8388616 | tf_op jit(solution)/shard_map/jit(dynamic_index_in_dim)/squeeze | solution.py:312
  100.2 7.2 %all-to-all-done = bf16[320,16,128]{2,1,0:T(8,128)(2,1)} async-done(((bf16[320,16,128]{2,1,0:T(8,128)(2,1)}), bf16[320,16,128]{2,1,0:T(8,128)(2,1)}, u32[]{:S(2)}, u32[]{:S(2)}) %all-to-all-start) | async-done | bytes 1310752 | tf_op jit(solution)/shard_map/all_to_all | solution.py:339
  107.4 3.7 %all-to-all-start.1 = ((bf16[320,16,128]{2,1,0:T(8,128)(2,1)}), bf16[320,16,128]{2,1,0:T(8,128)(2,1)S(1)}, u32[]{:S(2)}, u32[]{:S(2)}) async-start(bf16[320,16,128]{2,1,0:T(8,128)(2,1)} %copy-done.2), calls=%async_computation.1 | async-start | bytes 2621440 | tf_op jit(solution)/shard_map/all_to_all | solution.py:339
  112.9 3.1 %shard_map.86 = (bf16[2,20,64,128]{3,2,1,0:T(8,128)(2,1)S(1)}, bf16[2,20,64,128]{3,2,1,0:T(8,128)(2,1)}, bf16[2,20,64,128]{3,2,1,0:T(8,128)(2,1)}, bf16[2,20,64,128]{3,2,1,0:T(8,128)(2,1)}) custom-call(bf16[512,256]{1,0:T(8,128)(2,1)S(1)} %fusion.2.selector, bf16[16,20,16,128]{3,2,1,0:T(8,128)(2,1)} %bitcast.27.columns), custom_call_target="tpu_custom_call" | custom-call | flops 671088640 | bytes 8388608 | tf_op jit(solution)/shard_map/pallas_call | solution.py:224
  116.0 2.7 %collective-permute-start.24 = (bf16[2,20,64,128]{3,2,1,0:T(8,128)(2,1)}, bf16[2,20,64,128]{3,2,1,0:T(8,128)(2,1)}, u32[]{:S(2)}, u32[]{:S(2)}) collective-permute-start(bf16[2,20,64,128]{3,2,1,0:T(8,128)(2,1)} %get-tuple-element.88), channel_id=1, source_target_pairs={{0,96},{32,0},{64,32},{96,64},{1,97},{33,1},{65,33},{97,65},{2,98}... | collective-permute-start | bytes 1966088 | tf_op jit(solution)/shard_map/ppermute | solution.py:19
  118.7 11.0 %all-to-all-done.1 = bf16[320,16,128]{2,1,0:T(8,128)(2,1)S(1)} async-done(((bf16[320,16,128]{2,1,0:T(8,128)(2,1)}), bf16[320,16,128]{2,1,0:T(8,128)(2,1)S(1)}, u32[]{:S(2)}, u32[]{:S(2)}) %all-to-all-start.1) | async-done | bytes 1310752 | tf_op jit(solution)/shard_map/all_to_all | solution.py:339
  133.6 3.1 %collective-permute-start.25 = (bf16[2,20,64,128]{3,2,1,0:T(8,128)(2,1)S(1)}, bf16[2,20,64,128]{3,2,1,0:T(8,128)(2,1)S(1)}, u32[]{:S(2)}, u32[]{:S(2)}) collective-permute-start(bf16[2,20,64,128]{3,2,1,0:T(8,128)(2,1)S(1)} %get-tuple-element.89.refs_0_), channel_id=1, source_target_pairs={{0,16},{16,0},{1,17},{17,1},{2,18},{18,2},{3,19},{19,3},{4,20},{20... | collective-permute-start | bytes 1966088 | tf_op jit(solution)/shard_map/ppermute | solution.py:23
  136.7 9.9 %collective-permute-done.22.refs_1_ = bf16[2,20,64,128]{3,2,1,0:T(8,128)(2,1)S(1)} collective-permute-done((bf16[2,20,64,128]{3,2,1,0:T(8,128)(2,1)}, bf16[2,20,64,128]{3,2,1,0:T(8,128)(2,1)S(1)}, u32[]{:S(2)}, u32[]{:S(2)}) %collective-permute-start.22) | collective-permute-done | bytes 655392 | tf_op jit(solution)/shard_map/ppermute | solution.py:19
  147.1 2.2 %collective-permute-start.27 = (bf16[2,20,64,128]{3,2,1,0:T(8,128)(2,1)S(1)}, bf16[2,20,64,128]{3,2,1,0:T(8,128)(2,1)}, u32[]{:S(2)}, u32[]{:S(2)}) collective-permute-start(bf16[2,20,64,128]{3,2,1,0:T(8,128)(2,1)S(1)} %collective-permute-done.22.refs_1_), channel_id=1, source_target_pairs={{0,16},{16,0},{1,17},{17,1},{2,18},{18,2},{3,19},{19,3},{4,20},{20... | collective-permute-start | bytes 1966088 | tf_op jit(solution)/shard_map/ppermute | solution.py:23
  151.3 2.6 %collective-permute-start.32 = (bf16[2,20,64,128]{3,2,1,0:T(8,128)(2,1)}, bf16[2,20,64,128]{3,2,1,0:T(8,128)(2,1)S(1)}, u32[]{:S(2)}, u32[]{:S(2)}) collective-permute-start(bf16[2,20,64,128]{3,2,1,0:T(8,128)(2,1)} %copy-done.16), channel_id=1, source_target_pairs={{0,96},{32,0},{64,32},{96,64},{1,97},{33,1},{65,33},{97,65},{2,98}... | collective-permute-start | bytes 1966088 | tf_op jit(solution)/shard_map/ppermute | solution.py:19
  153.9 3.4 %shard_map.87 = f32[20,256,128]{2,1,0:T(8,128)} custom-call(bf16[256,512]{1,0:T(8,128)(2,1)S(1)} %fusion.3.placer, bf16[2,20,64,128]{3,2,1,0:T(8,128)(2,1)S(1)} %get-tuple-element.85.refs_0_, bf16[2,20,64,128]{3,2,1,0:T(8,128)(2,1)S(1)} %collective-permute-done.22.refs_1_, bf16[2,20,64,128]{3,2,1,0:T(8,128)(2,1)} %collective-permute-done.23.refs_2_, ...), custom_call_target="tpu_custom_call" | custom-call | flops 671088640 | bytes 10485760 | tf_op jit(solution)/shard_map/pallas_call | solution.py:253
  157.9 11.1 %collective-permute-done.30.refs_1_ = bf16[2,20,64,128]{3,2,1,0:T(8,128)(2,1)S(1)} collective-permute-done((bf16[2,20,64,128]{3,2,1,0:T(8,128)(2,1)}, bf16[2,20,64,128]{3,2,1,0:T(8,128)(2,1)S(1)}, u32[]{:S(2)}, u32[]{:S(2)}) %collective-permute-start.30) | collective-permute-done | bytes 655392 | tf_op jit(solution)/shard_map/ppermute | solution.py:19
  169.8 12.2 %collective-permute-done.32.refs_3_ = bf16[2,20,64,128]{3,2,1,0:T(8,128)(2,1)S(1)} collective-permute-done((bf16[2,20,64,128]{3,2,1,0:T(8,128)(2,1)}, bf16[2,20,64,128]{3,2,1,0:T(8,128)(2,1)S(1)}, u32[]{:S(2)}, u32[]{:S(2)}) %collective-permute-start.32) | collective-permute-done | bytes 655392 | tf_op jit(solution)/shard_map/ppermute | solution.py:19
  (156 shorter events, 66.3 us)
Async XLA Ops:
  13.0 8.4 %collective-permute-start.2 = (bf16[160,1024]{1,0:T(8,128)(2,1)S(1)}, bf16[160,1024]{1,0:T(8,128)(2,1)S(1)}, u32[]{:S(2)}, u32[]{:S(2)}) collective-permute-start(bf16[160,1024]{1,0:T(8,128)(2,1)S(1)} %get-tuple-element.62), channel_id=1, source_target_pairs={{0,1},{1,2},{2,3},{3,0},{4,5},{5,6},{6,7},{7,4},{8,9},{9,10},{10,1... | collective-permute-start | bytes 983048 | tf_op jit(solution)/shard_map/ppermute | solution.py:35
  14.8 9.7 %collective-permute-start.3 = (bf16[160,1024]{1,0:T(8,128)(2,1)S(1)}, bf16[160,1024]{1,0:T(8,128)(2,1)S(1)}, u32[]{:S(2)}, u32[]{:S(2)}) collective-permute-start(bf16[160,1024]{1,0:T(8,128)(2,1)S(1)} %get-tuple-element.63), channel_id=1, source_target_pairs={{0,3},{1,0},{2,1},{3,2},{4,7},{5,4},{6,5},{7,6},{8,11},{9,8},{10,9... | collective-permute-start | bytes 983048 | tf_op jit(solution)/shard_map/ppermute | solution.py:35
  17.0 9.1 %collective-permute-start.4 = (bf16[160,1024]{1,0:T(8,128)(2,1)S(1)}, bf16[160,1024]{1,0:T(8,128)(2,1)S(1)}, u32[]{:S(2)}, u32[]{:S(2)}) collective-permute-start(bf16[160,1024]{1,0:T(8,128)(2,1)S(1)} %get-tuple-element.64), channel_id=1, source_target_pairs={{0,2},{1,3},{2,0},{3,1},{4,6},{5,7},{6,4},{7,5},{8,10},{9,11},{10,... | collective-permute-start | bytes 983048 | tf_op jit(solution)/shard_map/ppermute | solution.py:35
  38.2 5.6 %collective-permute-start.9 = (bf16[48,1024]{1,0:T(8,128)(2,1)S(1)}, bf16[48,1024]{1,0:T(8,128)(2,1)S(1)}, u32[]{:S(2)}, u32[]{:S(2)}) collective-permute-start(bf16[48,1024]{1,0:T(8,128)(2,1)S(1)} %shard_map.79.a), channel_id=1, source_target_pairs={{0,32},{32,64},{64,96},{96,0},{1,33},{33,65},{65,97},{97,1},{2,34}... | collective-permute-start | bytes 294920 | tf_op jit(solution)/shard_map/ppermute | solution.py:19
  45.1 5.8 %collective-permute-start.12 = (bf16[48,1024]{1,0:T(8,128)(2,1)S(1)}, bf16[48,1024]{1,0:T(8,128)(2,1)S(1)}, u32[]{:S(2)}, u32[]{:S(2)}) collective-permute-start(bf16[48,1024]{1,0:T(8,128)(2,1)S(1)} %shard_map.80), channel_id=1, source_target_pairs={{0,4},{1,5},{2,6},{3,7},{4,8},{5,9},{6,10},{7,11},{8,12},{9,13},{1... | collective-permute-start | bytes 294920 | tf_op jit(solution)/shard_map/ppermute | solution.py:35
  45.2 5.7 %collective-permute-start.13 = (bf16[48,1024]{1,0:T(8,128)(2,1)S(1)}, bf16[48,1024]{1,0:T(8,128)(2,1)S(1)}, u32[]{:S(2)}, u32[]{:S(2)}) collective-permute-start(bf16[48,1024]{1,0:T(8,128)(2,1)S(1)} %shard_map.80), channel_id=1, source_target_pairs={{0,8},{1,9},{2,10},{3,11},{4,12},{5,13},{6,14},{7,15},{8,0},{9,1},... | collective-permute-start | bytes 294920 | tf_op jit(solution)/shard_map/ppermute | solution.py:35
  51.6 10.5 %collective-permute-start.15 = (bf16[4,48,1024]{2,1,0:T(8,128)(2,1)S(1)}, bf16[4,48,1024]{2,1,0:T(8,128)(2,1)S(1)}, u32[]{:S(2)}, u32[]{:S(2)}) collective-permute-start(bf16[4,48,1024]{2,1,0:T(8,128)(2,1)S(1)} %pad_maximum_fusion.refs_0_), channel_id=1, source_target_pairs={{0,1},{1,2},{2,3},{3,0},{4,5},{5,6},{6,7},{7,4},{8,9},{9,10},{10,1... | collective-permute-start | bytes 1179656 | tf_op jit(solution)/shard_map/ppermute | solution.py:35
  52.4 13.8 %collective-permute-start.16 = (bf16[4,48,1024]{2,1,0:T(8,128)(2,1)S(1)}, bf16[4,48,1024]{2,1,0:T(8,128)(2,1)S(1)}, u32[]{:S(2)}, u32[]{:S(2)}) collective-permute-start(bf16[4,48,1024]{2,1,0:T(8,128)(2,1)S(1)} %pad_maximum_fusion.refs_0_), channel_id=1, source_target_pairs={{0,2},{1,3},{2,0},{3,1},{4,6},{5,7},{6,4},{7,5},{8,10},{9,11},{10,... | collective-permute-start | bytes 1179656 | tf_op jit(solution)/shard_map/ppermute | solution.py:35
  54.4 16.1 %collective-permute-start.17 = (bf16[4,48,1024]{2,1,0:T(8,128)(2,1)S(1)}, bf16[4,48,1024]{2,1,0:T(8,128)(2,1)S(1)}, u32[]{:S(2)}, u32[]{:S(2)}) collective-permute-start(bf16[4,48,1024]{2,1,0:T(8,128)(2,1)S(1)} %pad_maximum_fusion.refs_0_), channel_id=1, source_target_pairs={{0,3},{1,0},{2,1},{3,2},{4,7},{5,4},{6,5},{7,6},{8,11},{9,8},{10,9... | collective-permute-start | bytes 1179656 | tf_op jit(solution)/shard_map/ppermute | solution.py:35
  54.9 18.5 %collective-permute-start.18 = (bf16[4,48,1024]{2,1,0:T(8,128)(2,1)S(1)}, bf16[4,48,1024]{2,1,0:T(8,128)(2,1)S(1)}, u32[]{:S(2)}, u32[]{:S(2)}) collective-permute-start(bf16[4,48,1024]{2,1,0:T(8,128)(2,1)S(1)} %pad_maximum_fusion.refs_0_), channel_id=1, source_target_pairs={{0,16},{16,0},{1,17},{17,1},{2,18},{18,2},{3,19},{19,3},{4,20},{20... | collective-permute-start | bytes 1179656 | tf_op jit(solution)/shard_map/ppermute | solution.py:23
  62.1 11.4 %collective-permute-start.19 = (bf16[4,48,1024]{2,1,0:T(8,128)(2,1)S(1)}, bf16[4,48,1024]{2,1,0:T(8,128)(2,1)S(1)}, u32[]{:S(2)}, u32[]{:S(2)}) collective-permute-start(bf16[4,48,1024]{2,1,0:T(8,128)(2,1)S(1)} %collective-permute-done.15.refs_1_), channel_id=1, source_target_pairs={{0,16},{16,0},{1,17},{17,1},{2,18},{18,2},{3,19},{19,3},{4,20},{20... | collective-permute-start | bytes 1179656 | tf_op jit(solution)/shard_map/ppermute | solution.py:23
  66.3 7.2 %collective-permute-start.20 = (bf16[4,48,1024]{2,1,0:T(8,128)(2,1)S(1)}, bf16[4,48,1024]{2,1,0:T(8,128)(2,1)S(1)}, u32[]{:S(2)}, u32[]{:S(2)}) collective-permute-start(bf16[4,48,1024]{2,1,0:T(8,128)(2,1)S(1)} %collective-permute-done.16.refs_2_), channel_id=1, source_target_pairs={{0,16},{16,0},{1,17},{17,1},{2,18},{18,2},{3,19},{19,3},{4,20},{20... | collective-permute-start | bytes 1179656 | tf_op jit(solution)/shard_map/ppermute | solution.py:23
  76.6 30.8 %all-to-all-start = ((bf16[320,16,128]{2,1,0:T(8,128)(2,1)}), bf16[320,16,128]{2,1,0:T(8,128)(2,1)}, u32[]{:S(2)}, u32[]{:S(2)}) async-start(bf16[320,16,128]{2,1,0:T(8,128)(2,1)} %copy-done.1), calls=%async_computation | async-start | bytes 2621440 | tf_op jit(solution)/shard_map/all_to_all | solution.py:339
  107.4 22.3 %all-to-all-start.1 = ((bf16[320,16,128]{2,1,0:T(8,128)(2,1)}), bf16[320,16,128]{2,1,0:T(8,128)(2,1)S(1)}, u32[]{:S(2)}, u32[]{:S(2)}) async-start(bf16[320,16,128]{2,1,0:T(8,128)(2,1)} %copy-done.2), calls=%async_computation.1 | async-start | bytes 2621440 | tf_op jit(solution)/shard_map/all_to_all | solution.py:339
  116.0 30.6 %collective-permute-start.22 = (bf16[2,20,64,128]{3,2,1,0:T(8,128)(2,1)}, bf16[2,20,64,128]{3,2,1,0:T(8,128)(2,1)S(1)}, u32[]{:S(2)}, u32[]{:S(2)}) collective-permute-start(bf16[2,20,64,128]{3,2,1,0:T(8,128)(2,1)} %get-tuple-element.86), channel_id=1, source_target_pairs={{0,32},{32,64},{64,96},{96,0},{1,33},{33,65},{65,97},{97,1},{2,34}... | collective-permute-start | bytes 1966088 | tf_op jit(solution)/shard_map/ppermute | solution.py:19
  116.0 30.6 %collective-permute-start.23 = (bf16[2,20,64,128]{3,2,1,0:T(8,128)(2,1)}, bf16[2,20,64,128]{3,2,1,0:T(8,128)(2,1)}, u32[]{:S(2)}, u32[]{:S(2)}) collective-permute-start(bf16[2,20,64,128]{3,2,1,0:T(8,128)(2,1)} %get-tuple-element.87), channel_id=1, source_target_pairs={{0,64},{32,96},{64,0},{96,32},{1,65},{33,97},{65,1},{97,33},{2,66}... | collective-permute-start | bytes 1966088 | tf_op jit(solution)/shard_map/ppermute | solution.py:19
  116.0 31.1 %collective-permute-start.24 = (bf16[2,20,64,128]{3,2,1,0:T(8,128)(2,1)}, bf16[2,20,64,128]{3,2,1,0:T(8,128)(2,1)}, u32[]{:S(2)}, u32[]{:S(2)}) collective-permute-start(bf16[2,20,64,128]{3,2,1,0:T(8,128)(2,1)} %get-tuple-element.88), channel_id=1, source_target_pairs={{0,96},{32,0},{64,32},{96,64},{1,97},{33,1},{65,33},{97,65},{2,98}... | collective-permute-start | bytes 1966088 | tf_op jit(solution)/shard_map/ppermute | solution.py:19
  133.6 13.5 %collective-permute-start.25 = (bf16[2,20,64,128]{3,2,1,0:T(8,128)(2,1)S(1)}, bf16[2,20,64,128]{3,2,1,0:T(8,128)(2,1)S(1)}, u32[]{:S(2)}, u32[]{:S(2)}) collective-permute-start(bf16[2,20,64,128]{3,2,1,0:T(8,128)(2,1)S(1)} %get-tuple-element.89.refs_0_), channel_id=1, source_target_pairs={{0,16},{16,0},{1,17},{17,1},{2,18},{18,2},{3,19},{19,3},{4,20},{20... | collective-permute-start | bytes 1966088 | tf_op jit(solution)/shard_map/ppermute | solution.py:23
  136.7 14.5 %collective-permute-start.26 = (bf16[2,20,64,128]{3,2,1,0:T(8,128)(2,1)S(1)}, bf16[2,20,64,128]{3,2,1,0:T(8,128)(2,1)S(1)}, u32[]{:S(2)}, u32[]{:S(2)}) collective-permute-start(bf16[2,20,64,128]{3,2,1,0:T(8,128)(2,1)S(1)} %get-tuple-element.85.refs_0_), channel_id=1, source_target_pairs={{0,16},{16,0},{1,17},{17,1},{2,18},{18,2},{3,19},{19,3},{4,20},{20... | collective-permute-start | bytes 1966088 | tf_op jit(solution)/shard_map/ppermute | solution.py:23
  147.1 6.8 %collective-permute-start.27 = (bf16[2,20,64,128]{3,2,1,0:T(8,128)(2,1)S(1)}, bf16[2,20,64,128]{3,2,1,0:T(8,128)(2,1)}, u32[]{:S(2)}, u32[]{:S(2)}) collective-permute-start(bf16[2,20,64,128]{3,2,1,0:T(8,128)(2,1)S(1)} %collective-permute-done.22.refs_1_), channel_id=1, source_target_pairs={{0,16},{16,0},{1,17},{17,1},{2,18},{18,2},{3,19},{19,3},{4,20},{20... | collective-permute-start | bytes 1966088 | tf_op jit(solution)/shard_map/ppermute | solution.py:23
  151.2 17.9 %collective-permute-start.30 = (bf16[2,20,64,128]{3,2,1,0:T(8,128)(2,1)}, bf16[2,20,64,128]{3,2,1,0:T(8,128)(2,1)S(1)}, u32[]{:S(2)}, u32[]{:S(2)}) collective-permute-start(bf16[2,20,64,128]{3,2,1,0:T(8,128)(2,1)} %copy-done.17), channel_id=1, source_target_pairs={{0,32},{32,64},{64,96},{96,0},{1,33},{33,65},{65,97},{97,1},{2,34}... | collective-permute-start | bytes 1966088 | tf_op jit(solution)/shard_map/ppermute | solution.py:19
  151.3 30.7 %collective-permute-start.32 = (bf16[2,20,64,128]{3,2,1,0:T(8,128)(2,1)}, bf16[2,20,64,128]{3,2,1,0:T(8,128)(2,1)S(1)}, u32[]{:S(2)}, u32[]{:S(2)}) collective-permute-start(bf16[2,20,64,128]{3,2,1,0:T(8,128)(2,1)} %copy-done.16), channel_id=1, source_target_pairs={{0,96},{32,0},{64,32},{96,64},{1,97},{33,1},{65,33},{97,65},{2,98}... | collective-permute-start | bytes 1966088 | tf_op jit(solution)/shard_map/ppermute | solution.py:19
  157.3 26.3 %collective-permute-start.31 = (bf16[2,20,64,128]{3,2,1,0:T(8,128)(2,1)S(1)}, bf16[2,20,64,128]{3,2,1,0:T(8,128)(2,1)S(1)}, u32[]{:S(2)}, u32[]{:S(2)}) collective-permute-start(bf16[2,20,64,128]{3,2,1,0:T(8,128)(2,1)S(1)} %copy-done.15), channel_id=1, source_target_pairs={{0,64},{32,96},{64,0},{96,32},{1,65},{33,97},{65,1},{97,33},{2,66}... | collective-permute-start | bytes 1966088 | tf_op jit(solution)/shard_map/ppermute | solution.py:19
  169.0 15.4 %collective-permute-start.33 = (bf16[2,20,64,128]{3,2,1,0:T(8,128)(2,1)S(1)}, bf16[2,20,64,128]{3,2,1,0:T(8,128)(2,1)S(1)}, u32[]{:S(2)}, u32[]{:S(2)}) collective-permute-start(bf16[2,20,64,128]{3,2,1,0:T(8,128)(2,1)S(1)} %collective-permute-done.30.refs_1_), channel_id=1, source_target_pairs={{0,16},{16,0},{1,17},{17,1},{2,18},{18,2},{3,19},{19,3},{4,20},{20... | collective-permute-start | bytes 1966088 | tf_op jit(solution)/shard_map/ppermute | solution.py:23
  (39 other events, 187.4 us)

commit v4 on v3

--- a/solution.py
+++ b/solution.py
@@ -246,8 +246,8 @@
         out[s + 1] = got[:, BLK:]
 
 
-def place_blocks(placer, near, far_first):
-    far = [far_first] + [swap_core(p) for p in near[1:]]
+def place_blocks(placer, near):
+    far = [swap_core(p) for p in near]
     _, share, capacity, _ = near[0].shape
     spec = lambda half: pl.BlockSpec((1, GROUP, capacity, BLK), lambda g: (half, g, 0, 0))
     return pl.pallas_call(
@@ -344,12 +344,10 @@
     y_out = send(selector, y_cols, capacity)
     y_out = [y_out[0]] + [ring_y(y_out[k], k) for k in (1, 2, 3)]
     z_out = list(send(selector, columns(z_samp), capacity))
-    z_far = swap_core(z_out[0])
-    y_out[1:], z_far = lax.optimization_barrier((y_out[1:], z_far))
-    parent_y = place_blocks(placer, y_out, swap_core(y_out[0]))
+    parent_y = place_blocks(placer, y_out)
     z_out[2], parent_y = lax.optimization_barrier((z_out[2], parent_y))
     z_out = [z_out[0]] + [ring_y(z_out[k], k) for k in (1, 2, 3)]
-    return parent_y, place_blocks(placer, z_out, z_far)
+    return parent_y, place_blocks(placer, z_out)
 
 
 def solution(mesh):

time: 189 us -> 189 us (level)
  waiting for transfers between devices: 73.5 us -> 66.7 us
  local copies, waits for them, and re-layouts: 17.1 us -> 20 us
  Pallas kernels: 21 us -> 23.6 us
    all_to_all x2, waiting for transfers between devices: 18.2 us -> 2.74 us  [columns(): lax.all_to_all(samp, ('z', 'x'), split_axis=0, concat_axis=0, tiled=True)]
    ppermute x9, waiting for transfers between devices: 38.8 us -> 50.1 us  [ring_y(): return lax.ppermute(x, 'y', [(i, (i + step) % RING) for i in range(RING)])]
    pallas_call x4, Pallas kernels: 8.14 us -> 10.8 us  [expand(): pl.pallas_call(functools.partial(expand_kernel, kind, own), in_specs=[SME...]
    ppermute x12, waiting for transfers between devices: 12.5 us -> 9.89 us  [ring_zx(): return lax.ppermute(x, ('core', 'z', 'x'), pairs)]
    unnamed x51 -> x37, local copies, waits for them, and re-layouts: 5.12 us -> 4.55 us
  transfers between devices with their start and end apart: 38 -> 38, of which waited for: 21 -> 18; matrix products, arithmetic and copies ran while one was open for 9% -> 11% of each run, Pallas kernels for 7% -> 7%
where the time goes in v4:
time: 189 us; the launch traced here: 188 us
  starting transfers between devices  66.7 us (35%)
  waiting for transfers between devices  66.7 us (35%)
  Pallas kernels  23.6 us (12%)
  local copies, waits for them, and re-layouts  20 us (11%)
  matrix products  5.84 us (3%)
  other arithmetic  3.79 us (2%)
    ppermute x9, waiting for transfers between devices, ring_y(): return lax.ppermute(x, 'y', [(i, (i + step) % RING) for i in range(RING)])  50.1 us
    ppermute x15, starting transfers between devices, swap_core(): return lax.ppermute(x, 'core', [(0, 1), (1, 0)])  26.9 us
    ppermute x12, starting transfers between devices, ring_zx(): return lax.ppermute(x, ('core', 'z', 'x'), pairs)  16.1 us
    all_to_all x2, starting transfers between devices, columns(): lax.all_to_all(samp, ('z', 'x'), split_axis=0, concat_axis=0, tiled=True)  13 us
    pallas_call x4, Pallas kernels, expand(): pl.pallas_call(functools.partial(expand_kernel, kind, own), in_specs=[SME...  10.8 us
    ppermute x9, starting transfers between devices, ring_y(): return lax.ppermute(x, 'y', [(i, (i + step) % RING) for i in range(RING)])  10.7 us
    ppermute x12, waiting for transfers between devices, ring_zx(): return lax.ppermute(x, ('core', 'z', 'x'), pairs)  9.89 us
    dot_general x2, matrix products, per_device(): jnp.einsum('scn,cnr->csr', omega, basis, preferred_element_type=F32)  5.84 us
  transfers between devices with their start and end apart: 38, of which 18 were waited for; matrix products, arithmetic and copies ran while one was open for 11% of the time, Pallas kernels for 7%

profile of v4, /device:TPU:1, one launch (start us, length us, event | category | flops | bytes accessed | tf_op | source)
XLA Modules:
  0.0 187.8 jit_solution(15944435845054157504)
XLA Ops:
  0.6 4.3 %convolution_convert_fusion.1 = bf16[2,320,1024]{2,1,0:T(8,128)(2,1)S(1)} fusion(bf16[2,1024,1024]{2,1,0:T(8,128)(2,1)} %param.10, bf16[320,2,1024]{2,1,0:T(2,128)(2,1)} %param.8), kind=kOutput, calls=%fused_computation.8 | convolution fusion | flops 1342832640 | bytes 6815744 | tf_op jit(solution)/shard_map/scn,cnr->csr/dot_general | solution.py:290
  14.8 2.2 %collective-permute-start.3 = (bf16[160,1024]{1,0:T(8,128)(2,1)S(1)}, bf16[160,1024]{1,0:T(8,128)(2,1)S(1)}, u32[]{:S(2)}, u32[]{:S(2)}) collective-permute-start(bf16[160,1024]{1,0:T(8,128)(2,1)S(1)} %get-tuple-element.59), channel_id=1, source_target_pairs={{0,3},{1,0},{2,1},{3,2},{4,7},{5,4},{6,5},{7,6},{8,11},{9,8},{10,9... | collective-permute-start | bytes 983048 | tf_op jit(solution)/shard_map/ppermute | solution.py:35
  21.4 3.1 %collective-permute-done.3 = bf16[160,1024]{1,0:T(8,128)(2,1)S(1)} collective-permute-done((bf16[160,1024]{1,0:T(8,128)(2,1)S(1)}, bf16[160,1024]{1,0:T(8,128)(2,1)S(1)}, u32[]{:S(2)}, u32[]{:S(2)}) %collective-permute-start.3) | collective-permute-done | bytes 327712 | tf_op jit(solution)/shard_map/ppermute | solution.py:35
  34.4 3.0 %collective-permute-start.10 = (bf16[48,1024]{1,0:T(8,128)(2,1)S(1)}, bf16[48,1024]{1,0:T(8,128)(2,1)S(1)}, u32[]{:S(2)}, u32[]{:S(2)}) collective-permute-start(bf16[48,1024]{1,0:T(8,128)(2,1)S(1)} %shard_map.79.a), channel_id=1, source_target_pairs={{0,64},{32,96},{64,0},{96,32},{1,65},{33,97},{65,1},{97,33},{2,66}... | collective-permute-start | bytes 294920 | tf_op jit(solution)/shard_map/ppermute | solution.py:19
  40.9 2.9 %collective-permute-done.9.b = bf16[48,1024]{1,0:T(8,128)(2,1)S(1)} collective-permute-done((bf16[48,1024]{1,0:T(8,128)(2,1)S(1)}, bf16[48,1024]{1,0:T(8,128)(2,1)S(1)}, u32[]{:S(2)}, u32[]{:S(2)}) %collective-permute-start.9) | collective-permute-done | bytes 98336 | tf_op jit(solution)/shard_map/ppermute | solution.py:19
  45.2 2.5 %collective-permute-start.13 = (bf16[48,1024]{1,0:T(8,128)(2,1)S(1)}, bf16[48,1024]{1,0:T(8,128)(2,1)S(1)}, u32[]{:S(2)}, u32[]{:S(2)}) collective-permute-start(bf16[48,1024]{1,0:T(8,128)(2,1)S(1)} %shard_map.80), channel_id=1, source_target_pairs={{0,8},{1,9},{2,10},{3,11},{4,12},{5,13},{6,14},{7,15},{8,0},{9,1},... | collective-permute-start | bytes 294920 | tf_op jit(solution)/shard_map/ppermute | solution.py:35
  55.1 7.3 %collective-permute-start.18 = (bf16[4,48,1024]{2,1,0:T(8,128)(2,1)S(1)}, bf16[4,48,1024]{2,1,0:T(8,128)(2,1)S(1)}, u32[]{:S(2)}, u32[]{:S(2)}) collective-permute-start(bf16[4,48,1024]{2,1,0:T(8,128)(2,1)S(1)} %pad_maximum_fusion.refs_0_), channel_id=1, source_target_pairs={{0,16},{16,0},{1,17},{17,1},{2,18},{18,2},{3,19},{19,3},{4,20},{20... | collective-permute-start | bytes 1179656 | tf_op jit(solution)/shard_map/ppermute | solution.py:23
  62.5 3.9 %collective-permute-start.19 = (bf16[4,48,1024]{2,1,0:T(8,128)(2,1)}, bf16[4,48,1024]{2,1,0:T(8,128)(2,1)S(1)}, u32[]{:S(2)}, u32[]{:S(2)}) collective-permute-start(bf16[4,48,1024]{2,1,0:T(8,128)(2,1)} %collective-permute-done.15.refs_1_), channel_id=1, source_target_pairs={{0,16},{16,0},{1,17},{17,1},{2,18},{18,2},{3,19},{19,3},{4,20},{20... | collective-permute-start | bytes 1179656 | tf_op jit(solution)/shard_map/ppermute | solution.py:23
  66.4 4.2 %collective-permute-start.20 = (bf16[4,48,1024]{2,1,0:T(8,128)(2,1)}, bf16[4,48,1024]{2,1,0:T(8,128)(2,1)S(1)}, u32[]{:S(2)}, u32[]{:S(2)}) collective-permute-start(bf16[4,48,1024]{2,1,0:T(8,128)(2,1)} %collective-permute-done.16.refs_2_), channel_id=1, source_target_pairs={{0,16},{16,0},{1,17},{17,1},{2,18},{18,2},{3,19},{19,3},{4,20},{20... | collective-permute-start | bytes 1179656 | tf_op jit(solution)/shard_map/ppermute | solution.py:23
  73.1 2.8 %shard_map.81 = (bf16[320,8,128]{2,1,0:T(8,128)(2,1)S(1)}, bf16[4,4,16,128]{3,2,1,0:T(8,128)(2,1)S(1)}) custom-call(s32[5]{0:T(128)S(1)} %stack.38.place, bf16[4,48,1024]{2,1,0:T(8,128)(2,1)S(1)} %pad_maximum_fusion.refs_0_, bf16[4,48,1024]{2,1,0:T(8,128)(2,1)} %collective-permute-done.15.refs_1_, bf16[4,48,1024]{2,1,0:T(8,128)(2,1)} %collective-permute-done.16.refs_2_, ...), custom_call_target="tpu_custom_call" | custom-call | flops 838860800 | bytes 6291456 | tf_op jit(solution)/shard_map/pallas_call | solution.py:194
  79.2 9.0 %all-to-all-start = ((bf16[320,16,128]{2,1,0:T(8,128)(2,1)}), bf16[320,16,128]{2,1,0:T(8,128)(2,1)}, u32[]{:S(2)}, u32[]{:S(2)}) async-start(bf16[320,16,128]{2,1,0:T(8,128)(2,1)} %copy-done.3), calls=%async_computation | async-start | bytes 2621440 | tf_op jit(solution)/shard_map/all_to_all | solution.py:339
  97.1 2.7 %dynamic-slice_bitcast_fusion = (bf16[1024,1024]{1,0:T(8,128)(2,1)S(1)}, bf16[1024,1024]{1,0:T(8,128)(2,1)S(1)}) fusion(bf16[2,1024,1024]{2,1,0:T(8,128)(2,1)} %param.10, s32[]{:T(128)S(6)} %select_n.132, s32[]{:T(128)S(6)} %select_n.133), kind=kLoop, calls=%fused_computation.1 | loop fusion | bytes 8388616 | tf_op jit(solution)/shard_map/jit(dynamic_index_in_dim)/squeeze | solution.py:312
  99.8 2.8 %shard_map.83.refs_7_ = bf16[320,8,128]{2,1,0:T(8,128)(2,1)S(1)} custom-call(s32[5]{0:T(128)S(1)} %stack.38.place, bf16[4,48,1024]{2,1,0:T(8,128)(2,1)S(1)} %pad_maximum_fusion.refs_0_, bf16[4,48,1024]{2,1,0:T(8,128)(2,1)} %collective-permute-done.15.refs_1_, bf16[4,48,1024]{2,1,0:T(8,128)(2,1)} %collective-permute-done.16.refs_2_, ...), custom_call_target="tpu_custom_call" | custom-call | flops 838860800 | bytes 6291456 | tf_op jit(solution)/shard_map/pallas_call | solution.py:194
  102.6 3.1 %shard_map.84 = bf16[320,16,128]{2,1,0:T(8,128)(2,1)} custom-call(s32[5]{0:T(128)S(1)} %stack.38.place, bf16[4,48,1024]{2,1,0:T(8,128)(2,1)S(1)} %collective-permute-done.18.refs_0_, bf16[4,48,1024]{2,1,0:T(8,128)(2,1)S(1)} %collective-permute-done.19.refs_1_, bf16[4,48,1024]{2,1,0:T(8,128)(2,1)S(1)} %copy-done.5, bf16[4,48,1024]{2,1,0:T(8,128)(2,1)S(1)} %copy-done.7, ...), custom_call_target="tpu_custom_call" | custom-call | flops 838860800 | bytes 6291456 | tf_op jit(solution)/shard_map/pallas_call | solution.py:194
  107.3 2.7 %all-to-all-done = bf16[320,16,128]{2,1,0:T(8,128)(2,1)} async-done(((bf16[320,16,128]{2,1,0:T(8,128)(2,1)}), bf16[320,16,128]{2,1,0:T(8,128)(2,1)}, u32[]{:S(2)}, u32[]{:S(2)}) %all-to-all-start) | async-done | bytes 1310752 | tf_op jit(solution)/shard_map/all_to_all | solution.py:339
  110.0 3.1 %shard_map.86 = (bf16[2,20,64,128]{3,2,1,0:T(8,128)(2,1)S(1)}, bf16[2,20,64,128]{3,2,1,0:T(8,128)(2,1)}, bf16[2,20,64,128]{3,2,1,0:T(8,128)(2,1)}, bf16[2,20,64,128]{3,2,1,0:T(8,128)(2,1)}) custom-call(bf16[512,256]{1,0:T(8,128)(2,1)S(1)} %fusion.2.selector, bf16[16,20,16,128]{3,2,1,0:T(8,128)(2,1)} %bitcast.27.columns), custom_call_target="tpu_custom_call" | custom-call | flops 671088640 | bytes 8388608 | tf_op jit(solution)/shard_map/pallas_call | solution.py:224
  113.1 2.7 %collective-permute-start.24 = (bf16[2,20,64,128]{3,2,1,0:T(8,128)(2,1)}, bf16[2,20,64,128]{3,2,1,0:T(8,128)(2,1)}, u32[]{:S(2)}, u32[]{:S(2)}) collective-permute-start(bf16[2,20,64,128]{3,2,1,0:T(8,128)(2,1)} %get-tuple-element.84), channel_id=1, source_target_pairs={{0,96},{32,0},{64,32},{96,64},{1,97},{33,1},{65,33},{97,65},{2,98}... | collective-permute-start | bytes 1966088 | tf_op jit(solution)/shard_map/ppermute | solution.py:19
  115.8 4.0 %all-to-all-start.1 = ((bf16[320,16,128]{2,1,0:T(8,128)(2,1)}), bf16[320,16,128]{2,1,0:T(8,128)(2,1)S(1)}, u32[]{:S(2)}, u32[]{:S(2)}) async-start(bf16[320,16,128]{2,1,0:T(8,128)(2,1)} %shard_map.84), calls=%async_computation.1 | async-start | bytes 2621440 | tf_op jit(solution)/shard_map/all_to_all | solution.py:339
  121.2 22.4 %collective-permute-done.22.refs_1_ = bf16[2,20,64,128]{3,2,1,0:T(8,128)(2,1)S(1)} collective-permute-done((bf16[2,20,64,128]{3,2,1,0:T(8,128)(2,1)}, bf16[2,20,64,128]{3,2,1,0:T(8,128)(2,1)S(1)}, u32[]{:S(2)}, u32[]{:S(2)}) %collective-permute-start.22) | collective-permute-done | bytes 655392 | tf_op jit(solution)/shard_map/ppermute | solution.py:19
  151.0 2.7 %collective-permute-start.31 = (bf16[2,20,64,128]{3,2,1,0:T(8,128)(2,1)S(1)}, bf16[2,20,64,128]{3,2,1,0:T(8,128)(2,1)S(1)}, u32[]{:S(2)}, u32[]{:S(2)}) collective-permute-start(bf16[2,20,64,128]{3,2,1,0:T(8,128)(2,1)S(1)} %get-tuple-element.89), channel_id=1, source_target_pairs={{0,96},{32,0},{64,32},{96,64},{1,97},{33,1},{65,33},{97,65},{2,98}... | collective-permute-start | bytes 1966088 | tf_op jit(solution)/shard_map/ppermute | solution.py:19
  153.7 3.4 %shard_map.87 = f32[20,256,128]{2,1,0:T(8,128)} custom-call(bf16[256,512]{1,0:T(8,128)(2,1)S(1)} %fusion.3.placer, bf16[2,20,64,128]{3,2,1,0:T(8,128)(2,1)S(1)} %get-tuple-element.81.refs_0_, bf16[2,20,64,128]{3,2,1,0:T(8,128)(2,1)S(1)} %collective-permute-done.22.refs_1_, bf16[2,20,64,128]{3,2,1,0:T(8,128)(2,1)S(1)} %collective-permute-done.23.refs_2_, ...), custom_call_target="tpu_custom_call" | custom-call | flops 671088640 | bytes 10485760 | tf_op jit(solution)/shard_map/pallas_call | solution.py:253
  158.2 10.4 %collective-permute-done.29.refs_1_ = bf16[2,20,64,128]{3,2,1,0:T(8,128)(2,1)S(1)} collective-permute-done((bf16[2,20,64,128]{3,2,1,0:T(8,128)(2,1)S(1)}, bf16[2,20,64,128]{3,2,1,0:T(8,128)(2,1)S(1)}, u32[]{:S(2)}, u32[]{:S(2)}) %collective-permute-start.29) | collective-permute-done | bytes 655392 | tf_op jit(solution)/shard_map/ppermute | solution.py:19
  169.3 12.1 %collective-permute-done.31.refs_3_ = bf16[2,20,64,128]{3,2,1,0:T(8,128)(2,1)S(1)} collective-permute-done((bf16[2,20,64,128]{3,2,1,0:T(8,128)(2,1)S(1)}, bf16[2,20,64,128]{3,2,1,0:T(8,128)(2,1)S(1)}, u32[]{:S(2)}, u32[]{:S(2)}) %collective-permute-start.31) | collective-permute-done | bytes 655392 | tf_op jit(solution)/shard_map/ppermute | solution.py:19
  185.7 2.1 %shard_map.88 = f32[20,256,128]{2,1,0:T(8,128)} custom-call(bf16[256,512]{1,0:T(8,128)(2,1)S(1)} %fusion.3.placer, bf16[2,20,64,128]{3,2,1,0:T(8,128)(2,1)S(1)} %get-tuple-element.86.refs_0_, bf16[2,20,64,128]{3,2,1,0:T(8,128)(2,1)S(1)} %collective-permute-done.29.refs_1_, bf16[2,20,64,128]{3,2,1,0:T(8,128)(2,1)S(1)} %collective-permute-done.30.refs_2_, ...), custom_call_target="tpu_custom_call" | custom-call | flops 671088640 | bytes 10485760 | tf_op jit(solution)/shard_map/pallas_call | solution.py:253
  (142 shorter events, 67.2 us)
Async XLA Ops:
  13.0 8.4 %collective-permute-start.2 = (bf16[160,1024]{1,0:T(8,128)(2,1)S(1)}, bf16[160,1024]{1,0:T(8,128)(2,1)S(1)}, u32[]{:S(2)}, u32[]{:S(2)}) collective-permute-start(bf16[160,1024]{1,0:T(8,128)(2,1)S(1)} %get-tuple-element.58), channel_id=1, source_target_pairs={{0,1},{1,2},{2,3},{3,0},{4,5},{5,6},{6,7},{7,4},{8,9},{9,10},{10,1... | collective-permute-start | bytes 983048 | tf_op jit(solution)/shard_map/ppermute | solution.py:35
  14.8 9.7 %collective-permute-start.3 = (bf16[160,1024]{1,0:T(8,128)(2,1)S(1)}, bf16[160,1024]{1,0:T(8,128)(2,1)S(1)}, u32[]{:S(2)}, u32[]{:S(2)}) collective-permute-start(bf16[160,1024]{1,0:T(8,128)(2,1)S(1)} %get-tuple-element.59), channel_id=1, source_target_pairs={{0,3},{1,0},{2,1},{3,2},{4,7},{5,4},{6,5},{7,6},{8,11},{9,8},{10,9... | collective-permute-start | bytes 983048 | tf_op jit(solution)/shard_map/ppermute | solution.py:35
  17.0 9.1 %collective-permute-start.4 = (bf16[160,1024]{1,0:T(8,128)(2,1)S(1)}, bf16[160,1024]{1,0:T(8,128)(2,1)S(1)}, u32[]{:S(2)}, u32[]{:S(2)}) collective-permute-start(bf16[160,1024]{1,0:T(8,128)(2,1)S(1)} %get-tuple-element.60), channel_id=1, source_target_pairs={{0,2},{1,3},{2,0},{3,1},{4,6},{5,7},{6,4},{7,5},{8,10},{9,11},{10,... | collective-permute-start | bytes 983048 | tf_op jit(solution)/shard_map/ppermute | solution.py:35
  45.1 5.8 %collective-permute-start.12 = (bf16[48,1024]{1,0:T(8,128)(2,1)S(1)}, bf16[48,1024]{1,0:T(8,128)(2,1)S(1)}, u32[]{:S(2)}, u32[]{:S(2)}) collective-permute-start(bf16[48,1024]{1,0:T(8,128)(2,1)S(1)} %shard_map.80), channel_id=1, source_target_pairs={{0,4},{1,5},{2,6},{3,7},{4,8},{5,9},{6,10},{7,11},{8,12},{9,13},{1... | collective-permute-start | bytes 294920 | tf_op jit(solution)/shard_map/ppermute | solution.py:35
  51.6 10.9 %collective-permute-start.15 = (bf16[4,48,1024]{2,1,0:T(8,128)(2,1)S(1)}, bf16[4,48,1024]{2,1,0:T(8,128)(2,1)}, u32[]{:S(2)}, u32[]{:S(2)}) collective-permute-start(bf16[4,48,1024]{2,1,0:T(8,128)(2,1)S(1)} %pad_maximum_fusion.refs_0_), channel_id=1, source_target_pairs={{0,1},{1,2},{2,3},{3,0},{4,5},{5,6},{6,7},{7,4},{8,9},{9,10},{10,1... | collective-permute-start | bytes 1179656 | tf_op jit(solution)/shard_map/ppermute | solution.py:35
  52.4 14.0 %collective-permute-start.16 = (bf16[4,48,1024]{2,1,0:T(8,128)(2,1)S(1)}, bf16[4,48,1024]{2,1,0:T(8,128)(2,1)}, u32[]{:S(2)}, u32[]{:S(2)}) collective-permute-start(bf16[4,48,1024]{2,1,0:T(8,128)(2,1)S(1)} %pad_maximum_fusion.refs_0_), channel_id=1, source_target_pairs={{0,2},{1,3},{2,0},{3,1},{4,6},{5,7},{6,4},{7,5},{8,10},{9,11},{10,... | collective-permute-start | bytes 1179656 | tf_op jit(solution)/shard_map/ppermute | solution.py:35
  54.4 16.2 %collective-permute-start.17 = (bf16[4,48,1024]{2,1,0:T(8,128)(2,1)S(1)}, bf16[4,48,1024]{2,1,0:T(8,128)(2,1)}, u32[]{:S(2)}, u32[]{:S(2)}) collective-permute-start(bf16[4,48,1024]{2,1,0:T(8,128)(2,1)S(1)} %pad_maximum_fusion.refs_0_), channel_id=1, source_target_pairs={{0,3},{1,0},{2,1},{3,2},{4,7},{5,4},{6,5},{7,6},{8,11},{9,8},{10,9... | collective-permute-start | bytes 1179656 | tf_op jit(solution)/shard_map/ppermute | solution.py:35
  55.1 20.9 %collective-permute-start.18 = (bf16[4,48,1024]{2,1,0:T(8,128)(2,1)S(1)}, bf16[4,48,1024]{2,1,0:T(8,128)(2,1)S(1)}, u32[]{:S(2)}, u32[]{:S(2)}) collective-permute-start(bf16[4,48,1024]{2,1,0:T(8,128)(2,1)S(1)} %pad_maximum_fusion.refs_0_), channel_id=1, source_target_pairs={{0,16},{16,0},{1,17},{17,1},{2,18},{18,2},{3,19},{19,3},{4,20},{20... | collective-permute-start | bytes 1179656 | tf_op jit(solution)/shard_map/ppermute | solution.py:23
  62.5 13.5 %collective-permute-start.19 = (bf16[4,48,1024]{2,1,0:T(8,128)(2,1)}, bf16[4,48,1024]{2,1,0:T(8,128)(2,1)S(1)}, u32[]{:S(2)}, u32[]{:S(2)}) collective-permute-start(bf16[4,48,1024]{2,1,0:T(8,128)(2,1)} %collective-permute-done.15.refs_1_), channel_id=1, source_target_pairs={{0,16},{16,0},{1,17},{17,1},{2,18},{18,2},{3,19},{19,3},{4,20},{20... | collective-permute-start | bytes 1179656 | tf_op jit(solution)/shard_map/ppermute | solution.py:23
  66.4 9.6 %collective-permute-start.20 = (bf16[4,48,1024]{2,1,0:T(8,128)(2,1)}, bf16[4,48,1024]{2,1,0:T(8,128)(2,1)S(1)}, u32[]{:S(2)}, u32[]{:S(2)}) collective-permute-start(bf16[4,48,1024]{2,1,0:T(8,128)(2,1)} %collective-permute-done.16.refs_2_), channel_id=1, source_target_pairs={{0,16},{16,0},{1,17},{17,1},{2,18},{18,2},{3,19},{19,3},{4,20},{20... | collective-permute-start | bytes 1179656 | tf_op jit(solution)/shard_map/ppermute | solution.py:23
  79.2 30.8 %all-to-all-start = ((bf16[320,16,128]{2,1,0:T(8,128)(2,1)}), bf16[320,16,128]{2,1,0:T(8,128)(2,1)}, u32[]{:S(2)}, u32[]{:S(2)}) async-start(bf16[320,16,128]{2,1,0:T(8,128)(2,1)} %copy-done.3), calls=%async_computation | async-start | bytes 2621440 | tf_op jit(solution)/shard_map/all_to_all | solution.py:339
  113.1 30.6 %collective-permute-start.22 = (bf16[2,20,64,128]{3,2,1,0:T(8,128)(2,1)}, bf16[2,20,64,128]{3,2,1,0:T(8,128)(2,1)S(1)}, u32[]{:S(2)}, u32[]{:S(2)}) collective-permute-start(bf16[2,20,64,128]{3,2,1,0:T(8,128)(2,1)} %get-tuple-element.82), channel_id=1, source_target_pairs={{0,32},{32,64},{64,96},{96,0},{1,33},{33,65},{65,97},{97,1},{2,34}... | collective-permute-start | bytes 1966088 | tf_op jit(solution)/shard_map/ppermute | solution.py:19
  113.1 32.6 %collective-permute-start.23 = (bf16[2,20,64,128]{3,2,1,0:T(8,128)(2,1)}, bf16[2,20,64,128]{3,2,1,0:T(8,128)(2,1)S(1)}, u32[]{:S(2)}, u32[]{:S(2)}) collective-permute-start(bf16[2,20,64,128]{3,2,1,0:T(8,128)(2,1)} %get-tuple-element.83), channel_id=1, source_target_pairs={{0,64},{32,96},{64,0},{96,32},{1,65},{33,97},{65,1},{97,33},{2,66}... | collective-permute-start | bytes 1966088 | tf_op jit(solution)/shard_map/ppermute | solution.py:19
  113.1 32.6 %collective-permute-start.24 = (bf16[2,20,64,128]{3,2,1,0:T(8,128)(2,1)}, bf16[2,20,64,128]{3,2,1,0:T(8,128)(2,1)}, u32[]{:S(2)}, u32[]{:S(2)}) collective-permute-start(bf16[2,20,64,128]{3,2,1,0:T(8,128)(2,1)} %get-tuple-element.84), channel_id=1, source_target_pairs={{0,96},{32,0},{64,32},{96,64},{1,97},{33,1},{65,33},{97,65},{2,98}... | collective-permute-start | bytes 1966088 | tf_op jit(solution)/shard_map/ppermute | solution.py:19
  115.8 32.7 %all-to-all-start.1 = ((bf16[320,16,128]{2,1,0:T(8,128)(2,1)}), bf16[320,16,128]{2,1,0:T(8,128)(2,1)S(1)}, u32[]{:S(2)}, u32[]{:S(2)}) async-start(bf16[320,16,128]{2,1,0:T(8,128)(2,1)} %shard_map.84), calls=%async_computation.1 | async-start | bytes 2621440 | tf_op jit(solution)/shard_map/all_to_all | solution.py:339
  119.8 31.2 %collective-permute-start.25 = (bf16[2,20,64,128]{3,2,1,0:T(8,128)(2,1)S(1)}, bf16[2,20,64,128]{3,2,1,0:T(8,128)(2,1)}, u32[]{:S(2)}, u32[]{:S(2)}) collective-permute-start(bf16[2,20,64,128]{3,2,1,0:T(8,128)(2,1)S(1)} %get-tuple-element.81.refs_0_), channel_id=1, source_target_pairs={{0,16},{16,0},{1,17},{17,1},{2,18},{18,2},{3,19},{19,3},{4,20},{20... | collective-permute-start | bytes 1966088 | tf_op jit(solution)/shard_map/ppermute | solution.py:23
  143.7 10.0 %collective-permute-start.26 = (bf16[2,20,64,128]{3,2,1,0:T(8,128)(2,1)S(1)}, bf16[2,20,64,128]{3,2,1,0:T(8,128)(2,1)}, u32[]{:S(2)}, u32[]{:S(2)}) collective-permute-start(bf16[2,20,64,128]{3,2,1,0:T(8,128)(2,1)S(1)} %collective-permute-done.22.refs_1_), channel_id=1, source_target_pairs={{0,16},{16,0},{1,17},{17,1},{2,18},{18,2},{3,19},{19,3},{4,20},{20... | collective-permute-start | bytes 1966088 | tf_op jit(solution)/shard_map/ppermute | solution.py:23
  145.7 8.0 %collective-permute-start.27 = (bf16[2,20,64,128]{3,2,1,0:T(8,128)(2,1)S(1)}, bf16[2,20,64,128]{3,2,1,0:T(8,128)(2,1)}, u32[]{:S(2)}, u32[]{:S(2)}) collective-permute-start(bf16[2,20,64,128]{3,2,1,0:T(8,128)(2,1)S(1)} %collective-permute-done.23.refs_2_), channel_id=1, source_target_pairs={{0,16},{16,0},{1,17},{17,1},{2,18},{18,2},{3,19},{19,3},{4,20},{20... | collective-permute-start | bytes 1966088 | tf_op jit(solution)/shard_map/ppermute | solution.py:23
  145.7 8.0 %collective-permute-start.28 = (bf16[2,20,64,128]{3,2,1,0:T(8,128)(2,1)}, bf16[2,20,64,128]{3,2,1,0:T(8,128)(2,1)}, u32[]{:S(2)}, u32[]{:S(2)}) collective-permute-start(bf16[2,20,64,128]{3,2,1,0:T(8,128)(2,1)} %collective-permute-done.24.refs_3_), channel_id=1, source_target_pairs={{0,16},{16,0},{1,17},{17,1},{2,18},{18,2},{3,19},{19,3},{4,20},{20... | collective-permute-start | bytes 1966088 | tf_op jit(solution)/shard_map/ppermute | solution.py:23
  150.7 17.9 %collective-permute-start.29 = (bf16[2,20,64,128]{3,2,1,0:T(8,128)(2,1)S(1)}, bf16[2,20,64,128]{3,2,1,0:T(8,128)(2,1)S(1)}, u32[]{:S(2)}, u32[]{:S(2)}) collective-permute-start(bf16[2,20,64,128]{3,2,1,0:T(8,128)(2,1)S(1)} %get-tuple-element.87), channel_id=1, source_target_pairs={{0,32},{32,64},{64,96},{96,0},{1,33},{33,65},{65,97},{97,1},{2,34}... | collective-permute-start | bytes 1966088 | tf_op jit(solution)/shard_map/ppermute | solution.py:19
  151.0 30.4 %collective-permute-start.31 = (bf16[2,20,64,128]{3,2,1,0:T(8,128)(2,1)S(1)}, bf16[2,20,64,128]{3,2,1,0:T(8,128)(2,1)S(1)}, u32[]{:S(2)}, u32[]{:S(2)}) collective-permute-start(bf16[2,20,64,128]{3,2,1,0:T(8,128)(2,1)S(1)} %get-tuple-element.89), channel_id=1, source_target_pairs={{0,96},{32,0},{64,32},{96,64},{1,97},{33,1},{65,33},{97,65},{2,98}... | collective-permute-start | bytes 1966088 | tf_op jit(solution)/shard_map/ppermute | solution.py:19
  157.1 26.1 %collective-permute-start.30 = (bf16[2,20,64,128]{3,2,1,0:T(8,128)(2,1)S(1)}, bf16[2,20,64,128]{3,2,1,0:T(8,128)(2,1)S(1)}, u32[]{:S(2)}, u32[]{:S(2)}) collective-permute-start(bf16[2,20,64,128]{3,2,1,0:T(8,128)(2,1)S(1)} %get-tuple-element.88), channel_id=1, source_target_pairs={{0,64},{32,96},{64,0},{96,32},{1,65},{33,97},{65,1},{97,33},{2,66}... | collective-permute-start | bytes 1966088 | tf_op jit(solution)/shard_map/ppermute | solution.py:19
  157.6 26.3 %collective-permute-start.32 = (bf16[2,20,64,128]{3,2,1,0:T(8,128)(2,1)S(1)}, bf16[2,20,64,128]{3,2,1,0:T(8,128)(2,1)S(1)}, u32[]{:S(2)}, u32[]{:S(2)}) collective-permute-start(bf16[2,20,64,128]{3,2,1,0:T(8,128)(2,1)S(1)} %get-tuple-element.86.refs_0_), channel_id=1, source_target_pairs={{0,16},{16,0},{1,17},{17,1},{2,18},{18,2},{3,19},{19,3},{4,20},{20... | collective-permute-start | bytes 1966088 | tf_op jit(solution)/shard_map/ppermute | solution.py:23
  168.6 15.4 %collective-permute-start.33 = (bf16[2,20,64,128]{3,2,1,0:T(8,128)(2,1)S(1)}, bf16[2,20,64,128]{3,2,1,0:T(8,128)(2,1)S(1)}, u32[]{:S(2)}, u32[]{:S(2)}) collective-permute-start(bf16[2,20,64,128]{3,2,1,0:T(8,128)(2,1)S(1)} %collective-permute-done.29.refs_1_), channel_id=1, source_target_pairs={{0,16},{16,0},{1,17},{17,1},{2,18},{18,2},{3,19},{19,3},{4,20},{20... | collective-permute-start | bytes 1966088 | tf_op jit(solution)/shard_map/ppermute | solution.py:23
  (32 other events, 159.5 us)

commit v5 on v4

--- a/solution.py
+++ b/solution.py
@@ -330,11 +330,6 @@
     step = (dest[0] // 2 - y_me) % RING
     slot = (jnp.where(dest[0] % 2 == core, 0, RING) + step) * capacity + order[0]
     selector = (jnp.arange(row_count * capacity)[:, None] == slot[None, :]).astype(BF16)
-    arriving = jnp.where(dest == y_me * 2 + core, order, -1)
-    spots = jnp.arange(capacity)
-    ids = jnp.sum((spots[None, :, None] == arriving[:, None, :]) * (home + 1)[:, None, :], axis=2) - 1
-    placer = (jnp.arange(owner_rows)[:, None] == ids.reshape(-1)[None, :]).astype(BF16)
-
     def columns(samp):
         got = lax.all_to_all(samp, ("z", "x"), split_axis=0, concat_axis=0, tiled=True)
         return got.reshape(col_count, share, near, BLK)
@@ -344,6 +339,12 @@
     y_out = send(selector, y_cols, capacity)
     y_out = [y_out[0]] + [ring_y(y_out[k], k) for k in (1, 2, 3)]
     z_out = list(send(selector, columns(z_samp), capacity))
+    order, home, z_out[0] = lax.optimization_barrier((order, home, z_out[0]))
+    arriving = jnp.where(dest == y_me * 2 + core, order, -1)
+    spots = jnp.arange(capacity)
+    ids = jnp.sum((spots[None, :, None] == arriving[:, None, :]) * (home + 1)[:, None, :], axis=2) - 1
+    placer = (jnp.arange(owner_rows)[:, None] == ids.reshape(-1)[None, :]).astype(BF16)
+
     parent_y = place_blocks(placer, y_out)
     z_out[2], parent_y = lax.optimization_barrier((z_out[2], parent_y))
     z_out = [z_out[0]] + [ring_y(z_out[k], k) for k in (1, 2, 3)]

time: 189 us -> 197 us (1.042)
  local copies, waits for them, and re-layouts: 20 us -> 26.8 us
    unnamed x37 -> x41, local copies, waits for them, and re-layouts: 4.55 us -> 8.03 us
    slice x0 -> x3, local copies, waits for them, and re-layouts: none -> 2.76 us  [per_device(): dest, home = (seen[0], seen[1])]
  transfers between devices with their start and end apart: 38 -> 38, of which waited for: 18 -> 18; matrix products, arithmetic and copies ran while one was open for 11% -> 13% of each run, Pallas kernels for 7% -> 8%
where the time goes in v5:
time: 197 us; the launch traced here: 196 us
  starting transfers between devices  67.5 us (34%)
  waiting for transfers between devices  67.1 us (34%)
  local copies, waits for them, and re-layouts  26.8 us (14%)
  Pallas kernels  23.7 us (12%)
  matrix products  5.84 us (3%)
  other arithmetic  4.3 us (2%)
    ppermute x9, waiting for transfers between devices, ring_y(): return lax.ppermute(x, 'y', [(i, (i + step) % RING) for i in range(RING)])  51.3 us
    ppermute x15, starting transfers between devices, swap_core(): return lax.ppermute(x, 'core', [(0, 1), (1, 0)])  26.8 us
    ppermute x12, starting transfers between devices, ring_zx(): return lax.ppermute(x, ('core', 'z', 'x'), pairs)  16.1 us
    all_to_all x2, starting transfers between devices, columns(): lax.all_to_all(samp, ('z', 'x'), split_axis=0, concat_axis=0, tiled=True)  13.8 us
    pallas_call x4, Pallas kernels, expand(): pl.pallas_call(functools.partial(expand_kernel, kind, own), in_specs=[SME...  10.9 us
    ppermute x9, starting transfers between devices, ring_y(): return lax.ppermute(x, 'y', [(i, (i + step) % RING) for i in range(RING)])  10.8 us
    ppermute x12, waiting for transfers between devices, ring_zx(): return lax.ppermute(x, ('core', 'z', 'x'), pairs)  9.89 us
    unnamed x41, local copies, waits for them, and re-layouts  8.03 us
  transfers between devices with their start and end apart: 38, of which 18 were waited for; matrix products, arithmetic and copies ran while one was open for 13% of the time, Pallas kernels for 8%

profile of v5, /device:TPU:1, one launch (start us, length us, event | category | flops | bytes accessed | tf_op | source)
XLA Modules:
  0.0 196.3 jit_solution(4443724128616386407)
XLA Ops:
  0.6 4.3 %convolution_convert_fusion.1 = bf16[2,320,1024]{2,1,0:T(8,128)(2,1)S(1)} fusion(bf16[2,1024,1024]{2,1,0:T(8,128)(2,1)} %param.10, bf16[320,2,1024]{2,1,0:T(2,128)(2,1)} %param.8), kind=kOutput, calls=%fused_computation.8 | convolution fusion | flops 1342832640 | bytes 6815744 | tf_op jit(solution)/shard_map/scn,cnr->csr/dot_general | solution.py:290
  14.8 2.2 %collective-permute-start.3 = (bf16[160,1024]{1,0:T(8,128)(2,1)S(1)}, bf16[160,1024]{1,0:T(8,128)(2,1)S(1)}, u32[]{:S(2)}, u32[]{:S(2)}) collective-permute-start(bf16[160,1024]{1,0:T(8,128)(2,1)S(1)} %get-tuple-element.62), channel_id=1, source_target_pairs={{0,3},{1,0},{2,1},{3,2},{4,7},{5,4},{6,5},{7,6},{8,11},{9,8},{10,9... | collective-permute-start | bytes 983048 | tf_op jit(solution)/shard_map/ppermute | solution.py:35
  21.4 3.1 %collective-permute-done.3 = bf16[160,1024]{1,0:T(8,128)(2,1)S(1)} collective-permute-done((bf16[160,1024]{1,0:T(8,128)(2,1)S(1)}, bf16[160,1024]{1,0:T(8,128)(2,1)S(1)}, u32[]{:S(2)}, u32[]{:S(2)}) %collective-permute-start.3) | collective-permute-done | bytes 327712 | tf_op jit(solution)/shard_map/ppermute | solution.py:35
  34.4 3.0 %collective-permute-start.10 = (bf16[48,1024]{1,0:T(8,128)(2,1)S(1)}, bf16[48,1024]{1,0:T(8,128)(2,1)S(1)}, u32[]{:S(2)}, u32[]{:S(2)}) collective-permute-start(bf16[48,1024]{1,0:T(8,128)(2,1)S(1)} %shard_map.79.a), channel_id=1, source_target_pairs={{0,64},{32,96},{64,0},{96,32},{1,65},{33,97},{65,1},{97,33},{2,66}... | collective-permute-start | bytes 294920 | tf_op jit(solution)/shard_map/ppermute | solution.py:19
  40.9 2.9 %collective-permute-done.9.b = bf16[48,1024]{1,0:T(8,128)(2,1)S(1)} collective-permute-done((bf16[48,1024]{1,0:T(8,128)(2,1)S(1)}, bf16[48,1024]{1,0:T(8,128)(2,1)S(1)}, u32[]{:S(2)}, u32[]{:S(2)}) %collective-permute-start.9) | collective-permute-done | bytes 98336 | tf_op jit(solution)/shard_map/ppermute | solution.py:19
  45.2 2.5 %collective-permute-start.13 = (bf16[48,1024]{1,0:T(8,128)(2,1)S(1)}, bf16[48,1024]{1,0:T(8,128)(2,1)S(1)}, u32[]{:S(2)}, u32[]{:S(2)}) collective-permute-start(bf16[48,1024]{1,0:T(8,128)(2,1)S(1)} %shard_map.80), channel_id=1, source_target_pairs={{0,8},{1,9},{2,10},{3,11},{4,12},{5,13},{6,14},{7,15},{8,0},{9,1},... | collective-permute-start | bytes 294920 | tf_op jit(solution)/shard_map/ppermute | solution.py:35
  54.9 7.4 %collective-permute-start.18 = (bf16[4,48,1024]{2,1,0:T(8,128)(2,1)S(1)}, bf16[4,48,1024]{2,1,0:T(8,128)(2,1)S(1)}, u32[]{:S(2)}, u32[]{:S(2)}) collective-permute-start(bf16[4,48,1024]{2,1,0:T(8,128)(2,1)S(1)} %pad_maximum_fusion.refs_0_), channel_id=1, source_target_pairs={{0,16},{16,0},{1,17},{17,1},{2,18},{18,2},{3,19},{19,3},{4,20},{20... | collective-permute-start | bytes 1179656 | tf_op jit(solution)/shard_map/ppermute | solution.py:23
  62.4 4.0 %collective-permute-start.19 = (bf16[4,48,1024]{2,1,0:T(8,128)(2,1)}, bf16[4,48,1024]{2,1,0:T(8,128)(2,1)S(1)}, u32[]{:S(2)}, u32[]{:S(2)}) collective-permute-start(bf16[4,48,1024]{2,1,0:T(8,128)(2,1)} %collective-permute-done.15.refs_1_), channel_id=1, source_target_pairs={{0,16},{16,0},{1,17},{17,1},{2,18},{18,2},{3,19},{19,3},{4,20},{20... | collective-permute-start | bytes 1179656 | tf_op jit(solution)/shard_map/ppermute | solution.py:23
  66.4 4.2 %collective-permute-start.20 = (bf16[4,48,1024]{2,1,0:T(8,128)(2,1)}, bf16[4,48,1024]{2,1,0:T(8,128)(2,1)}, u32[]{:S(2)}, u32[]{:S(2)}) collective-permute-start(bf16[4,48,1024]{2,1,0:T(8,128)(2,1)} %collective-permute-done.16.refs_2_), channel_id=1, source_target_pairs={{0,16},{16,0},{1,17},{17,1},{2,18},{18,2},{3,19},{19,3},{4,20},{20... | collective-permute-start | bytes 1179656 | tf_op jit(solution)/shard_map/ppermute | solution.py:23
  73.3 2.9 %shard_map.81 = (bf16[320,8,128]{2,1,0:T(8,128)(2,1)S(1)}, bf16[4,4,16,128]{3,2,1,0:T(8,128)(2,1)S(1)}) custom-call(s32[5]{0:T(128)S(1)} %stack.38.place, bf16[4,48,1024]{2,1,0:T(8,128)(2,1)S(1)} %pad_maximum_fusion.refs_0_, bf16[4,48,1024]{2,1,0:T(8,128)(2,1)} %collective-permute-done.15.refs_1_, bf16[4,48,1024]{2,1,0:T(8,128)(2,1)} %collective-permute-done.16.refs_2_, ...), custom_call_target="tpu_custom_call" | custom-call | flops 838860800 | bytes 6291456 | tf_op jit(solution)/shard_map/pallas_call | solution.py:194
  76.2 2.6 %shard_map.82 = bf16[320,16,128]{2,1,0:T(8,128)(2,1)S(1)} custom-call(s32[5]{0:T(128)S(1)} %stack.38.place, bf16[4,48,1024]{2,1,0:T(8,128)(2,1)S(1)} %collective-permute-done.18.refs_0_, bf16[4,48,1024]{2,1,0:T(8,128)(2,1)S(1)} %collective-permute-done.19.refs_1_, bf16[4,48,1024]{2,1,0:T(8,128)(2,1)} %collective-permute-done.20.refs_2_, ...), custom_call_target="tpu_custom_call" | custom-call | flops 838860800 | bytes 6291456 | tf_op jit(solution)/shard_map/pallas_call | solution.py:194
  79.9 9.0 %all-to-all-start = ((bf16[320,16,128]{2,1,0:T(8,128)(2,1)}), bf16[320,16,128]{2,1,0:T(8,128)(2,1)}, u32[]{:S(2)}, u32[]{:S(2)}) async-start(bf16[320,16,128]{2,1,0:T(8,128)(2,1)} %copy-done.4), calls=%async_computation | async-start | bytes 2621440 | tf_op jit(solution)/shard_map/all_to_all | solution.py:334
  99.6 2.7 %dynamic-slice_bitcast_fusion = (bf16[1024,1024]{1,0:T(8,128)(2,1)S(1)}, bf16[1024,1024]{1,0:T(8,128)(2,1)S(1)}) fusion(bf16[2,1024,1024]{2,1,0:T(8,128)(2,1)} %param.10, s32[]{:T(128)S(6)} %select_n.128, s32[]{:T(128)S(6)} %select_n.129), kind=kLoop, calls=%fused_computation.1 | loop fusion | bytes 8388616 | tf_op jit(solution)/shard_map/jit(dynamic_index_in_dim)/squeeze | solution.py:312
  102.2 2.7 %shard_map.83.refs_7_ = bf16[320,8,128]{2,1,0:T(8,128)(2,1)S(1)} custom-call(s32[5]{0:T(128)S(1)} %stack.38.place, bf16[4,48,1024]{2,1,0:T(8,128)(2,1)S(1)} %pad_maximum_fusion.refs_0_, bf16[4,48,1024]{2,1,0:T(8,128)(2,1)} %collective-permute-done.15.refs_1_, bf16[4,48,1024]{2,1,0:T(8,128)(2,1)} %collective-permute-done.16.refs_2_, ...), custom_call_target="tpu_custom_call" | custom-call | flops 838860800 | bytes 6291456 | tf_op jit(solution)/shard_map/pallas_call | solution.py:194
  105.0 2.7 %shard_map.84 = bf16[320,16,128]{2,1,0:T(8,128)(2,1)S(1)} custom-call(s32[5]{0:T(128)S(1)} %stack.38.place, bf16[4,48,1024]{2,1,0:T(8,128)(2,1)S(1)} %collective-permute-done.18.refs_0_, bf16[4,48,1024]{2,1,0:T(8,128)(2,1)S(1)} %collective-permute-done.19.refs_1_, bf16[4,48,1024]{2,1,0:T(8,128)(2,1)} %collective-permute-done.20.refs_2_, ...), custom_call_target="tpu_custom_call" | custom-call | flops 838860800 | bytes 6291456 | tf_op jit(solution)/shard_map/pallas_call | solution.py:194
  110.7 4.7 %all-to-all-start.1 = ((bf16[320,16,128]{2,1,0:T(8,128)(2,1)}), bf16[320,16,128]{2,1,0:T(8,128)(2,1)S(1)}, u32[]{:S(2)}, u32[]{:S(2)}) async-start(bf16[320,16,128]{2,1,0:T(8,128)(2,1)} %copy-done.3), calls=%async_computation.1 | async-start | bytes 2621440 | tf_op jit(solution)/shard_map/all_to_all | solution.py:334
  116.9 3.1 %shard_map.86 = (bf16[2,20,64,128]{3,2,1,0:T(8,128)(2,1)S(1)}, bf16[2,20,64,128]{3,2,1,0:T(8,128)(2,1)}, bf16[2,20,64,128]{3,2,1,0:T(8,128)(2,1)}, bf16[2,20,64,128]{3,2,1,0:T(8,128)(2,1)}) custom-call(bf16[512,256]{1,0:T(8,128)(2,1)S(1)} %fusion.2.selector, bf16[16,20,16,128]{3,2,1,0:T(8,128)(2,1)} %bitcast.27.columns), custom_call_target="tpu_custom_call" | custom-call | flops 671088640 | bytes 8388608 | tf_op jit(solution)/shard_map/pallas_call | solution.py:224
  120.0 2.7 %collective-permute-start.24 = (bf16[2,20,64,128]{3,2,1,0:T(8,128)(2,1)}, bf16[2,20,64,128]{3,2,1,0:T(8,128)(2,1)}, u32[]{:S(2)}, u32[]{:S(2)}) collective-permute-start(bf16[2,20,64,128]{3,2,1,0:T(8,128)(2,1)} %get-tuple-element.90), channel_id=1, source_target_pairs={{0,96},{32,0},{64,32},{96,64},{1,97},{33,1},{65,33},{97,65},{2,98}... | collective-permute-start | bytes 1966088 | tf_op jit(solution)/shard_map/ppermute | solution.py:19
  127.1 23.8 %collective-permute-done.22.refs_1_ = bf16[2,20,64,128]{3,2,1,0:T(8,128)(2,1)S(1)} collective-permute-done((bf16[2,20,64,128]{3,2,1,0:T(8,128)(2,1)}, bf16[2,20,64,128]{3,2,1,0:T(8,128)(2,1)S(1)}, u32[]{:S(2)}, u32[]{:S(2)}) %collective-permute-start.22) | collective-permute-done | bytes 655392 | tf_op jit(solution)/shard_map/ppermute | solution.py:19
  159.4 2.7 %collective-permute-start.31 = (bf16[2,20,64,128]{3,2,1,0:T(8,128)(2,1)}, bf16[2,20,64,128]{3,2,1,0:T(8,128)(2,1)S(1)}, u32[]{:S(2)}, u32[]{:S(2)}) collective-permute-start(bf16[2,20,64,128]{3,2,1,0:T(8,128)(2,1)} %copy-done.10), channel_id=1, source_target_pairs={{0,96},{32,0},{64,32},{96,64},{1,97},{33,1},{65,33},{97,65},{2,98}... | collective-permute-start | bytes 1966088 | tf_op jit(solution)/shard_map/ppermute | solution.py:19
  162.1 3.4 %shard_map.87 = f32[20,256,128]{2,1,0:T(8,128)} custom-call(bf16[256,512]{1,0:T(8,128)(2,1)S(1)} %fusion.3.placer, bf16[2,20,64,128]{3,2,1,0:T(8,128)(2,1)S(1)} %get-tuple-element.87.refs_0_, bf16[2,20,64,128]{3,2,1,0:T(8,128)(2,1)S(1)} %collective-permute-done.22.refs_1_, bf16[2,20,64,128]{3,2,1,0:T(8,128)(2,1)S(1)} %collective-permute-done.23.refs_2_, ...), custom_call_target="tpu_custom_call" | custom-call | flops 671088640 | bytes 10485760 | tf_op jit(solution)/shard_map/pallas_call | solution.py:253
  166.8 10.2 %collective-permute-done.29.refs_1_ = bf16[2,20,64,128]{3,2,1,0:T(8,128)(2,1)S(1)} collective-permute-done((bf16[2,20,64,128]{3,2,1,0:T(8,128)(2,1)}, bf16[2,20,64,128]{3,2,1,0:T(8,128)(2,1)S(1)}, u32[]{:S(2)}, u32[]{:S(2)}) %collective-permute-start.29) | collective-permute-done | bytes 655392 | tf_op jit(solution)/shard_map/ppermute | solution.py:19
  177.8 12.3 %collective-permute-done.31.refs_3_ = bf16[2,20,64,128]{3,2,1,0:T(8,128)(2,1)S(1)} collective-permute-done((bf16[2,20,64,128]{3,2,1,0:T(8,128)(2,1)}, bf16[2,20,64,128]{3,2,1,0:T(8,128)(2,1)S(1)}, u32[]{:S(2)}, u32[]{:S(2)}) %collective-permute-start.31) | collective-permute-done | bytes 655392 | tf_op jit(solution)/shard_map/ppermute | solution.py:19
  194.2 2.1 %shard_map.88 = f32[20,256,128]{2,1,0:T(8,128)} custom-call(bf16[256,512]{1,0:T(8,128)(2,1)S(1)} %fusion.3.placer, bf16[2,20,64,128]{3,2,1,0:T(8,128)(2,1)S(1)} %copy-done.6, bf16[2,20,64,128]{3,2,1,0:T(8,128)(2,1)S(1)} %collective-permute-done.29.refs_1_, bf16[2,20,64,128]{3,2,1,0:T(8,128)(2,1)S(1)} %collective-permute-done.30.refs_2_, ...), custom_call_target="tpu_custom_call" | custom-call | flops 671088640 | bytes 10485760 | tf_op jit(solution)/shard_map/pallas_call | solution.py:253
  (149 shorter events, 73.9 us)
Async XLA Ops:
  13.0 8.4 %collective-permute-start.2 = (bf16[160,1024]{1,0:T(8,128)(2,1)S(1)}, bf16[160,1024]{1,0:T(8,128)(2,1)S(1)}, u32[]{:S(2)}, u32[]{:S(2)}) collective-permute-start(bf16[160,1024]{1,0:T(8,128)(2,1)S(1)} %get-tuple-element.61), channel_id=1, source_target_pairs={{0,1},{1,2},{2,3},{3,0},{4,5},{5,6},{6,7},{7,4},{8,9},{9,10},{10,1... | collective-permute-start | bytes 983048 | tf_op jit(solution)/shard_map/ppermute | solution.py:35
  14.8 9.7 %collective-permute-start.3 = (bf16[160,1024]{1,0:T(8,128)(2,1)S(1)}, bf16[160,1024]{1,0:T(8,128)(2,1)S(1)}, u32[]{:S(2)}, u32[]{:S(2)}) collective-permute-start(bf16[160,1024]{1,0:T(8,128)(2,1)S(1)} %get-tuple-element.62), channel_id=1, source_target_pairs={{0,3},{1,0},{2,1},{3,2},{4,7},{5,4},{6,5},{7,6},{8,11},{9,8},{10,9... | collective-permute-start | bytes 983048 | tf_op jit(solution)/shard_map/ppermute | solution.py:35
  17.0 9.1 %collective-permute-start.4 = (bf16[160,1024]{1,0:T(8,128)(2,1)S(1)}, bf16[160,1024]{1,0:T(8,128)(2,1)S(1)}, u32[]{:S(2)}, u32[]{:S(2)}) collective-permute-start(bf16[160,1024]{1,0:T(8,128)(2,1)S(1)} %get-tuple-element.63), channel_id=1, source_target_pairs={{0,2},{1,3},{2,0},{3,1},{4,6},{5,7},{6,4},{7,5},{8,10},{9,11},{10,... | collective-permute-start | bytes 983048 | tf_op jit(solution)/shard_map/ppermute | solution.py:35
  45.1 5.8 %collective-permute-start.12 = (bf16[48,1024]{1,0:T(8,128)(2,1)S(1)}, bf16[48,1024]{1,0:T(8,128)(2,1)S(1)}, u32[]{:S(2)}, u32[]{:S(2)}) collective-permute-start(bf16[48,1024]{1,0:T(8,128)(2,1)S(1)} %shard_map.80), channel_id=1, source_target_pairs={{0,4},{1,5},{2,6},{3,7},{4,8},{5,9},{6,10},{7,11},{8,12},{9,13},{1... | collective-permute-start | bytes 294920 | tf_op jit(solution)/shard_map/ppermute | solution.py:35
  51.6 10.8 %collective-permute-start.15 = (bf16[4,48,1024]{2,1,0:T(8,128)(2,1)S(1)}, bf16[4,48,1024]{2,1,0:T(8,128)(2,1)}, u32[]{:S(2)}, u32[]{:S(2)}) collective-permute-start(bf16[4,48,1024]{2,1,0:T(8,128)(2,1)S(1)} %pad_maximum_fusion.refs_0_), channel_id=1, source_target_pairs={{0,1},{1,2},{2,3},{3,0},{4,5},{5,6},{6,7},{7,4},{8,9},{9,10},{10,1... | collective-permute-start | bytes 1179656 | tf_op jit(solution)/shard_map/ppermute | solution.py:35
  52.4 14.0 %collective-permute-start.16 = (bf16[4,48,1024]{2,1,0:T(8,128)(2,1)S(1)}, bf16[4,48,1024]{2,1,0:T(8,128)(2,1)}, u32[]{:S(2)}, u32[]{:S(2)}) collective-permute-start(bf16[4,48,1024]{2,1,0:T(8,128)(2,1)S(1)} %pad_maximum_fusion.refs_0_), channel_id=1, source_target_pairs={{0,2},{1,3},{2,0},{3,1},{4,6},{5,7},{6,4},{7,5},{8,10},{9,11},{10,... | collective-permute-start | bytes 1179656 | tf_op jit(solution)/shard_map/ppermute | solution.py:35
  54.4 16.2 %collective-permute-start.17 = (bf16[4,48,1024]{2,1,0:T(8,128)(2,1)S(1)}, bf16[4,48,1024]{2,1,0:T(8,128)(2,1)}, u32[]{:S(2)}, u32[]{:S(2)}) collective-permute-start(bf16[4,48,1024]{2,1,0:T(8,128)(2,1)S(1)} %pad_maximum_fusion.refs_0_), channel_id=1, source_target_pairs={{0,3},{1,0},{2,1},{3,2},{4,7},{5,4},{6,5},{7,6},{8,11},{9,8},{10,9... | collective-permute-start | bytes 1179656 | tf_op jit(solution)/shard_map/ppermute | solution.py:35
  54.9 21.2 %collective-permute-start.18 = (bf16[4,48,1024]{2,1,0:T(8,128)(2,1)S(1)}, bf16[4,48,1024]{2,1,0:T(8,128)(2,1)S(1)}, u32[]{:S(2)}, u32[]{:S(2)}) collective-permute-start(bf16[4,48,1024]{2,1,0:T(8,128)(2,1)S(1)} %pad_maximum_fusion.refs_0_), channel_id=1, source_target_pairs={{0,16},{16,0},{1,17},{17,1},{2,18},{18,2},{3,19},{19,3},{4,20},{20... | collective-permute-start | bytes 1179656 | tf_op jit(solution)/shard_map/ppermute | solution.py:23
  62.4 13.8 %collective-permute-start.19 = (bf16[4,48,1024]{2,1,0:T(8,128)(2,1)}, bf16[4,48,1024]{2,1,0:T(8,128)(2,1)S(1)}, u32[]{:S(2)}, u32[]{:S(2)}) collective-permute-start(bf16[4,48,1024]{2,1,0:T(8,128)(2,1)} %collective-permute-done.15.refs_1_), channel_id=1, source_target_pairs={{0,16},{16,0},{1,17},{17,1},{2,18},{18,2},{3,19},{19,3},{4,20},{20... | collective-permute-start | bytes 1179656 | tf_op jit(solution)/shard_map/ppermute | solution.py:23
  66.4 9.8 %collective-permute-start.20 = (bf16[4,48,1024]{2,1,0:T(8,128)(2,1)}, bf16[4,48,1024]{2,1,0:T(8,128)(2,1)}, u32[]{:S(2)}, u32[]{:S(2)}) collective-permute-start(bf16[4,48,1024]{2,1,0:T(8,128)(2,1)} %collective-permute-done.16.refs_2_), channel_id=1, source_target_pairs={{0,16},{16,0},{1,17},{17,1},{2,18},{18,2},{3,19},{19,3},{4,20},{20... | collective-permute-start | bytes 1179656 | tf_op jit(solution)/shard_map/ppermute | solution.py:23
  79.9 30.8 %all-to-all-start = ((bf16[320,16,128]{2,1,0:T(8,128)(2,1)}), bf16[320,16,128]{2,1,0:T(8,128)(2,1)}, u32[]{:S(2)}, u32[]{:S(2)}) async-start(bf16[320,16,128]{2,1,0:T(8,128)(2,1)} %copy-done.4), calls=%async_computation | async-start | bytes 2621440 | tf_op jit(solution)/shard_map/all_to_all | solution.py:334
  110.7 42.6 %all-to-all-start.1 = ((bf16[320,16,128]{2,1,0:T(8,128)(2,1)}), bf16[320,16,128]{2,1,0:T(8,128)(2,1)S(1)}, u32[]{:S(2)}, u32[]{:S(2)}) async-start(bf16[320,16,128]{2,1,0:T(8,128)(2,1)} %copy-done.3), calls=%async_computation.1 | async-start | bytes 2621440 | tf_op jit(solution)/shard_map/all_to_all | solution.py:334
  120.0 30.9 %collective-permute-start.22 = (bf16[2,20,64,128]{3,2,1,0:T(8,128)(2,1)}, bf16[2,20,64,128]{3,2,1,0:T(8,128)(2,1)S(1)}, u32[]{:S(2)}, u32[]{:S(2)}) collective-permute-start(bf16[2,20,64,128]{3,2,1,0:T(8,128)(2,1)} %get-tuple-element.88), channel_id=1, source_target_pairs={{0,32},{32,64},{64,96},{96,0},{1,33},{33,65},{65,97},{97,1},{2,34}... | collective-permute-start | bytes 1966088 | tf_op jit(solution)/shard_map/ppermute | solution.py:19
  120.0 32.6 %collective-permute-start.23 = (bf16[2,20,64,128]{3,2,1,0:T(8,128)(2,1)}, bf16[2,20,64,128]{3,2,1,0:T(8,128)(2,1)S(1)}, u32[]{:S(2)}, u32[]{:S(2)}) collective-permute-start(bf16[2,20,64,128]{3,2,1,0:T(8,128)(2,1)} %get-tuple-element.89), channel_id=1, source_target_pairs={{0,64},{32,96},{64,0},{96,32},{1,65},{33,97},{65,1},{97,33},{2,66}... | collective-permute-start | bytes 1966088 | tf_op jit(solution)/shard_map/ppermute | solution.py:19
  120.0 32.6 %collective-permute-start.24 = (bf16[2,20,64,128]{3,2,1,0:T(8,128)(2,1)}, bf16[2,20,64,128]{3,2,1,0:T(8,128)(2,1)}, u32[]{:S(2)}, u32[]{:S(2)}) collective-permute-start(bf16[2,20,64,128]{3,2,1,0:T(8,128)(2,1)} %get-tuple-element.90), channel_id=1, source_target_pairs={{0,96},{32,0},{64,32},{96,64},{1,97},{33,1},{65,33},{97,65},{2,98}... | collective-permute-start | bytes 1966088 | tf_op jit(solution)/shard_map/ppermute | solution.py:19
  125.7 33.7 %collective-permute-start.25 = (bf16[2,20,64,128]{3,2,1,0:T(8,128)(2,1)S(1)}, bf16[2,20,64,128]{3,2,1,0:T(8,128)(2,1)}, u32[]{:S(2)}, u32[]{:S(2)}) collective-permute-start(bf16[2,20,64,128]{3,2,1,0:T(8,128)(2,1)S(1)} %get-tuple-element.87.refs_0_), channel_id=1, source_target_pairs={{0,16},{16,0},{1,17},{17,1},{2,18},{18,2},{3,19},{19,3},{4,20},{20... | collective-permute-start | bytes 1966088 | tf_op jit(solution)/shard_map/ppermute | solution.py:23
  150.9 11.2 %collective-permute-start.26 = (bf16[2,20,64,128]{3,2,1,0:T(8,128)(2,1)S(1)}, bf16[2,20,64,128]{3,2,1,0:T(8,128)(2,1)}, u32[]{:S(2)}, u32[]{:S(2)}) collective-permute-start(bf16[2,20,64,128]{3,2,1,0:T(8,128)(2,1)S(1)} %collective-permute-done.22.refs_1_), channel_id=1, source_target_pairs={{0,16},{16,0},{1,17},{17,1},{2,18},{18,2},{3,19},{19,3},{4,20},{20... | collective-permute-start | bytes 1966088 | tf_op jit(solution)/shard_map/ppermute | solution.py:23
  152.6 9.5 %collective-permute-start.27 = (bf16[2,20,64,128]{3,2,1,0:T(8,128)(2,1)S(1)}, bf16[2,20,64,128]{3,2,1,0:T(8,128)(2,1)}, u32[]{:S(2)}, u32[]{:S(2)}) collective-permute-start(bf16[2,20,64,128]{3,2,1,0:T(8,128)(2,1)S(1)} %collective-permute-done.23.refs_2_), channel_id=1, source_target_pairs={{0,16},{16,0},{1,17},{17,1},{2,18},{18,2},{3,19},{19,3},{4,20},{20... | collective-permute-start | bytes 1966088 | tf_op jit(solution)/shard_map/ppermute | solution.py:23
  152.6 9.5 %collective-permute-start.28 = (bf16[2,20,64,128]{3,2,1,0:T(8,128)(2,1)}, bf16[2,20,64,128]{3,2,1,0:T(8,128)(2,1)}, u32[]{:S(2)}, u32[]{:S(2)}) collective-permute-start(bf16[2,20,64,128]{3,2,1,0:T(8,128)(2,1)} %collective-permute-done.24.refs_3_), channel_id=1, source_target_pairs={{0,16},{16,0},{1,17},{17,1},{2,18},{18,2},{3,19},{19,3},{4,20},{20... | collective-permute-start | bytes 1966088 | tf_op jit(solution)/shard_map/ppermute | solution.py:23
  159.1 18.0 %collective-permute-start.29 = (bf16[2,20,64,128]{3,2,1,0:T(8,128)(2,1)}, bf16[2,20,64,128]{3,2,1,0:T(8,128)(2,1)S(1)}, u32[]{:S(2)}, u32[]{:S(2)}) collective-permute-start(bf16[2,20,64,128]{3,2,1,0:T(8,128)(2,1)} %copy-done.11), channel_id=1, source_target_pairs={{0,32},{32,64},{64,96},{96,0},{1,33},{33,65},{65,97},{97,1},{2,34}... | collective-permute-start | bytes 1966088 | tf_op jit(solution)/shard_map/ppermute | solution.py:19
  159.4 30.8 %collective-permute-start.31 = (bf16[2,20,64,128]{3,2,1,0:T(8,128)(2,1)}, bf16[2,20,64,128]{3,2,1,0:T(8,128)(2,1)S(1)}, u32[]{:S(2)}, u32[]{:S(2)}) collective-permute-start(bf16[2,20,64,128]{3,2,1,0:T(8,128)(2,1)} %copy-done.10), channel_id=1, source_target_pairs={{0,96},{32,0},{64,32},{96,64},{1,97},{33,1},{65,33},{97,65},{2,98}... | collective-permute-start | bytes 1966088 | tf_op jit(solution)/shard_map/ppermute | solution.py:19
  165.5 26.1 %collective-permute-start.30 = (bf16[2,20,64,128]{3,2,1,0:T(8,128)(2,1)S(1)}, bf16[2,20,64,128]{3,2,1,0:T(8,128)(2,1)S(1)}, u32[]{:S(2)}, u32[]{:S(2)}) collective-permute-start(bf16[2,20,64,128]{3,2,1,0:T(8,128)(2,1)S(1)} %copy-done.9), channel_id=1, source_target_pairs={{0,64},{32,96},{64,0},{96,32},{1,65},{33,97},{65,1},{97,33},{2,66}... | collective-permute-start | bytes 1966088 | tf_op jit(solution)/shard_map/ppermute | solution.py:19
  166.2 26.2 %collective-permute-start.32 = (bf16[2,20,64,128]{3,2,1,0:T(8,128)(2,1)S(1)}, bf16[2,20,64,128]{3,2,1,0:T(8,128)(2,1)S(1)}, u32[]{:S(2)}, u32[]{:S(2)}) collective-permute-start(bf16[2,20,64,128]{3,2,1,0:T(8,128)(2,1)S(1)} %copy-done.6), channel_id=1, source_target_pairs={{0,16},{16,0},{1,17},{17,1},{2,18},{18,2},{3,19},{19,3},{4,20},{20... | collective-permute-start | bytes 1966088 | tf_op jit(solution)/shard_map/ppermute | solution.py:23
  177.0 15.4 %collective-permute-start.33 = (bf16[2,20,64,128]{3,2,1,0:T(8,128)(2,1)S(1)}, bf16[2,20,64,128]{3,2,1,0:T(8,128)(2,1)S(1)}, u32[]{:S(2)}, u32[]{:S(2)}) collective-permute-start(bf16[2,20,64,128]{3,2,1,0:T(8,128)(2,1)S(1)} %collective-permute-done.29.refs_1_), channel_id=1, source_target_pairs={{0,16},{16,0},{1,17},{17,1},{2,18},{18,2},{3,19},{19,3},{4,20},{20... | collective-permute-start | bytes 1966088 | tf_op jit(solution)/shard_map/ppermute | solution.py:23
  (34 other events, 163.9 us)

commit v6 on v4

--- a/solution.py
+++ b/solution.py
@@ -340,7 +340,6 @@
         return got.reshape(col_count, share, near, BLK)
 
     y_cols = columns(y_samp)
-    z_samp, y_cols = lax.optimization_barrier((z_samp, y_cols))
     y_out = send(selector, y_cols, capacity)
     y_out = [y_out[0]] + [ring_y(y_out[k], k) for k in (1, 2, 3)]
     z_out = list(send(selector, columns(z_samp), capacity))

time: 189 us -> 193 us (1.021)
  waiting for transfers between devices: 66.7 us -> 49.2 us
  starting transfers between devices: 66.7 us -> 83.4 us
  matrix products: 5.84 us -> 8.9 us
  local copies, waits for them, and re-layouts: 20 us -> 22.6 us
    ppermute x9, waiting for transfers between devices: 50.1 us -> 18.3 us  [ring_y(): return lax.ppermute(x, 'y', [(i, (i + step) % RING) for i in range(RING)])]
    ppermute x15, starting transfers between devices: 26.9 us -> 46.2 us  [swap_core(): return lax.ppermute(x, 'core', [(0, 1), (1, 0)])]
    all_to_all x2, waiting for transfers between devices: 2.74 us -> 15.6 us  [columns(): lax.all_to_all(samp, ('z', 'x'), split_axis=0, concat_axis=0, tiled=True)]
    all_to_all x2, starting transfers between devices: 13 us -> 8.22 us  [columns(): lax.all_to_all(samp, ('z', 'x'), split_axis=0, concat_axis=0, tiled=True)]
    dot_general x2, matrix products: 5.84 us -> 8.9 us  [per_device(): jnp.einsum('scn,cnr->csr', omega, basis, preferred_element_type=F32)]
    unnamed x37 -> x43, local copies, waits for them, and re-layouts: 4.55 us -> 7.42 us
  transfers between devices with their start and end apart: 38 -> 38, of which waited for: 18 -> 16; matrix products, arithmetic and copies ran while one was open for 11% -> 9% of each run, Pallas kernels for 7% -> 6%
where the time goes in v6:
time: 193 us; the launch traced here: 192 us
  starting transfers between devices  83.4 us (43%)
  waiting for transfers between devices  49.2 us (25%)
  local copies, waits for them, and re-layouts  22.6 us (12%)
  Pallas kernels  22.6 us (12%)
  matrix products  8.9 us (5%)
  other arithmetic  3.8 us (2%)
    ppermute x15, starting transfers between devices, swap_core(): return lax.ppermute(x, 'core', [(0, 1), (1, 0)])  46.2 us
    ppermute x9, waiting for transfers between devices, ring_y(): return lax.ppermute(x, 'y', [(i, (i + step) % RING) for i in range(RING)])  18.3 us
    ppermute x12, starting transfers between devices, ring_zx(): return lax.ppermute(x, ('core', 'z', 'x'), pairs)  16.5 us
    all_to_all x2, waiting for transfers between devices, columns(): lax.all_to_all(samp, ('z', 'x'), split_axis=0, concat_axis=0, tiled=True)  15.6 us
    ppermute x9, starting transfers between devices, ring_y(): return lax.ppermute(x, 'y', [(i, (i + step) % RING) for i in range(RING)])  12.5 us
    ppermute x12, waiting for transfers between devices, ring_zx(): return lax.ppermute(x, ('core', 'z', 'x'), pairs)  10.7 us
    pallas_call x4, Pallas kernels, expand(): pl.pallas_call(functools.partial(expand_kernel, kind, own), in_specs=[SME...  9.77 us
    dot_general x2, matrix products, per_device(): jnp.einsum('scn,cnr->csr', omega, basis, preferred_element_type=F32)  8.9 us
  transfers between devices with their start and end apart: 38, of which 16 were waited for; matrix products, arithmetic and copies ran while one was open for 9% of the time, Pallas kernels for 6%

profile of v6, /device:TPU:1, one launch (start us, length us, event | category | flops | bytes accessed | tf_op | source)
XLA Modules:
  0.0 191.6 jit_solution(4077028972465290504)
XLA Ops:
  0.6 5.2 %convolution_convert_fusion.1 = bf16[2,320,1024]{2,1,0:T(8,128)(2,1)} fusion(bf16[2,1024,1024]{2,1,0:T(8,128)(2,1)} %param.10, bf16[320,2,1024]{2,1,0:T(2,128)(2,1)} %param.8), kind=kOutput, calls=%fused_computation.8 | convolution fusion | flops 1342832640 | bytes 6815744 | tf_op jit(solution)/shard_map/scn,cnr->csr/dot_general | solution.py:290
  8.8 3.7 %convolution_convert_fusion = bf16[2,320,1024]{2,1,0:T(8,128)(2,1)S(1)} fusion(bf16[2,1024,1024]{2,1,0:T(8,128)(2,1)} %param.9, bf16[320,2,1024]{2,1,0:T(2,128)(2,1)S(1)} %copy-done.14), kind=kOutput, calls=%fused_computation.7 | convolution fusion | flops 1342832640 | bytes 6815744 | tf_op jit(solution)/shard_map/scn,cnr->csr/dot_general | solution.py:290
  18.5 2.2 %collective-permute-start.3 = (bf16[160,1024]{1,0:T(8,128)(2,1)S(1)}, bf16[160,1024]{1,0:T(8,128)(2,1)S(1)}, u32[]{:S(2)}, u32[]{:S(2)}) collective-permute-start(bf16[160,1024]{1,0:T(8,128)(2,1)S(1)} %get-tuple-element.57), channel_id=1, source_target_pairs={{0,3},{1,0},{2,1},{3,2},{4,7},{5,4},{6,5},{7,6},{8,11},{9,8},{10,9... | collective-permute-start | bytes 983048 | tf_op jit(solution)/shard_map/ppermute | solution.py:35
  25.1 3.1 %collective-permute-done.3 = bf16[160,1024]{1,0:T(8,128)(2,1)S(1)} collective-permute-done((bf16[160,1024]{1,0:T(8,128)(2,1)S(1)}, bf16[160,1024]{1,0:T(8,128)(2,1)S(1)}, u32[]{:S(2)}, u32[]{:S(2)}) %collective-permute-start.3) | collective-permute-done | bytes 327712 | tf_op jit(solution)/shard_map/ppermute | solution.py:35
  39.5 2.6 %collective-permute-start.10 = (bf16[48,1024]{1,0:T(8,128)(2,1)S(1)}, bf16[48,1024]{1,0:T(8,128)(2,1)S(1)}, u32[]{:S(2)}, u32[]{:S(2)}) collective-permute-start(bf16[48,1024]{1,0:T(8,128)(2,1)S(1)} %shard_map.79.a), channel_id=1, source_target_pairs={{0,64},{32,96},{64,0},{96,32},{1,65},{33,97},{65,1},{97,33},{2,66}... | collective-permute-start | bytes 294920 | tf_op jit(solution)/shard_map/ppermute | solution.py:19
  58.3 7.5 %collective-permute-start.18 = (bf16[4,48,1024]{2,1,0:T(8,128)(2,1)S(1)}, bf16[4,48,1024]{2,1,0:T(8,128)(2,1)S(1)}, u32[]{:S(2)}, u32[]{:S(2)}) collective-permute-start(bf16[4,48,1024]{2,1,0:T(8,128)(2,1)S(1)} %pad_maximum_fusion.refs_0_), channel_id=1, source_target_pairs={{0,16},{16,0},{1,17},{17,1},{2,18},{18,2},{3,19},{19,3},{4,20},{20... | collective-permute-start | bytes 1179656 | tf_op jit(solution)/shard_map/ppermute | solution.py:23
  65.9 4.6 %collective-permute-start.19 = (bf16[4,48,1024]{2,1,0:T(8,128)(2,1)}, bf16[4,48,1024]{2,1,0:T(8,128)(2,1)S(1)}, u32[]{:S(2)}, u32[]{:S(2)}) collective-permute-start(bf16[4,48,1024]{2,1,0:T(8,128)(2,1)} %collective-permute-done.15.refs_1_), channel_id=1, source_target_pairs={{0,16},{16,0},{1,17},{17,1},{2,18},{18,2},{3,19},{19,3},{4,20},{20... | collective-permute-start | bytes 1179656 | tf_op jit(solution)/shard_map/ppermute | solution.py:23
  70.5 4.5 %collective-permute-start.20 = (bf16[4,48,1024]{2,1,0:T(8,128)(2,1)}, bf16[4,48,1024]{2,1,0:T(8,128)(2,1)S(1)}, u32[]{:S(2)}, u32[]{:S(2)}) collective-permute-start(bf16[4,48,1024]{2,1,0:T(8,128)(2,1)} %collective-permute-done.16.refs_2_), channel_id=1, source_target_pairs={{0,16},{16,0},{1,17},{17,1},{2,18},{18,2},{3,19},{19,3},{4,20},{20... | collective-permute-start | bytes 1179656 | tf_op jit(solution)/shard_map/ppermute | solution.py:23
  77.2 2.9 %shard_map.81 = (bf16[320,8,128]{2,1,0:T(8,128)(2,1)S(1)}, bf16[4,4,16,128]{3,2,1,0:T(8,128)(2,1)S(1)}) custom-call(s32[5]{0:T(128)S(1)} %stack.38.place, bf16[4,48,1024]{2,1,0:T(8,128)(2,1)S(1)} %pad_maximum_fusion.refs_0_, bf16[4,48,1024]{2,1,0:T(8,128)(2,1)} %collective-permute-done.15.refs_1_, bf16[4,48,1024]{2,1,0:T(8,128)(2,1)} %collective-permute-done.16.refs_2_, ...), custom_call_target="tpu_custom_call" | custom-call | flops 838860800 | bytes 6291456 | tf_op jit(solution)/shard_map/pallas_call | solution.py:194
  86.9 4.4 %all-to-all-start.1 = ((bf16[320,16,128]{2,1,0:T(8,128)(2,1)}), bf16[320,16,128]{2,1,0:T(8,128)(2,1)}, u32[]{:S(2)}, u32[]{:S(2)}) async-start(bf16[320,16,128]{2,1,0:T(8,128)(2,1)} %copy-done.4), calls=%async_computation.1 | async-start | bytes 2621440 | tf_op jit(solution)/shard_map/all_to_all | solution.py:339
  98.1 14.9 %all-to-all-done.1 = bf16[320,16,128]{2,1,0:T(8,128)(2,1)} async-done(((bf16[320,16,128]{2,1,0:T(8,128)(2,1)}), bf16[320,16,128]{2,1,0:T(8,128)(2,1)}, u32[]{:S(2)}, u32[]{:S(2)}) %all-to-all-start.1) | async-done | bytes 1310752 | tf_op jit(solution)/shard_map/all_to_all | solution.py:339
  114.0 3.1 %shard_map.86 = (bf16[2,20,64,128]{3,2,1,0:T(8,128)(2,1)S(1)}, bf16[2,20,64,128]{3,2,1,0:T(8,128)(2,1)}, bf16[2,20,64,128]{3,2,1,0:T(8,128)(2,1)}, bf16[2,20,64,128]{3,2,1,0:T(8,128)(2,1)}) custom-call(bf16[512,256]{1,0:T(8,128)(2,1)S(1)} %copy-done.11, bf16[16,20,16,128]{3,2,1,0:T(8,128)(2,1)} %bitcast.28.columns), custom_call_target="tpu_custom_call" | custom-call | flops 671088640 | bytes 8388608 | tf_op jit(solution)/shard_map/pallas_call | solution.py:224
  118.4 3.1 %collective-permute-start.23 = (bf16[2,20,64,128]{3,2,1,0:T(8,128)(2,1)}, bf16[2,20,64,128]{3,2,1,0:T(8,128)(2,1)}, u32[]{:S(2)}, u32[]{:S(2)}) collective-permute-start(bf16[2,20,64,128]{3,2,1,0:T(8,128)(2,1)} %get-tuple-element.79), channel_id=1, source_target_pairs={{0,64},{32,96},{64,0},{96,32},{1,65},{33,97},{65,1},{97,33},{2,66}... | collective-permute-start | bytes 1966088 | tf_op jit(solution)/shard_map/ppermute | solution.py:19
  122.3 2.7 %dynamic-slice_bitcast_fusion = (bf16[1024,1024]{1,0:T(8,128)(2,1)S(1)}, bf16[1024,1024]{1,0:T(8,128)(2,1)S(1)}) fusion(bf16[2,1024,1024]{2,1,0:T(8,128)(2,1)} %param.10, s32[]{:T(128)S(6)} %select_n.132, s32[]{:T(128)S(6)} %select_n.133), kind=kLoop, calls=%fused_computation.1 | loop fusion | bytes 8388616 | tf_op jit(solution)/shard_map/jit(dynamic_index_in_dim)/squeeze | solution.py:312
  125.0 2.8 %shard_map.83.refs_7_ = bf16[320,8,128]{2,1,0:T(8,128)(2,1)S(1)} custom-call(s32[5]{0:T(128)S(1)} %stack.38.place, bf16[4,48,1024]{2,1,0:T(8,128)(2,1)S(1)} %pad_maximum_fusion.refs_0_, bf16[4,48,1024]{2,1,0:T(8,128)(2,1)} %collective-permute-done.15.refs_1_, bf16[4,48,1024]{2,1,0:T(8,128)(2,1)} %collective-permute-done.16.refs_2_, ...), custom_call_target="tpu_custom_call" | custom-call | flops 838860800 | bytes 6291456 | tf_op jit(solution)/shard_map/pallas_call | solution.py:194
  130.9 3.8 %all-to-all-start = ((bf16[320,16,128]{2,1,0:T(8,128)(2,1)}), bf16[320,16,128]{2,1,0:T(8,128)(2,1)S(1)}, u32[]{:S(2)}, u32[]{:S(2)}) async-start(bf16[320,16,128]{2,1,0:T(8,128)(2,1)} %copy-done.3), calls=%async_computation | async-start | bytes 2621440 | tf_op jit(solution)/shard_map/all_to_all | solution.py:339
  137.4 12.1 %collective-permute-done.23.refs_2_ = bf16[2,20,64,128]{3,2,1,0:T(8,128)(2,1)} collective-permute-done((bf16[2,20,64,128]{3,2,1,0:T(8,128)(2,1)}, bf16[2,20,64,128]{3,2,1,0:T(8,128)(2,1)}, u32[]{:S(2)}, u32[]{:S(2)}) %collective-permute-start.23) | collective-permute-done | bytes 655392 | tf_op jit(solution)/shard_map/ppermute | solution.py:19
  155.7 2.1 %collective-permute-start.31 = (bf16[2,20,64,128]{3,2,1,0:T(8,128)(2,1)S(1)}, bf16[2,20,64,128]{3,2,1,0:T(8,128)(2,1)S(1)}, u32[]{:S(2)}, u32[]{:S(2)}) collective-permute-start(bf16[2,20,64,128]{3,2,1,0:T(8,128)(2,1)S(1)} %get-tuple-element.85), channel_id=1, source_target_pairs={{0,96},{32,0},{64,32},{96,64},{1,97},{33,1},{65,33},{97,65},{2,98}... | collective-permute-start | bytes 1966088 | tf_op jit(solution)/shard_map/ppermute | solution.py:19
  157.9 3.4 %shard_map.87 = f32[20,256,128]{2,1,0:T(8,128)} custom-call(bf16[256,512]{1,0:T(8,128)(2,1)S(1)} %fusion.3.placer, bf16[2,20,64,128]{3,2,1,0:T(8,128)(2,1)S(1)} %copy-done.10, bf16[2,20,64,128]{3,2,1,0:T(8,128)(2,1)} %collective-permute-done.22.refs_1_, bf16[2,20,64,128]{3,2,1,0:T(8,128)(2,1)} %collective-permute-done.23.refs_2_, ...), custom_call_target="tpu_custom_call" | custom-call | flops 671088640 | bytes 10485760 | tf_op jit(solution)/shard_map/pallas_call | solution.py:253
  161.4 4.0 %collective-permute-start.32 = (bf16[2,20,64,128]{3,2,1,0:T(8,128)(2,1)S(1)}, bf16[2,20,64,128]{3,2,1,0:T(8,128)(2,1)S(1)}, u32[]{:S(2)}, u32[]{:S(2)}) collective-permute-start(bf16[2,20,64,128]{3,2,1,0:T(8,128)(2,1)S(1)} %get-tuple-element.82.refs_0_), channel_id=1, source_target_pairs={{0,16},{16,0},{1,17},{17,1},{2,18},{18,2},{3,19},{19,3},{4,20},{20... | collective-permute-start | bytes 1966088 | tf_op jit(solution)/shard_map/ppermute | solution.py:23
  165.4 3.7 %collective-permute-done.29.refs_1_ = bf16[2,20,64,128]{3,2,1,0:T(8,128)(2,1)S(1)} collective-permute-done((bf16[2,20,64,128]{3,2,1,0:T(8,128)(2,1)S(1)}, bf16[2,20,64,128]{3,2,1,0:T(8,128)(2,1)S(1)}, u32[]{:S(2)}, u32[]{:S(2)}) %collective-permute-start.29) | collective-permute-done | bytes 655392 | tf_op jit(solution)/shard_map/ppermute | solution.py:19
  169.1 7.3 %collective-permute-start.33 = (bf16[2,20,64,128]{3,2,1,0:T(8,128)(2,1)S(1)}, bf16[2,20,64,128]{3,2,1,0:T(8,128)(2,1)S(1)}, u32[]{:S(2)}, u32[]{:S(2)}) collective-permute-start(bf16[2,20,64,128]{3,2,1,0:T(8,128)(2,1)S(1)} %collective-permute-done.29.refs_1_), channel_id=1, source_target_pairs={{0,16},{16,0},{1,17},{17,1},{2,18},{18,2},{3,19},{19,3},{4,20},{20... | collective-permute-start | bytes 1966088 | tf_op jit(solution)/shard_map/ppermute | solution.py:23
  176.3 10.6 %collective-permute-start.35 = (bf16[2,20,64,128]{3,2,1,0:T(8,128)(2,1)S(1)}, bf16[2,20,64,128]{3,2,1,0:T(8,128)(2,1)S(1)}, u32[]{:S(2)}, u32[]{:S(2)}) collective-permute-start(bf16[2,20,64,128]{3,2,1,0:T(8,128)(2,1)S(1)} %collective-permute-done.31.refs_3_), channel_id=1, source_target_pairs={{0,16},{16,0},{1,17},{17,1},{2,18},{18,2},{3,19},{19,3},{4,20},{20... | collective-permute-start | bytes 1966088 | tf_op jit(solution)/shard_map/ppermute | solution.py:23
  189.6 2.1 %shard_map.88 = f32[20,256,128]{2,1,0:T(8,128)} custom-call(bf16[256,512]{1,0:T(8,128)(2,1)S(1)} %fusion.3.placer, bf16[2,20,64,128]{3,2,1,0:T(8,128)(2,1)S(1)} %get-tuple-element.82.refs_0_, bf16[2,20,64,128]{3,2,1,0:T(8,128)(2,1)S(1)} %collective-permute-done.29.refs_1_, bf16[2,20,64,128]{3,2,1,0:T(8,128)(2,1)S(1)} %collective-permute-done.30.refs_2_, ...), custom_call_target="tpu_custom_call" | custom-call | flops 671088640 | bytes 10485760 | tf_op jit(solution)/shard_map/pallas_call | solution.py:253
  (148 shorter events, 74.1 us)
Async XLA Ops:
  7.3 6.5 %collective-permute-start = (bf16[320,1024]{1,0:T(8,128)(2,1)S(1)}, bf16[320,1024]{1,0:T(8,128)(2,1)S(1)}, u32[]{:S(2)}, u32[]{:S(2)}) collective-permute-start(bf16[320,1024]{1,0:T(8,128)(2,1)S(1)} %get-tuple-element.90), channel_id=1, source_target_pairs={{0,16},{16,0},{1,17},{17,1},{2,18},{18,2},{3,19},{19,3},{4,20},{20... | collective-permute-start | bytes 1966088 | tf_op jit(solution)/shard_map/ppermute | solution.py:23
  16.7 8.4 %collective-permute-start.2 = (bf16[160,1024]{1,0:T(8,128)(2,1)S(1)}, bf16[160,1024]{1,0:T(8,128)(2,1)S(1)}, u32[]{:S(2)}, u32[]{:S(2)}) collective-permute-start(bf16[160,1024]{1,0:T(8,128)(2,1)S(1)} %get-tuple-element.56), channel_id=1, source_target_pairs={{0,1},{1,2},{2,3},{3,0},{4,5},{5,6},{6,7},{7,4},{8,9},{9,10},{10,1... | collective-permute-start | bytes 983048 | tf_op jit(solution)/shard_map/ppermute | solution.py:35
  18.5 9.7 %collective-permute-start.3 = (bf16[160,1024]{1,0:T(8,128)(2,1)S(1)}, bf16[160,1024]{1,0:T(8,128)(2,1)S(1)}, u32[]{:S(2)}, u32[]{:S(2)}) collective-permute-start(bf16[160,1024]{1,0:T(8,128)(2,1)S(1)} %get-tuple-element.57), channel_id=1, source_target_pairs={{0,3},{1,0},{2,1},{3,2},{4,7},{5,4},{6,5},{7,6},{8,11},{9,8},{10,9... | collective-permute-start | bytes 983048 | tf_op jit(solution)/shard_map/ppermute | solution.py:35
  20.7 9.1 %collective-permute-start.4 = (bf16[160,1024]{1,0:T(8,128)(2,1)S(1)}, bf16[160,1024]{1,0:T(8,128)(2,1)S(1)}, u32[]{:S(2)}, u32[]{:S(2)}) collective-permute-start(bf16[160,1024]{1,0:T(8,128)(2,1)S(1)} %get-tuple-element.58), channel_id=1, source_target_pairs={{0,2},{1,3},{2,0},{3,1},{4,6},{5,7},{6,4},{7,5},{8,10},{9,11},{10,... | collective-permute-start | bytes 983048 | tf_op jit(solution)/shard_map/ppermute | solution.py:35
  54.4 11.5 %collective-permute-start.15 = (bf16[4,48,1024]{2,1,0:T(8,128)(2,1)S(1)}, bf16[4,48,1024]{2,1,0:T(8,128)(2,1)}, u32[]{:S(2)}, u32[]{:S(2)}) collective-permute-start(bf16[4,48,1024]{2,1,0:T(8,128)(2,1)S(1)} %pad_maximum_fusion.refs_0_), channel_id=1, source_target_pairs={{0,1},{1,2},{2,3},{3,0},{4,5},{5,6},{6,7},{7,4},{8,9},{9,10},{10,1... | collective-permute-start | bytes 1179656 | tf_op jit(solution)/shard_map/ppermute | solution.py:35
  55.6 14.8 %collective-permute-start.16 = (bf16[4,48,1024]{2,1,0:T(8,128)(2,1)S(1)}, bf16[4,48,1024]{2,1,0:T(8,128)(2,1)}, u32[]{:S(2)}, u32[]{:S(2)}) collective-permute-start(bf16[4,48,1024]{2,1,0:T(8,128)(2,1)S(1)} %pad_maximum_fusion.refs_0_), channel_id=1, source_target_pairs={{0,2},{1,3},{2,0},{3,1},{4,6},{5,7},{6,4},{7,5},{8,10},{9,11},{10,... | collective-permute-start | bytes 1179656 | tf_op jit(solution)/shard_map/ppermute | solution.py:35
  57.5 17.6 %collective-permute-start.17 = (bf16[4,48,1024]{2,1,0:T(8,128)(2,1)S(1)}, bf16[4,48,1024]{2,1,0:T(8,128)(2,1)}, u32[]{:S(2)}, u32[]{:S(2)}) collective-permute-start(bf16[4,48,1024]{2,1,0:T(8,128)(2,1)S(1)} %pad_maximum_fusion.refs_0_), channel_id=1, source_target_pairs={{0,3},{1,0},{2,1},{3,2},{4,7},{5,4},{6,5},{7,6},{8,11},{9,8},{10,9... | collective-permute-start | bytes 1179656 | tf_op jit(solution)/shard_map/ppermute | solution.py:35
  58.3 21.8 %collective-permute-start.18 = (bf16[4,48,1024]{2,1,0:T(8,128)(2,1)S(1)}, bf16[4,48,1024]{2,1,0:T(8,128)(2,1)S(1)}, u32[]{:S(2)}, u32[]{:S(2)}) collective-permute-start(bf16[4,48,1024]{2,1,0:T(8,128)(2,1)S(1)} %pad_maximum_fusion.refs_0_), channel_id=1, source_target_pairs={{0,16},{16,0},{1,17},{17,1},{2,18},{18,2},{3,19},{19,3},{4,20},{20... | collective-permute-start | bytes 1179656 | tf_op jit(solution)/shard_map/ppermute | solution.py:23
  65.9 14.2 %collective-permute-start.19 = (bf16[4,48,1024]{2,1,0:T(8,128)(2,1)}, bf16[4,48,1024]{2,1,0:T(8,128)(2,1)S(1)}, u32[]{:S(2)}, u32[]{:S(2)}) collective-permute-start(bf16[4,48,1024]{2,1,0:T(8,128)(2,1)} %collective-permute-done.15.refs_1_), channel_id=1, source_target_pairs={{0,16},{16,0},{1,17},{17,1},{2,18},{18,2},{3,19},{19,3},{4,20},{20... | collective-permute-start | bytes 1179656 | tf_op jit(solution)/shard_map/ppermute | solution.py:23
  70.5 9.6 %collective-permute-start.20 = (bf16[4,48,1024]{2,1,0:T(8,128)(2,1)}, bf16[4,48,1024]{2,1,0:T(8,128)(2,1)S(1)}, u32[]{:S(2)}, u32[]{:S(2)}) collective-permute-start(bf16[4,48,1024]{2,1,0:T(8,128)(2,1)} %collective-permute-done.16.refs_2_), channel_id=1, source_target_pairs={{0,16},{16,0},{1,17},{17,1},{2,18},{18,2},{3,19},{19,3},{4,20},{20... | collective-permute-start | bytes 1179656 | tf_op jit(solution)/shard_map/ppermute | solution.py:23
  86.9 26.1 %all-to-all-start.1 = ((bf16[320,16,128]{2,1,0:T(8,128)(2,1)}), bf16[320,16,128]{2,1,0:T(8,128)(2,1)}, u32[]{:S(2)}, u32[]{:S(2)}) async-start(bf16[320,16,128]{2,1,0:T(8,128)(2,1)} %copy-done.4), calls=%async_computation.1 | async-start | bytes 2621440 | tf_op jit(solution)/shard_map/all_to_all | solution.py:339
  117.9 18.7 %collective-permute-start.22 = (bf16[2,20,64,128]{3,2,1,0:T(8,128)(2,1)}, bf16[2,20,64,128]{3,2,1,0:T(8,128)(2,1)}, u32[]{:S(2)}, u32[]{:S(2)}) collective-permute-start(bf16[2,20,64,128]{3,2,1,0:T(8,128)(2,1)} %get-tuple-element.78), channel_id=1, source_target_pairs={{0,32},{32,64},{64,96},{96,0},{1,33},{33,65},{65,97},{97,1},{2,34}... | collective-permute-start | bytes 1966088 | tf_op jit(solution)/shard_map/ppermute | solution.py:19
  118.4 31.1 %collective-permute-start.23 = (bf16[2,20,64,128]{3,2,1,0:T(8,128)(2,1)}, bf16[2,20,64,128]{3,2,1,0:T(8,128)(2,1)}, u32[]{:S(2)}, u32[]{:S(2)}) collective-permute-start(bf16[2,20,64,128]{3,2,1,0:T(8,128)(2,1)} %get-tuple-element.79), channel_id=1, source_target_pairs={{0,64},{32,96},{64,0},{96,32},{1,65},{33,97},{65,1},{97,33},{2,66}... | collective-permute-start | bytes 1966088 | tf_op jit(solution)/shard_map/ppermute | solution.py:19
  121.5 30.0 %collective-permute-start.24 = (bf16[2,20,64,128]{3,2,1,0:T(8,128)(2,1)}, bf16[2,20,64,128]{3,2,1,0:T(8,128)(2,1)}, u32[]{:S(2)}, u32[]{:S(2)}) collective-permute-start(bf16[2,20,64,128]{3,2,1,0:T(8,128)(2,1)} %get-tuple-element.80), channel_id=1, source_target_pairs={{0,96},{32,0},{64,32},{96,64},{1,97},{33,1},{65,33},{97,65},{2,98}... | collective-permute-start | bytes 1966088 | tf_op jit(solution)/shard_map/ppermute | solution.py:19
  130.9 21.7 %all-to-all-start = ((bf16[320,16,128]{2,1,0:T(8,128)(2,1)}), bf16[320,16,128]{2,1,0:T(8,128)(2,1)S(1)}, u32[]{:S(2)}, u32[]{:S(2)}) async-start(bf16[320,16,128]{2,1,0:T(8,128)(2,1)} %copy-done.3), calls=%async_computation | async-start | bytes 2621440 | tf_op jit(solution)/shard_map/all_to_all | solution.py:339
  134.8 21.0 %collective-permute-start.25 = (bf16[2,20,64,128]{3,2,1,0:T(8,128)(2,1)S(1)}, bf16[2,20,64,128]{3,2,1,0:T(8,128)(2,1)S(1)}, u32[]{:S(2)}, u32[]{:S(2)}) collective-permute-start(bf16[2,20,64,128]{3,2,1,0:T(8,128)(2,1)S(1)} %copy-done.10), channel_id=1, source_target_pairs={{0,16},{16,0},{1,17},{17,1},{2,18},{18,2},{3,19},{19,3},{4,20},{20... | collective-permute-start | bytes 1966088 | tf_op jit(solution)/shard_map/ppermute | solution.py:23
  136.6 21.2 %collective-permute-start.26 = (bf16[2,20,64,128]{3,2,1,0:T(8,128)(2,1)}, bf16[2,20,64,128]{3,2,1,0:T(8,128)(2,1)S(1)}, u32[]{:S(2)}, u32[]{:S(2)}) collective-permute-start(bf16[2,20,64,128]{3,2,1,0:T(8,128)(2,1)} %collective-permute-done.22.refs_1_), channel_id=1, source_target_pairs={{0,16},{16,0},{1,17},{17,1},{2,18},{18,2},{3,19},{19,3},{4,20},{20... | collective-permute-start | bytes 1966088 | tf_op jit(solution)/shard_map/ppermute | solution.py:23
  149.5 8.4 %collective-permute-start.27 = (bf16[2,20,64,128]{3,2,1,0:T(8,128)(2,1)}, bf16[2,20,64,128]{3,2,1,0:T(8,128)(2,1)}, u32[]{:S(2)}, u32[]{:S(2)}) collective-permute-start(bf16[2,20,64,128]{3,2,1,0:T(8,128)(2,1)} %collective-permute-done.23.refs_2_), channel_id=1, source_target_pairs={{0,16},{16,0},{1,17},{17,1},{2,18},{18,2},{3,19},{19,3},{4,20},{20... | collective-permute-start | bytes 1966088 | tf_op jit(solution)/shard_map/ppermute | solution.py:23
  154.9 14.2 %collective-permute-start.29 = (bf16[2,20,64,128]{3,2,1,0:T(8,128)(2,1)S(1)}, bf16[2,20,64,128]{3,2,1,0:T(8,128)(2,1)S(1)}, u32[]{:S(2)}, u32[]{:S(2)}) collective-permute-start(bf16[2,20,64,128]{3,2,1,0:T(8,128)(2,1)S(1)} %get-tuple-element.83), channel_id=1, source_target_pairs={{0,32},{32,64},{64,96},{96,0},{1,33},{33,65},{65,97},{97,1},{2,34}... | collective-permute-start | bytes 1966088 | tf_op jit(solution)/shard_map/ppermute | solution.py:19
  155.7 20.6 %collective-permute-start.31 = (bf16[2,20,64,128]{3,2,1,0:T(8,128)(2,1)S(1)}, bf16[2,20,64,128]{3,2,1,0:T(8,128)(2,1)S(1)}, u32[]{:S(2)}, u32[]{:S(2)}) collective-permute-start(bf16[2,20,64,128]{3,2,1,0:T(8,128)(2,1)S(1)} %get-tuple-element.85), channel_id=1, source_target_pairs={{0,96},{32,0},{64,32},{96,64},{1,97},{33,1},{65,33},{97,65},{2,98}... | collective-permute-start | bytes 1966088 | tf_op jit(solution)/shard_map/ppermute | solution.py:19
  161.3 25.6 %collective-permute-start.30 = (bf16[2,20,64,128]{3,2,1,0:T(8,128)(2,1)S(1)}, bf16[2,20,64,128]{3,2,1,0:T(8,128)(2,1)S(1)}, u32[]{:S(2)}, u32[]{:S(2)}) collective-permute-start(bf16[2,20,64,128]{3,2,1,0:T(8,128)(2,1)S(1)} %get-tuple-element.84), channel_id=1, source_target_pairs={{0,64},{32,96},{64,0},{96,32},{1,65},{33,97},{65,1},{97,33},{2,66}... | collective-permute-start | bytes 1966088 | tf_op jit(solution)/shard_map/ppermute | solution.py:19
  161.4 26.2 %collective-permute-start.32 = (bf16[2,20,64,128]{3,2,1,0:T(8,128)(2,1)S(1)}, bf16[2,20,64,128]{3,2,1,0:T(8,128)(2,1)S(1)}, u32[]{:S(2)}, u32[]{:S(2)}) collective-permute-start(bf16[2,20,64,128]{3,2,1,0:T(8,128)(2,1)S(1)} %get-tuple-element.82.refs_0_), channel_id=1, source_target_pairs={{0,16},{16,0},{1,17},{17,1},{2,18},{18,2},{3,19},{19,3},{4,20},{20... | collective-permute-start | bytes 1966088 | tf_op jit(solution)/shard_map/ppermute | solution.py:23
  169.1 18.5 %collective-permute-start.33 = (bf16[2,20,64,128]{3,2,1,0:T(8,128)(2,1)S(1)}, bf16[2,20,64,128]{3,2,1,0:T(8,128)(2,1)S(1)}, u32[]{:S(2)}, u32[]{:S(2)}) collective-permute-start(bf16[2,20,64,128]{3,2,1,0:T(8,128)(2,1)S(1)} %collective-permute-done.29.refs_1_), channel_id=1, source_target_pairs={{0,16},{16,0},{1,17},{17,1},{2,18},{18,2},{3,19},{19,3},{4,20},{20... | collective-permute-start | bytes 1966088 | tf_op jit(solution)/shard_map/ppermute | solution.py:23
  176.3 12.3 %collective-permute-start.35 = (bf16[2,20,64,128]{3,2,1,0:T(8,128)(2,1)S(1)}, bf16[2,20,64,128]{3,2,1,0:T(8,128)(2,1)S(1)}, u32[]{:S(2)}, u32[]{:S(2)}) collective-permute-start(bf16[2,20,64,128]{3,2,1,0:T(8,128)(2,1)S(1)} %collective-permute-done.31.refs_3_), channel_id=1, source_target_pairs={{0,16},{16,0},{1,17},{17,1},{2,18},{18,2},{3,19},{19,3},{4,20},{20... | collective-permute-start | bytes 1966088 | tf_op jit(solution)/shard_map/ppermute | solution.py:23
  (35 other events, 196.5 us)
